TPU v7x, 32 devices: a whole 2x2x4 slice. The times are simulated.
32 devices in a mesh: grp: 2 (over y), section: 4 (over x, core), seg: 4 (over z).
Axes of the slice: x: 2, y: 2, z: 4, core: 2. Of those that a mesh axis runs over, the one named last changes fastest.
Arguments:
- inputs: bfloat16 [4, 8, 256, 2048], P('section', ('grp', 'seg')), parts along dimension 1, may hold values from -44 to 44
- memory: bfloat16 [4, 8, 32, 2048], P('section', ('grp', 'seg')), parts along dimension 1, may hold values from -6 to 6
- out_cot: bfloat16 [4, 8, 288, 2048], P('section', ('grp', 'seg')), parts along dimension 1, may hold values from -6 to 6
- head_cot: bfloat16 [4, 8, 288, 2048], P('section', ('grp', 'seg')), parts along dimension 1, may hold values from -6 to 6
- w_query: bfloat16 [4, 2048, 2048], P('section', 'seg'), may hold values from -0.61871843 to 0.61871843
- w_key: bfloat16 [4, 2048, 512], P('section', 'seg'), may hold values from -0.61871843 to 0.61871843
- w_value: bfloat16 [4, 2048, 512], P('section', 'seg'), may hold values from -0.125 to 0.125
- gain: bfloat16 [4, 2048], P('section'), may hold values from 0.5 to 1.5
Outputs:
- token_cot_below: bfloat16 [4, 8, 256, 2048], P('section', ('grp', 'seg')), parts along dimension 1
- memory_cot_before: bfloat16 [4, 8, 32, 2048], P('section', ('grp', 'seg')), parts along dimension 1
- grad_query: float32 [8, 2048, 2048], P(('grp', 'section'), 'seg'), parts along dimension 0
- grad_key: float32 [8, 2048, 512], P(('grp', 'section'), 'seg'), parts along dimension 0
- grad_value: float32 [8, 2048, 512], P(('grp', 'section'), 'seg'), parts along dimension 0
- grad_gain: float32 [8, 2048], P(('grp', 'section'), 'seg'), parts along dimension 0
There are 2 independent parts, one for each index of `grp`. A program takes and returns all parts, laid end to end along the dimension named above; an argument that names none is the same for every part. Nothing has to cross between parts.
All inputs are finite; a program needn't handle non-finite values.
Results may differ from a plain program's by a relative error of at most 0.01.
The roundings to bfloat16 on the way count: a program that leaves them out, or rounds other values in their place, can miss the bound.
Values may be sent and summed in bfloat16 or wider, within the bound.
No kernel may reach another device: no remote copies, remote signals or barrier semaphores. Data moves between devices by JAX's collectives and lax.ppermute only.
A program may use at most 128 MiB of HBM per device.

v0:
```python
import jax
import jax.numpy as jnp
from jax import lax
from jax.sharding import PartitionSpec as P

HEADS = 4
GROUP = 4
HD = 128


def from_behind(block, axis, distance):
    devices = range(lax.axis_size(axis))
    route = [(i - distance, i) for i in devices if i - distance in devices]
    return lax.ppermute(block, axis, route)


def times_t(left, right):
    return lax.dot_general(
        left, right, (((1,), (1,)), ((), ())), preferred_element_type=jnp.float32
    )


def inner_rows(left, right):
    return lax.dot_general(
        left, right, (((0,), (0,)), ((), ())), preferred_element_type=jnp.float32
    )


def deliver(token_part, memory_part):
    below = from_behind(token_part, "section", -1)
    before = from_behind(memory_part, "seg", -1)
    return (below, before)


def on_device(inputs, memory, out_cot, head_cot, w_query, w_key, w_value, gain):
    whole_q, whole_k, whole_v = (
        lax.all_gather(w_query, "seg", axis=1, tiled=True),
        lax.all_gather(w_key, "seg", axis=1, tiled=True),
        lax.all_gather(w_value, "seg", axis=1, tiled=True),
    )
    wq = whole_q[0]
    wk = whole_k[0]
    wv = whole_v[0]
    tokens_in = inputs[0, 0]
    mem = memory[0, 0]
    ocot = out_cot[0, 0]
    hcot = head_cot[0, 0]
    gain_f = gain[0].astype(jnp.float32)
    mem_len = mem.shape[0]
    seg_len = tokens_in.shape[0]
    width = tokens_in.shape[1]
    query_width = wq.shape[1]
    rows = jnp.concatenate([mem, tokens_in, mem], 0)
    total = rows.shape[0]
    zf = rows.astype(jnp.float32)
    inv = lax.rsqrt(jnp.mean(zf * zf, -1, keepdims=True) + 1e-05)
    unit = zf * inv
    normed = (unit * gain_f).astype(jnp.bfloat16)
    query = (
        jnp.dot(normed, wq, preferred_element_type=jnp.float32)
        .astype(jnp.bfloat16)
        .reshape(total, HEADS, GROUP, HD)
    )
    keys = (
        jnp.dot(normed, wk, preferred_element_type=jnp.float32)
        .astype(jnp.bfloat16)
        .reshape(total, HEADS, HD)
    )
    values = (
        jnp.dot(normed, wv, preferred_element_type=jnp.float32)
        .astype(jnp.bfloat16)
        .reshape(total, HEADS, HD)
    )
    scale = HD ** (-0.5)
    scores = jnp.einsum("qhgd,khd->hgqk", query, keys, preferred_element_type=jnp.float32) * scale
    places = jnp.arange(total)
    causal = places[:, None] >= places[None, :]
    scores = jnp.where(causal[None, None], scores, -1e30)
    probs = jax.nn.softmax(scores, -1)
    probs_b = probs.astype(jnp.bfloat16)
    cot = jnp.concatenate([jnp.zeros((mem_len, width), jnp.bfloat16), ocot], 0)
    d_attn = jnp.concatenate([jnp.zeros((mem_len, query_width), jnp.bfloat16), hcot], 0)
    d_heads = d_attn.reshape(total, HEADS, GROUP, HD)
    d_probs = jnp.einsum("qhgd,khd->hgqk", d_heads, values, preferred_element_type=jnp.float32)
    d_scores = (probs * (d_probs - jnp.sum(probs * d_probs, -1, keepdims=True)) * scale).astype(
        jnp.bfloat16
    )
    d_values = jnp.einsum("hgqk,qhgd->khd", probs_b, d_heads, preferred_element_type=jnp.float32)
    d_values = d_values.astype(jnp.bfloat16).reshape(total, HEADS * HD)
    d_query = jnp.einsum("hgqk,khd->qhgd", d_scores, keys, preferred_element_type=jnp.float32)
    d_query = d_query.astype(jnp.bfloat16).reshape(total, query_width)
    d_keys = jnp.einsum("hgqk,qhgd->khd", d_scores, query, preferred_element_type=jnp.float32)
    d_keys = d_keys.astype(jnp.bfloat16).reshape(total, HEADS * HD)
    d_normed = times_t(d_query, wq) + times_t(d_keys, wk) + times_t(d_values, wv)
    grad_g = jnp.sum(d_normed * unit, 0)
    d_unit = d_normed * gain_f
    d_rows = cot.astype(jnp.float32) + inv * (
        d_unit - unit * jnp.mean(d_unit * unit, -1, keepdims=True)
    )
    token_part = d_rows[mem_len : mem_len + seg_len].astype(jnp.bfloat16)
    memory_part = (d_rows[:mem_len] + d_rows[mem_len + seg_len :]).astype(jnp.bfloat16)
    grad_q = inner_rows(normed, d_query)
    grad_k = inner_rows(normed, d_keys)
    grad_v = inner_rows(normed, d_values)
    grad_query, grad_key, grad_value = (
        lax.psum_scatter(
            grad_q[None].astype(jnp.bfloat16), "seg", scatter_dimension=1, tiled=True
        ).astype(jnp.float32),
        lax.psum_scatter(
            grad_k[None].astype(jnp.bfloat16), "seg", scatter_dimension=1, tiled=True
        ).astype(jnp.float32),
        lax.psum_scatter(
            grad_v[None].astype(jnp.bfloat16), "seg", scatter_dimension=1, tiled=True
        ).astype(jnp.float32),
    )
    grad_gain = lax.psum_scatter(grad_g[None], "seg", scatter_dimension=1, tiled=True)
    below, before = deliver(token_part, memory_part)
    return (below[None, None], before[None, None], grad_query, grad_key, grad_value, grad_gain)


def solution(mesh):
    in_specs = (
        P("section", ("grp", "seg"), None, None),
        P("section", ("grp", "seg"), None, None),
        P("section", ("grp", "seg"), None, None),
        P("section", ("grp", "seg"), None, None),
        P("section", "seg", None),
        P("section", "seg", None),
        P("section", "seg", None),
        P("section", None),
    )
    out_specs = (
        P("section", ("grp", "seg"), None, None),
        P("section", ("grp", "seg"), None, None),
        P(("grp", "section"), "seg", None),
        P(("grp", "section"), "seg", None),
        P(("grp", "section"), "seg", None),
        P(("grp", "section"), "seg"),
    )
    return jax.shard_map(
        on_device, mesh=mesh, in_specs=in_specs, out_specs=out_specs, check_vma=False
    )
```

profile of v0, /device:TPU:7, one launch (start us, length us, event | category | flops | bytes accessed | tf_op | source)
XLA Modules:
  0.0 594.9 jit_solution(3217382233434655294)
XLA Ops:
  12.9 43.8 %all-gather.8.cloned.1.call-done = bf16[1,2048,512]{2,1,0:T(8,128)(2,1)} async-done(((bf16[1,512,512]{2,1,0:T(8,128)(2,1)}), bf16[1,2048,512]{2,1,0:T(8,128)(2,1)}) %all-gather.8.cloned.1.call-update) | async-done | bytes 2097168 | tf_op jit(solution)/shard_map/all_gather | solution.py:39
  56.7 2.9 fusion.55
  59.7 43.3 %all-gather.4.cloned.1.call-done = bf16[1,2048,512]{2,1,0:T(8,128)(2,1)} async-done(((bf16[1,512,512]{2,1,0:T(8,128)(2,1)}), bf16[1,2048,512]{2,1,0:T(8,128)(2,1)}) %all-gather.4.cloned.1.call-update) | async-done | bytes 2097168 | tf_op jit(solution)/shard_map/all_gather | solution.py:38
  103.0 2.5 fusion.52
  105.5 4.3 fusion.63
  109.9 143.3 %all-gather.6.cloned.1.call-done = bf16[1,2048,2048]{2,1,0:T(8,128)(2,1)} async-done(((bf16[1,512,2048]{2,1,0:T(8,128)(2,1)}), bf16[1,2048,2048]{2,1,0:T(8,128)(2,1)}) %all-gather.6.cloned.1.call-update) | async-done | bytes 8388624 | tf_op jit(solution)/shard_map/all_gather | solution.py:37
  253.2 7.4 %fusion.26 = bf16[320,2048]{1,0:T(8,128)(2,1)} fusion(bf16[1,2048,2048]{2,1,0:T(8,128)(2,1)} %all-gather.6.cloned.1.call-done, f32[2048]{0:T(1024)S(1)} %bitcast.160, f32[320]{0:T(512)S(1)} %add_rsqrt_fusion, bf16[32,2048]{1,0:T(8,128)(2,1)S(1)} %bitcast.148, bf16[256,2048]{1,0:T(8,128)(2,1)S(1)} %bitcast.135), kind=kOutput, calls=%fused_computation.37 | convolution fusion | flops 2690908160 | bytes 10888448 | tf_op jit(solution)/shard_map/dot_general | solution.py:60
  260.5 4.1 reshape.64
  264.7 7.6 %fusion.100 = (f32[4,4,320]{2,1,0:T(4,128)S(1)}, f32[4,4,320,320]{2,3,1,0:T(8,128)}) fusion(pred[320,320]{0,1:T(8,128)(4,1)S(1)} %copy-done.6, bf16[320,4,4,128]{3,2,1,0:T(4,128)(2,1)} %reshape.64, bf16[320,4,128,1]{2,1,0,3:T(4,128)(2,1)S(1)} %bitcast.154), kind=kOutput, calls=%fused_computation.93 | convolution fusion | flops 425984320 | bytes 8314880 | tf_op jit(solution)/shard_map/sub | solution.py:79
  272.3 4.4 fusion.59
  276.6 13.2 %fusion.58 = bf16[4,40,8,128]{3,2,1,0:T(8,128)(2,1)S(1)} fusion(f32[4,320,320,4]{2,1,3,0:T(8,128)} %fusion.63, bf16[320,4,4,128]{3,2,1,0:T(4,128)(2,1)} %reshape.64, f32[4,4,320,320]{2,3,1,0:T(8,128)} %get-tuple-element.9, f32[4,4,320]{2,1,0:T(4,128)S(1)} %get-tuple-element.8), kind=kOutput, calls=%fused_computation.61 | convolution fusion | flops 431068480 | bytes 14766080 | tf_op jit(solution)/shard_map/hgqk,qhgd->khd/dot_general | solution.py:92
  289.8 13.8 %fusion.43 = bf16[320,4,4,128]{3,0,2,1:T(8,128)(2,1)} fusion(f32[4,320,320,4]{2,1,3,0:T(8,128)} %fusion.63, bf16[320,4,128,1]{2,1,0,3:T(4,128)(2,1)S(1)} %bitcast.155, f32[4,4,320,320]{2,3,1,0:T(8,128)} %get-tuple-element.9, f32[4,4,320]{2,1,0:T(4,128)S(1)} %get-tuple-element.8), kind=kOutput, calls=%fused_computation.53 | convolution fusion | flops 431560000 | bytes 14766080 | tf_op jit(solution)/shard_map/hgqk,khd->qhgd/dot_general | solution.py:90
  307.7 6.1 %fusion.2 = f32[320,2048]{1,0:T(8,128)S(1)} fusion(bf16[320,2048]{1,0:T(8,128)(2,1)} %reshape.67, bf16[1,2048,2048]{2,1,0:T(8,128)(2,1)} %all-gather.6.cloned.1.call-done), kind=kOutput, calls=%fused_computation.2 | convolution fusion | flops 2684354560 | bytes 12320768 | tf_op jit(solution)/shard_map/dot_general | solution.py:18
  315.4 2.6 fusion.34
  319.5 2.7 fusion.25
  322.3 2.8 fusion.24
  325.2 6.9 %convert_bitcast_fusion = bf16[1,2048,2048]{2,1,0:T(8,128)(2,1)} fusion(bf16[320,2048]{1,0:T(8,128)(2,1)S(1)} %copy-done.2, f32[2048]{0:T(1024)S(1)} %bitcast.164, f32[320]{0:T(512)S(1)} %add_rsqrt_fusion, bf16[32,2048]{1,0:T(8,128)(2,1)S(1)} %bitcast.152, bf16[256,2048]{1,0:T(8,128)(2,1)S(1)} %bitcast.139), kind=kOutput, calls=%fused_computation.6 | convolution fusion | flops 2694447104 | bytes 10888448 | tf_op jit(solution)/shard_map/dot_general | solution.py:24
  333.4 2.6 fusion.33
  336.1 2.4 collective-permute-start
  339.9 4.8 reduce-scatter.13.cloned.1.call-done
  346.4 44.3 %reduce-scatter.11.cloned.1.call-done = bf16[1,512,512]{2,1,0:T(8,128)(2,1)} async-done(((bf16[1,2048,512]{2,1,0:T(8,128)(2,1)}), bf16[1,512,512]{2,1,0:T(8,128)(2,1)}) %reduce-scatter.11.cloned.1.call-update) | async-done | bytes 524304 | tf_op jit(solution)/shard_map/reduce_scatter | solution.py:112
  392.8 43.2 %reduce-scatter.9.cloned.1.call-done = bf16[1,512,512]{2,1,0:T(8,128)(2,1)} async-done(((bf16[1,2048,512]{2,1,0:T(8,128)(2,1)}), bf16[1,512,512]{2,1,0:T(8,128)(2,1)}) %reduce-scatter.9.cloned.1.call-update) | async-done | bytes 524304 | tf_op jit(solution)/shard_map/reduce_scatter | solution.py:109
  438.1 144.2 %reduce-scatter.7.cloned.1.call-done = bf16[1,512,2048]{2,1,0:T(8,128)(2,1)} async-done(((bf16[1,2048,2048]{2,1,0:T(8,128)(2,1)}), bf16[1,512,2048]{2,1,0:T(8,128)(2,1)}) %reduce-scatter.7.cloned.1.call-update) | async-done | bytes 2097168 | tf_op jit(solution)/shard_map/reduce_scatter | solution.py:106
  582.3 4.1 convert_element_type.92
  (55 shorter events, 23.3 us)
Async XLA Ops:
  7.2 2.3 copy-start.7
  7.2 2.3 copy-start.3
  7.2 49.5 %all-gather.8.cloned.1.call-start = ((), (), s32[]{:S(2)}) async-start(), calls=%async_computation.6 | async-start | bytes 2621440 | tf_op jit(solution)/shard_map/all_gather | solution.py:39
  7.9 95.1 %all-gather.4.cloned.1.call-start = ((), (), s32[]{:S(2)}) async-start(), calls=%async_computation.4 | async-start | bytes 2621440 | tf_op jit(solution)/shard_map/all_gather | solution.py:38
  8.7 244.5 %all-gather.6.cloned.1.call-start = ((), (), s32[]{:S(2)}) async-start(), calls=%async_computation.5 | async-start | bytes 10485760 | tf_op jit(solution)/shard_map/all_gather | solution.py:37
  9.4 1.2 copy-start.5
  9.4 335.3 %reduce-scatter.13.cloned.1.call-start = ((), (), s32[]{:S(2)}) async-start(), calls=%async_computation.10 | async-start | bytes 1310720
  56.7 46.3 %copy-start = (bf16[1,1,256,2048]{3,2,1,0:T(8,128)(2,1)S(1)}, bf16[1,1,256,2048]{3,2,1,0:T(8,128)(2,1)}, u32[]{:S(2)}) copy-start(bf16[1,1,256,2048]{3,2,1,0:T(8,128)(2,1)} %param.8) | copy-start | bytes 3145732
  260.5 4.2 copy-start.6
  307.7 6.1 %copy-start.1 = (bf16[1,2048,512]{2,1,0:T(8,128)(2,1)S(1)}, bf16[1,2048,512]{2,1,0:T(8,128)(2,1)}, u32[]{:S(2)}) copy-start(bf16[1,2048,512]{2,1,0:T(8,128)(2,1)} %all-gather.4.cloned.1.call-done) | copy-start | bytes 6291460
  313.9 1.6 copy-start.8
  319.5 71.2 %reduce-scatter.11.cloned.1.call-start = ((), (), s32[]{:S(2)}) async-start(), calls=%async_computation.9 | async-start | bytes 2621440 | tf_op jit(solution)/shard_map/reduce_scatter | solution.py:112
  322.2 2.9 copy-start.2
  322.3 113.7 %reduce-scatter.9.cloned.1.call-start = ((), (), s32[]{:S(2)}) async-start(), calls=%async_computation.8 | async-start | bytes 2621440 | tf_op jit(solution)/shard_map/reduce_scatter | solution.py:109
  325.1 257.2 %reduce-scatter.7.cloned.1.call-start = ((), (), s32[]{:S(2)}) async-start(), calls=%async_computation.7 | async-start | bytes 10485760 | tf_op jit(solution)/shard_map/reduce_scatter | solution.py:106
  332.1 1.3 copy-start.4
  336.1 10.3 %collective-permute-start = (bf16[256,2048]{1,0:T(8,128)(2,1)S(1)}, bf16[256,2048]{1,0:T(8,128)(2,1)S(1)}, u32[]{:S(2)}, u32[]{:S(2)}) collective-permute-start(bf16[256,2048]{1,0:T(8,128)(2,1)S(1)} %slice.21), channel_id=1, source_target_pairs={{4,0},{8,4},{12,8},{5,1},{9,5},{13,9},{6,2},{10,6},{14,10},{7,3},{... | collective-permute-start | bytes 3145736 | tf_op jit(solution)/shard_map/ppermute | solution.py:14
  338.6 7.8 %collective-permute-start.1 = (bf16[32,2048]{1,0:T(8,128)(2,1)S(1)}, bf16[32,2048]{1,0:T(8,128)(2,1)S(1)}, u32[]{:S(2)}, u32[]{:S(2)}) collective-permute-start(bf16[32,2048]{1,0:T(8,128)(2,1)S(1)} %fusion.82), channel_id=1, source_target_pairs={{1,0},{2,1},{3,2},{5,4},{6,5},{7,6},{9,8},{10,9},{11,10},{13,12},{... | collective-permute-start | bytes 393224 | tf_op jit(solution)/shard_map/ppermute | solution.py:14
Sparse Core Ops, SparseCore 0:
  9.6 47.0 all-gather.7
  58.3 44.6 all-gather.3
  104.6 148.5 all-gather.5
  319.6 25.1 reduce-scatter.12
  347.0 43.6 reduce-scatter.10
  392.8 43.1 reduce-scatter.8
  438.5 143.7 reduce-scatter.6
where the time goes:
time: 597 us; the launch traced here: 595 us
  waiting for transfers between devices  469 us (79%)
  matrix products  77.9 us (13%)
  local copies, waits for them, and re-layouts  16.3 us (3%)
  between operations  14.4 us (2%)
  other arithmetic  13.3 us (2%)
    reduce_scatter x1, waiting for transfers between devices, on_device(): lax.psum_scatter(grad_q[None].astype(jnp.bfloat16), 'seg', scatter_dimens...  144 us
    all_gather x1, waiting for transfers between devices, on_device(): lax.all_gather(w_query, 'seg', axis=1, tiled=True)  143 us
    reduce_scatter x1, waiting for transfers between devices, on_device(): lax.psum_scatter(grad_v[None].astype(jnp.bfloat16), 'seg', scatter_dimens...  44.3 us
    all_gather x1, waiting for transfers between devices, on_device(): lax.all_gather(w_value, 'seg', axis=1, tiled=True)  43.8 us
    all_gather x1, waiting for transfers between devices, on_device(): lax.all_gather(w_key, 'seg', axis=1, tiled=True)  43.3 us
    reduce_scatter x1, waiting for transfers between devices, on_device(): lax.psum_scatter(grad_k[None].astype(jnp.bfloat16), 'seg', scatter_dimens...  43.2 us
    dot_general x1, matrix products, on_device(): jnp.einsum('hgqk,khd->qhgd', d_scores, keys, preferred_element_type=jnp.f...  13.8 us
    dot_general x1, matrix products, on_device(): jnp.einsum('hgqk,qhgd->khd', d_scores, query, preferred_element_type=jnp....  13.2 us
  transfers between devices with their start and end apart: 9, of which 7 were waited for; matrix products, arithmetic and copies ran while one was open for 6% of the time, Pallas kernels for 0%

commit v1 on v0

--- a/solution.py
+++ b/solution.py
@@ -1,11 +1,16 @@
+import functools
+
 import jax
 import jax.numpy as jnp
 from jax import lax
+from jax.experimental import pallas as pl
+from jax.experimental.pallas import tpu as pltpu
 from jax.sharding import PartitionSpec as P
 
 HEADS = 4
 GROUP = 4
 HD = 128
+MIB = 1024 * 1024
 
 
 def from_behind(block, axis, distance):
@@ -118,6 +123,306 @@
     return (below[None, None], before[None, None], grad_query, grad_key, grad_value, grad_gain)
 
 
+SWAP = [(0, 1), (1, 0), (2, 3), (3, 2)]
+ACROSS = [(1, 2), (2, 1)]
+OUTWARD = [(1, 0), (2, 3)]
+INWARD = [(0, 1), (3, 2)]
+FAR_INWARD = [(0, 2), (3, 1)]
+GRPS = [(0, 1), (1, 0)]
+
+
+def full(shape_dtype=None):
+    return pl.BlockSpec(memory_space=pltpu.VMEM)
+
+
+def after(value, *others):
+    return lax.optimization_barrier((value,) + others)[0]
+
+
+def normalise_kernel(half, place_ref, tok_ref, mem_ref, gain_ref, n_ref, near_ref, far_ref):
+    seg_len = tok_ref.shape[0]
+    gain = gain_ref[...].astype(jnp.float32)
+
+    def piece(rows):
+        zf = rows.astype(jnp.float32)
+        inv = lax.rsqrt(jnp.mean(zf * zf, -1, keepdims=True) + 1e-05)
+        return (zf * inv * gain).astype(jnp.bfloat16)
+
+    step = 32
+
+    @pl.loop(0, seg_len // step)
+    def _(i):
+        at = pl.ds(pl.multiple_of(i * step, step), step)
+        n_ref[at, :] = piece(tok_ref[at, :])
+
+    n_ref[seg_len:, :] = piece(mem_ref[...])
+    near = pl.multiple_of(place_ref[0], 128)
+    far = pl.multiple_of(place_ref[1], 128)
+    near_ref[...] = n_ref[:, pl.ds(near, half)]
+    far_ref[...] = n_ref[:, pl.ds(far, half)]
+
+
+def pieces_of(own, a, far, ya, yfar):
+    quarter = a.shape[0]
+    return (
+        (own, 0, own.shape[0]),
+        (a, 0, quarter),
+        (far, 0, quarter),
+        (far, quarter, quarter),
+        (ya, 0, quarter),
+        (yfar, 0, quarter),
+        (yfar, quarter, quarter),
+    )
+
+
+def head_kernel(off_ref, n_ref, own, a, far, ya, yfar, hcot_ref, d_ref, qkv_ref):
+    rows = n_ref.shape[0]
+    total = None
+    for i, (ref, start, count) in enumerate(pieces_of(own, a, far, ya, yfar)):
+        at = pl.ds(pl.multiple_of(off_ref[i], 128), count)
+        part = jnp.dot(
+            n_ref[:, at], ref[start : start + count, :], preferred_element_type=jnp.float32
+        )
+        total = part if total is None else total + part
+    qkv_ref[...] = total.astype(jnp.bfloat16)
+    mem = rows - (rows // 128) * 128
+    seg_len = rows - mem
+    qw = GROUP * HD
+    keys = jnp.concatenate([qkv_ref[:, qw : qw + HD], qkv_ref[seg_len:, qw : qw + HD]], 0)
+    values = jnp.concatenate([qkv_ref[:, qw + HD :], qkv_ref[seg_len:, qw + HD :]], 0)
+    scale = HD ** (-0.5)
+    wide = rows + mem
+    row = lax.broadcasted_iota(jnp.int32, (rows, wide), 0)
+    col = lax.broadcasted_iota(jnp.int32, (rows, wide), 1)
+    need = jnp.where(col < seg_len, col, jnp.where(col < rows, 0, col - mem))
+    seen = row >= need
+    d_keys = None
+    d_values = None
+    for g in range(GROUP):
+        q = qkv_ref[:, g * HD : (g + 1) * HD]
+        da = hcot_ref[:, g * HD : (g + 1) * HD]
+        s = jnp.where(seen, times_t(q, keys) * scale, -1e30)
+        e = jnp.exp(s - jnp.max(s, -1, keepdims=True))
+        p = e / jnp.sum(e, -1, keepdims=True)
+        dp = times_t(da, values)
+        ds = (p * (dp - jnp.sum(p * dp, -1, keepdims=True)) * scale).astype(jnp.bfloat16)
+        d_ref[:, g * HD : (g + 1) * HD] = jnp.dot(
+            ds, keys, preferred_element_type=jnp.float32
+        ).astype(jnp.bfloat16)
+        dk = inner_rows(ds, q)
+        dv = inner_rows(p.astype(jnp.bfloat16), da)
+        d_keys = dk if d_keys is None else d_keys + dk
+        d_values = dv if d_values is None else d_values + dv
+    for at, both in ((qw, d_keys), (qw + HD, d_values)):
+        d_ref[:seg_len, at : at + HD] = both[:seg_len].astype(jnp.bfloat16)
+        d_ref[seg_len:, at : at + HD] = (both[seg_len:rows] + both[rows:]).astype(jnp.bfloat16)
+
+
+def rows_kernel(off_ref, tok_ref, mem_ref, gain_ref, cot_ref, *refs):
+    d_refs = refs[:HEADS]
+    w_refs = refs[HEADS : 6 * HEADS]
+    token_ref, memory_ref, gg_ref, dn_ref = refs[6 * HEADS :]
+    seg_len = tok_ref.shape[0]
+    all_pieces = [pieces_of(*w_refs[5 * c : 5 * c + 5]) for c in range(HEADS)]
+    for i in range(len(all_pieces[0])):
+        total = None
+        for c in range(HEADS):
+            ref, start, count = all_pieces[c][i]
+            part = times_t(d_refs[c][...], ref[start : start + count, :])
+            total = part if total is None else total + part
+        dn_ref[:, pl.ds(pl.multiple_of(off_ref[i], 128), count)] = total
+    gain = gain_ref[...].astype(jnp.float32)
+    step = mem_ref.shape[0]
+
+    def piece(rows, dn, cot):
+        zf = rows.astype(jnp.float32)
+        inv = lax.rsqrt(jnp.mean(zf * zf, -1, keepdims=True) + 1e-05)
+        unit = zf * inv
+        gg_ref[...] += jnp.sum(dn * unit, 0, keepdims=True)
+        du = dn * gain
+        out = cot.astype(jnp.float32) + inv * (
+            du - unit * jnp.mean(du * unit, -1, keepdims=True)
+        )
+        return out.astype(jnp.bfloat16)
+
+    gg_ref[...] = jnp.zeros_like(gg_ref)
+
+    @pl.loop(0, seg_len // step)
+    def _(i):
+        at = pl.ds(pl.multiple_of(i * step, step), step)
+        token_ref[at, :] = piece(tok_ref[at, :], dn_ref[at, :], cot_ref[at, :])
+
+    memory_ref[...] = piece(mem_ref[...], dn_ref[seg_len:, :], cot_ref[seg_len:, :])
+
+
+def grads_kernel(place_ref, nt_ref, d0, d1, d2, d3, other_ref, own_ref, dcat_ref):
+    rows = d0.shape[0]
+    for i, ref in enumerate((d0, d1, d2, d3)):
+        dcat_ref[i * rows : (i + 1) * rows, :] = ref[...]
+    block = own_ref.shape[0]
+    other = pl.ds(pl.multiple_of(place_ref[2], 128), block)
+    mine = pl.ds(pl.multiple_of(place_ref[3], 128), block)
+    other_ref[...] = jnp.dot(
+        nt_ref[other, :], dcat_ref[...], preferred_element_type=jnp.float32
+    ).astype(jnp.bfloat16)
+    own_ref[...] = jnp.dot(nt_ref[mine, :], dcat_ref[...], preferred_element_type=jnp.float32)
+
+
+def on_line(inputs, memory, out_cot, head_cot, w_query, w_key, w_value, gain):
+    tok = inputs[0, 0]
+    mem = memory[0, 0]
+    ocot = out_cot[0, 0]
+    hcot = head_cot[0, 0]
+    width = tok.shape[1]
+    rows = tok.shape[0] + mem.shape[0]
+    block = w_query.shape[1]
+    quarter = block // 2
+    qw = GROUP * HD
+    cw = qw + 2 * HD
+    z = lax.axis_index("seg")
+    grp = lax.axis_index("grp")
+    pair = z // 2
+    inner = (z == 1) | (z == 2)
+    partner = z + 1 - 2 * (z % 2)
+    far_in = jnp.where(z < 2, 2, 1)
+    far_out = jnp.where(z < 2, 3, 0)
+    mine = grp * quarter
+    theirs = (1 - grp) * quarter
+    offsets = jnp.stack(
+        [z * block]
+        + [b * block + mine for b in (partner, far_out, far_in)]
+        + [b * block + theirs for b in (partner, far_out, far_in)]
+    ).astype(jnp.int32)
+    places = jnp.stack(
+        [pair * 2 * block, (1 - pair) * 2 * block, pair * block, (1 - pair) * block]
+    ).astype(jnp.int32)
+
+    smem = pl.BlockSpec(memory_space=pltpu.SMEM)
+    vmem = pl.BlockSpec(memory_space=pltpu.VMEM)
+    bf16 = jnp.bfloat16
+
+    def shape(r, c, dtype=bf16):
+        return jax.ShapeDtypeStruct((r, c), dtype)
+
+    own = [
+        jnp.concatenate(
+            [
+                w_query[0][:, c * qw : (c + 1) * qw],
+                w_key[0][:, c * HD : (c + 1) * HD],
+                w_value[0][:, c * HD : (c + 1) * HD],
+            ],
+            1,
+        )
+        for c in range(HEADS)
+    ]
+    half = [lax.dynamic_slice_in_dim(w, mine, quarter, 0) for w in own]
+
+    normed, near, far = pl.pallas_call(
+        functools.partial(normalise_kernel, 2 * block),
+        out_shape=(shape(rows, width), shape(rows, 2 * block), shape(rows, 2 * block)),
+        in_specs=[smem, vmem, vmem, vmem],
+        out_specs=(vmem, vmem, vmem),
+        compiler_params=pltpu.CompilerParams(vmem_limit_bytes=16 * MIB),
+        cost_estimate=pl.CostEstimate(
+            flops=8 * rows * width, bytes_accessed=6 * rows * width, transcendentals=rows
+        ),
+    )(places, tok, mem, gain)
+
+    n_across = lax.ppermute(far, "seg", ACROSS)
+
+    a, ya, b, c_, far_w, yfar = ([None] * HEADS for _ in range(6))
+    for i in range(HEADS):
+        send = half[i]
+        if i == 3:
+            send = after(send, b[0])
+        a[i] = lax.ppermute(send, "seg", SWAP)
+        ya[i] = lax.ppermute(a[i], "grp", GRPS)
+        b[i] = lax.ppermute(jnp.concatenate([a[i], half[i]], 0), "seg", ACROSS)
+        c_[i] = lax.ppermute(b[i], "seg", OUTWARD)
+        far_w[i] = jnp.where(inner, b[i], c_[i])
+        yfar[i] = lax.ppermute(far_w[i], "grp", GRPS)
+
+    near_w = after(near, a[3])
+    far_n = after(far, a[3])
+    n_in = lax.ppermute(near_w, "seg", INWARD)
+    n_far = lax.ppermute(far_n, "seg", FAR_INWARD)
+    n_t = jnp.concatenate([near, n_in, n_across, n_far], 0).T
+
+    pieces = [[own[i], a[i], far_w[i], ya[i], yfar[i]] for i in range(HEADS)]
+    d = []
+    recv = []
+    kept = []
+    for i in range(HEADS):
+        d_i = pl.pallas_call(
+            head_kernel,
+            out_shape=shape(rows, cw),
+            in_specs=[smem] + [vmem] * 7,
+            out_specs=vmem,
+            scratch_shapes=[pltpu.VMEM((rows, cw), bf16)],
+            compiler_params=pltpu.CompilerParams(vmem_limit_bytes=32 * MIB),
+            cost_estimate=pl.CostEstimate(
+                flops=2 * rows * width * cw + 3 * 10 * GROUP * rows * rows * HD,
+                bytes_accessed=2 * (width * cw + rows * width),
+                transcendentals=GROUP * rows * rows,
+            ),
+        )(offsets, normed, *pieces[i], hcot[:, i * qw : (i + 1) * qw])
+        d.append(d_i)
+        d_across = lax.ppermute(d_i, "seg", ACROSS)
+        d_in = lax.ppermute(d_i, "seg", INWARD)
+        d_far = lax.ppermute(d_i, "seg", FAR_INWARD)
+        other, mine_g = pl.pallas_call(
+            grads_kernel,
+            out_shape=(shape(block, cw), shape(block, cw, jnp.float32)),
+            in_specs=[smem] + [vmem] * 5,
+            out_specs=(vmem, vmem),
+            scratch_shapes=[pltpu.VMEM((4 * rows, cw), bf16)],
+            compiler_params=pltpu.CompilerParams(vmem_limit_bytes=32 * MIB),
+            cost_estimate=pl.CostEstimate(
+                flops=2 * 2 * block * 4 * rows * cw,
+                bytes_accessed=2 * 4 * rows * (2 * block + cw) + 6 * block * cw,
+                transcendentals=0,
+            ),
+        )(places, n_t, d_i, d_in, d_across, d_far)
+        recv.append(lax.ppermute(other, "seg", OUTWARD))
+        kept.append(mine_g)
+
+    flat = [p for ps in pieces for p in ps]
+    token_part, memory_part, grad_g = pl.pallas_call(
+        rows_kernel,
+        out_shape=(
+            shape(tok.shape[0], width),
+            shape(mem.shape[0], width),
+            shape(1, width, jnp.float32),
+        ),
+        in_specs=[smem] + [vmem] * (4 + 6 * HEADS),
+        out_specs=(vmem, vmem, vmem),
+        scratch_shapes=[pltpu.VMEM((rows, width), jnp.float32)],
+        compiler_params=pltpu.CompilerParams(vmem_limit_bytes=40 * MIB),
+        cost_estimate=pl.CostEstimate(
+            flops=2 * rows * width * cw * HEADS,
+            bytes_accessed=2 * HEADS * cw * (width + rows) + 8 * rows * width,
+            transcendentals=rows,
+        ),
+    )(offsets, tok, mem, gain, ocot, *d, *flat)
+
+    below, before = deliver(token_part, memory_part)
+    grad_gain = jnp.sum(
+        lax.all_to_all(grad_g.reshape(4, width // 4), "seg", 0, 0, tiled=True), 0, keepdims=True
+    )
+    whole = [jnp.where(inner, k, r.astype(jnp.float32)) for k, r in zip(kept, recv)]
+    grad_query = jnp.concatenate([w[:, :qw] for w in whole], 1)
+    grad_key = jnp.concatenate([w[:, qw : qw + HD] for w in whole], 1)
+    grad_value = jnp.concatenate([w[:, qw + HD :] for w in whole], 1)
+    return (
+        below[None, None],
+        before[None, None],
+        grad_query[None],
+        grad_key[None],
+        grad_value[None],
+        grad_gain,
+    )
+
+
 def solution(mesh):
     in_specs = (
         P("section", ("grp", "seg"), None, None),
@@ -137,6 +442,11 @@
         P(("grp", "section"), "seg", None),
         P(("grp", "section"), "seg"),
     )
+    line = mesh.shape["seg"] == 4 and mesh.shape["grp"] == 2
     return jax.shard_map(
-        on_device, mesh=mesh, in_specs=in_specs, out_specs=out_specs, check_vma=False
-    )
+        on_line if line else on_device,
+        mesh=mesh,
+        in_specs=in_specs,
+        out_specs=out_specs,
+        check_vma=False,
+    )

time: 597 us -> 305 us (0.51)
  waiting for transfers between devices: 469 us -> 60.2 us
  starting transfers between devices: 4.01 us -> 118 us
  matrix products: 77.9 us -> 0 us
  Pallas kernels: 0 us -> 56.3 us
  local copies, waits for them, and re-layouts: 16.3 us -> 44.2 us
  between operations: 14.4 us -> 1.34 us
  other arithmetic: 13.3 us -> 20.3 us
    reduce_scatter x3 -> x0, waiting for transfers between devices: 232 us -> none  [the longest x1 144 us: on_device(): lax.psum_scatter(grad_q[None].astype(jnp.bfloat16), 'seg', scatter_dimens...]
    all_gather x3 -> x0, waiting for transfers between devices: 230 us -> none  [the longest x1 143 us: on_device(): lax.all_gather(w_query, 'seg', axis=1, tiled=True)]
    ppermute x0 -> x39, starting transfers between devices: none -> 92.8 us  [the longest x1 20.4 us: on_line(): n_far = lax.ppermute(far_n, 'seg', FAR_INWARD)]
    dot_general x13 -> x0, matrix products: 70.3 us -> none  [the longest x1 13.8 us: on_device(): jnp.einsum('hgqk,khd->qhgd', d_scores, keys, preferred_element_type=jnp.f...]
    ppermute x0 -> x39, waiting for transfers between devices: none -> 60.2 us  [the longest x4 25.1 us: on_line(): c_[i] = lax.ppermute(b[i], 'seg', OUTWARD)]
    pallas_call x0 -> x10, Pallas kernels: none -> 56.3 us  [the longest x4 26.2 us: on_line(): pl.pallas_call(head_kernel, out_shape=shape(rows, cw), in_specs=[smem] +...]
    ppermute x2, starting transfers between devices: 3.74 us -> 20.8 us  [from_behind(): return lax.ppermute(block, axis, route)]
    unnamed x22 -> x102, local copies, waits for them, and re-layouts: 6.57 us -> 21.7 us
  transfers between devices with their start and end apart: 9 -> 42, of which waited for: 7 -> 6; matrix products, arithmetic and copies ran while one was open for 6% -> 11% of each run, Pallas kernels for 0% -> 19%
where the time goes in v1:
time: 305 us; the launch traced here: 300 us
  starting transfers between devices  118 us (39%)
  waiting for transfers between devices  60.2 us (20%)
  Pallas kernels  56.3 us (18%)
  local copies, waits for them, and re-layouts  44.2 us (14%)
  other arithmetic  20.3 us (7%)
    pallas_call x4, Pallas kernels, on_line(): pl.pallas_call(head_kernel, out_shape=shape(rows, cw), in_specs=[smem] +...  26.2 us
    ppermute x4, waiting for transfers between devices, on_line(): c_[i] = lax.ppermute(b[i], 'seg', OUTWARD)  25.1 us
    unnamed x102, local copies, waits for them, and re-layouts  21.7 us
    ppermute x2, starting transfers between devices, from_behind(): return lax.ppermute(block, axis, route)  20.8 us
    ppermute x1, starting transfers between devices, on_line(): n_far = lax.ppermute(far_n, 'seg', FAR_INWARD)  20.4 us
    ppermute x4, waiting for transfers between devices, on_line(): recv.append(lax.ppermute(other, 'seg', OUTWARD))  17.6 us
    ppermute x4, waiting for transfers between devices, on_line(): a[i] = lax.ppermute(send, 'seg', SWAP)  17.3 us
    pallas_call x4, Pallas kernels, on_line(): pl.pallas_call(grads_kernel, out_shape=(shape(block, cw), shape(block, cw...  16.3 us
  transfers between devices with their start and end apart: 42, of which 6 were waited for; matrix products, arithmetic and copies ran while one was open for 11% of the time, Pallas kernels for 19%

profile of v1, /device:TPU:7, one launch (start us, length us, event | category | flops | bytes accessed | tf_op | source)
XLA Modules:
  0.0 300.0 jit_solution(16081362089905134765)
XLA Ops:
  6.3 8.3 %collective-permute-done.a.refs_5_ = bf16[256,768]{1,0:T(8,128)(2,1)S(1)} collective-permute-done((bf16[256,768]{1,0:T(8,128)(2,1)S(1)}, bf16[256,768]{1,0:T(8,128)(2,1)S(1)}, u32[]{:S(2)}, u32[]{:S(2)}) %collective-permute-start) | collective-permute-done | bytes 393248 | tf_op jit(solution)/shard_map/ppermute | solution.py:338
  15.4 7.7 %collective-permute-done.5.a.refs_10_ = bf16[256,768]{1,0:T(8,128)(2,1)S(1)} collective-permute-done((bf16[256,768]{1,0:T(8,128)(2,1)S(1)}, bf16[256,768]{1,0:T(8,128)(2,1)S(1)}, u32[]{:S(2)}, u32[]{:S(2)}) %collective-permute-start.5) | collective-permute-done | bytes 393248 | tf_op jit(solution)/shard_map/ppermute | solution.py:338
  24.9 3.0 %collective-permute-start.10 = (bf16[256,768]{1,0:T(8,128)(2,1)S(1)}, bf16[256,768]{1,0:T(8,128)(2,1)}, u32[]{:S(2)}, u32[]{:S(2)}) collective-permute-start(bf16[256,768]{1,0:T(8,128)(2,1)S(1)} %constant_dynamic-slice_fusion.1), channel_id=1, source_target_pairs={{0,1},{1,0},{2,3},{3,2},{4,5},{5,4},{6,7},{7,6},{8,9},{9,8},{10,11... | collective-permute-start | bytes 1179656 | tf_op jit(solution)/shard_map/ppermute | solution.py:338
  28.8 5.5 %collective-permute-start.15 = (bf16[256,768]{1,0:T(8,128)(2,1)}, bf16[256,768]{1,0:T(8,128)(2,1)}, u32[]{:S(2)}, u32[]{:S(2)}) collective-permute-start(bf16[256,768]{1,0:T(8,128)(2,1)} %constant_dynamic-slice_fusion), channel_id=1, source_target_pairs={{0,1},{1,0},{2,3},{3,2},{4,5},{5,4},{6,7},{7,6},{8,9},{9,8},{10,11... | collective-permute-start | bytes 1179656 | tf_op jit(solution)/shard_map/ppermute | solution.py:338
  53.3 10.5 %collective-permute-done.7 = bf16[512,768]{1,0:T(8,128)(2,1)} collective-permute-done((bf16[512,768]{1,0:T(8,128)(2,1)}, bf16[512,768]{1,0:T(8,128)(2,1)}, u32[]{:S(2)}, u32[]{:S(2)}) %collective-permute-start.7) | collective-permute-done | bytes 786464 | tf_op jit(solution)/shard_map/ppermute | solution.py:341
  67.9 14.6 %collective-permute-done.2 = bf16[512,768]{1,0:T(8,128)(2,1)} collective-permute-done((bf16[512,768]{1,0:T(8,128)(2,1)}, bf16[512,768]{1,0:T(8,128)(2,1)}, u32[]{:S(2)}, u32[]{:S(2)}) %collective-permute-start.2) | collective-permute-done | bytes 786464 | tf_op jit(solution)/shard_map/ppermute | solution.py:341
  86.1 20.4 %collective-permute-start.24 = (bf16[288,1024]{1,0:T(8,128)(2,1)}, bf16[288,1024]{1,0:T(8,128)(2,1)}, u32[]{:S(2)}, u32[]{:S(2)}) collective-permute-start(bf16[288,1024]{1,0:T(8,128)(2,1)} %get-tuple-element.30), channel_id=1, source_target_pairs={{0,2},{3,1},{4,6},{7,5},{8,10},{11,9},{12,14},{15,13},{16,18},{19,... | collective-permute-start | bytes 1769480 | tf_op jit(solution)/shard_map/ppermute | solution.py:348
  106.5 7.4 %collective-permute-start.22 = (bf16[288,1024]{1,0:T(8,128)(2,1)}, bf16[288,1024]{1,0:T(8,128)(2,1)}, u32[]{:S(2)}, u32[]{:S(2)}) collective-permute-start(bf16[288,1024]{1,0:T(8,128)(2,1)} %get-tuple-element.28), channel_id=1, source_target_pairs={{0,1},{3,2},{4,5},{7,6},{8,9},{11,10},{12,13},{15,14},{16,17},{19,... | collective-permute-start | bytes 1769480 | tf_op jit(solution)/shard_map/ppermute | solution.py:347
  124.9 5.8 %shard_map.129.refs_1_.d0 = bf16[288,768]{1,0:T(8,128)(2,1)} custom-call(s32[7]{0:T(128)S(1)} %stack.46.off_ref, bf16[288,2048]{1,0:T(8,128)(2,1)S(1)} %copy-done.32, bf16[512,768]{1,0:T(8,128)(2,1)S(1)} %pad_maximum_fusion.2.own.refs_9_, bf16[256,768]{1,0:T(8,128)(2,1)S(1)} %copy-done.13, bf16[512,768]{1,0:T(8,128)(2,1)S(1)} %copy-done.2, ...), custom_call_target="tpu_custom_call" | custom-call | flops 2179989504 | bytes 4325376 | tf_op jit(solution)/shard_map/pallas_call | solution.py:356
  134.3 3.6 %collective-permute-start.29 = (bf16[288,768]{1,0:T(8,128)(2,1)}, bf16[288,768]{1,0:T(8,128)(2,1)}, u32[]{:S(2)}, u32[]{:S(2)}) collective-permute-start(bf16[288,768]{1,0:T(8,128)(2,1)} %shard_map.129.refs_1_.d0), channel_id=1, source_target_pairs={{0,1},{3,2},{4,5},{7,6},{8,9},{11,10},{12,13},{15,14},{16,17},{19,... | collective-permute-start | bytes 1327112 | tf_op jit(solution)/shard_map/ppermute | solution.py:371
  140.2 6.6 %shard_map.128.refs_0_.d0 = bf16[288,768]{1,0:T(8,128)(2,1)} custom-call(s32[7]{0:T(128)S(1)} %stack.46.off_ref, bf16[288,2048]{1,0:T(8,128)(2,1)S(1)} %copy-done.32, bf16[512,768]{1,0:T(8,128)(2,1)S(1)} %pad_maximum_fusion.own.refs_4_, bf16[256,768]{1,0:T(8,128)(2,1)S(1)} %collective-permute-done.a.refs_5_, ...), custom_call_target="tpu_custom_call" | custom-call | flops 2179989504 | bytes 4325376 | tf_op jit(solution)/shard_map/pallas_call | solution.py:356
  162.9 5.8 %concatenate.44 = bf16[1152,1024]{0,1:T(8,128)(2,1)} concatenate(bf16[288,1024]{0,1:T(8,128)(2,1)} %copy.18, bf16[288,1024]{0,1:T(8,128)(2,1)} %copy.19, bf16[288,1024]{0,1:T(8,128)(2,1)} %copy.20, bf16[288,1024]{0,1:T(8,128)(2,1)} %copy.21), dimensions={0} | concatenate | bytes 4718592 | tf_op jit(solution)/shard_map/concatenate | solution.py:349
  172.1 7.0 %shard_map.130.refs_2_.d0 = bf16[288,768]{1,0:T(8,128)(2,1)} custom-call(s32[7]{0:T(128)S(1)} %stack.46.off_ref, bf16[288,2048]{1,0:T(8,128)(2,1)S(1)} %copy-done.33, bf16[512,768]{1,0:T(8,128)(2,1)S(1)} %pad_maximum_fusion.4.own.refs_14_, bf16[256,768]{1,0:T(8,128)(2,1)} %collective-permute-done.10.a.refs_15_, ...), custom_call_target="tpu_custom_call" | custom-call | flops 2179989504 | bytes 4325376 | tf_op jit(solution)/shard_map/pallas_call | solution.py:356
  179.1 4.0 %shard_map.134 = (bf16[512,768]{1,0:T(8,128)(2,1)}, f32[512,768]{1,0:T(8,128)S(1)}) custom-call(s32[4]{0:T(128)S(1)} %pad_add_fusion.place_ref, bf16[1024,1152]{1,0:T(8,128)(2,1)S(1)} %bitcast.31, bf16[288,768]{1,0:T(8,128)(2,1)} %shard_map.129.refs_1_.d0, bf16[288,768]{1,0:T(8,128)(2,1)} %collective-permute-done.29.d1, bf16[288,768]{1,0:T(8,128)(2,1)S(1)} %copy-done.38, ...), custom_call_target="tpu_custom_call" | custom-call | flops 1811939328 | bytes 6488064 | tf_op jit(solution)/shard_map/pallas_call | solution.py:373
  189.3 4.4 %shard_map.133 = (bf16[512,768]{1,0:T(8,128)(2,1)}, f32[512,768]{1,0:T(8,128)S(1)}) custom-call(s32[4]{0:T(128)S(1)} %pad_add_fusion.place_ref, bf16[1024,1152]{1,0:T(8,128)(2,1)S(1)} %bitcast.32, bf16[288,768]{1,0:T(8,128)(2,1)} %shard_map.128.refs_0_.d0, bf16[288,768]{1,0:T(8,128)(2,1)} %collective-permute-done.25.d1, ...), custom_call_target="tpu_custom_call" | custom-call | flops 1811939328 | bytes 6488064 | tf_op jit(solution)/shard_map/pallas_call | solution.py:373
  194.8 5.7 %collective-permute-start.33 = (bf16[288,768]{1,0:T(8,128)(2,1)}, bf16[288,768]{1,0:T(8,128)(2,1)}, u32[]{:S(2)}, u32[]{:S(2)}) collective-permute-start(bf16[288,768]{1,0:T(8,128)(2,1)} %shard_map.130.refs_2_.d0), channel_id=1, source_target_pairs={{0,1},{3,2},{4,5},{7,6},{8,9},{11,10},{12,13},{15,14},{16,17},{19,... | collective-permute-start | bytes 1327112 | tf_op jit(solution)/shard_map/ppermute | solution.py:371
  202.1 6.9 %shard_map.131.refs_3_.d0 = bf16[288,768]{1,0:T(8,128)(2,1)} custom-call(s32[7]{0:T(128)S(1)} %stack.46.off_ref, bf16[288,2048]{1,0:T(8,128)(2,1)S(1)} %copy-done.34, bf16[512,768]{1,0:T(8,128)(2,1)S(1)} %pad_maximum_fusion.6.own.refs_19_, bf16[256,768]{1,0:T(8,128)(2,1)} %collective-permute-done.15.a.refs_20_, ...), custom_call_target="tpu_custom_call" | custom-call | flops 2179989504 | bytes 4325376 | tf_op jit(solution)/shard_map/pallas_call | solution.py:356
  209.0 10.9 %shard_map.132 = (bf16[256,2048]{1,0:T(8,128)(2,1)}, bf16[32,2048]{1,0:T(8,128)(2,1)S(1)}, f32[1,2048]{1,0:T(1,128)}) custom-call(s32[7]{0:T(128)S(1)} %stack.46.off_ref, bf16[256,2048]{1,0:T(8,128)(2,1)} %bitcast.29, bf16[32,2048]{1,0:T(8,128)(2,1)S(1)} %bitcast.36, bf16[1,2048]{1,0:T(2,128)(2,1)S(1)} %copy-done.30, bf16[288,2048]{1,0:T(8,128)(2,1)} %bitcast.38, ...), custom_call_target="tpu_custom_call" | custom-call | flops 3623878656 | bytes 19070976 | tf_op jit(solution)/shard_map/pallas_call | solution.py:390
  220.5 4.1 %all-to-all-start = ((f32[4,1,512]{2,1,0:T(1,128)}), f32[4,1,512]{2,1,0:T(1,128)S(1)}, u32[]{:S(2)}, u32[]{:S(2)}) async-start(f32[4,1,512]{2,1,0:T(1,128)} %bitcast.24), calls=%async_computation | async-start | bytes 16384 | tf_op jit(solution)/shard_map/all_to_all | solution.py:410
  226.3 4.4 %shard_map.135 = (bf16[512,768]{1,0:T(8,128)(2,1)}, f32[512,768]{1,0:T(8,128)S(1)}) custom-call(s32[4]{0:T(128)S(1)} %pad_add_fusion.place_ref, bf16[1024,1152]{1,0:T(8,128)(2,1)S(1)} %bitcast.33, bf16[288,768]{1,0:T(8,128)(2,1)} %shard_map.130.refs_2_.d0, bf16[288,768]{1,0:T(8,128)(2,1)} %collective-permute-done.33.d1, ...), custom_call_target="tpu_custom_call" | custom-call | flops 1811939328 | bytes 6488064 | tf_op jit(solution)/shard_map/pallas_call | solution.py:373
  232.0 7.7 %collective-permute-start.39 = (bf16[288,768]{1,0:T(8,128)(2,1)}, bf16[288,768]{1,0:T(8,128)(2,1)}, u32[]{:S(2)}, u32[]{:S(2)}) collective-permute-start(bf16[288,768]{1,0:T(8,128)(2,1)} %shard_map.131.refs_3_.d0), channel_id=1, source_target_pairs={{0,2},{3,1},{4,6},{7,5},{8,10},{11,9},{12,14},{15,13},{16,18},{19,... | collective-permute-start | bytes 1327112 | tf_op jit(solution)/shard_map/ppermute | solution.py:372
  247.4 19.5 %collective-permute-start.20 = (bf16[256,2048]{1,0:T(8,128)(2,1)S(1)}, bf16[256,2048]{1,0:T(8,128)(2,1)S(1)}, u32[]{:S(2)}, u32[]{:S(2)}) collective-permute-start(bf16[256,2048]{1,0:T(8,128)(2,1)S(1)} %copy-done.49), channel_id=1, source_target_pairs={{4,0},{8,4},{12,8},{5,1},{9,5},{13,9},{6,2},{10,6},{14,10},{7,3},{... | collective-permute-start | bytes 3145736 | tf_op jit(solution)/shard_map/ppermute | solution.py:19
  267.0 3.5 %shard_map.136 = (bf16[512,768]{1,0:T(8,128)(2,1)S(1)}, f32[512,768]{1,0:T(8,128)S(1)}) custom-call(s32[4]{0:T(128)S(1)} %pad_add_fusion.place_ref, bf16[1024,1152]{1,0:T(8,128)(2,1)S(1)} %bitcast.34, bf16[288,768]{1,0:T(8,128)(2,1)} %shard_map.131.refs_3_.d0, bf16[288,768]{1,0:T(8,128)(2,1)S(1)} %collective-permute-done.37.d1, ...), custom_call_target="tpu_custom_call" | custom-call | flops 1811939328 | bytes 6488064 | tf_op jit(solution)/shard_map/pallas_call | solution.py:373
  274.3 17.6 %collective-permute-done.40 = bf16[512,768]{1,0:T(8,128)(2,1)S(1)} collective-permute-done((bf16[512,768]{1,0:T(8,128)(2,1)S(1)}, bf16[512,768]{1,0:T(8,128)(2,1)S(1)}, u32[]{:S(2)}, u32[]{:S(2)}) %collective-permute-start.40) | collective-permute-done | bytes 786464 | tf_op jit(solution)/shard_map/ppermute | solution.py:386
  (217 shorter events, 103.8 us)
Async XLA Ops:
  48.1 34.4 %collective-permute-start.2 = (bf16[512,768]{1,0:T(8,128)(2,1)}, bf16[512,768]{1,0:T(8,128)(2,1)}, u32[]{:S(2)}, u32[]{:S(2)}) collective-permute-start(bf16[512,768]{1,0:T(8,128)(2,1)} %copy-done.46), channel_id=1, source_target_pairs={{1,0},{2,3},{5,4},{6,7},{9,8},{10,11},{13,12},{14,15},{17,16},{18,... | collective-permute-start | bytes 2359304 | tf_op jit(solution)/shard_map/ppermute | solution.py:341
  51.5 31.3 %collective-permute-start.16 = (bf16[512,768]{1,0:T(8,128)(2,1)}, bf16[512,768]{1,0:T(8,128)(2,1)}, u32[]{:S(2)}, u32[]{:S(2)}) collective-permute-start(bf16[512,768]{1,0:T(8,128)(2,1)} %pad_maximum_fusion.7), channel_id=1, source_target_pairs={{1,2},{2,1},{5,6},{6,5},{9,10},{10,9},{13,14},{14,13},{17,18},{18,... | collective-permute-start | bytes 2359304 | tf_op jit(solution)/shard_map/ppermute | solution.py:340
  63.8 50.2 %collective-permute-start.12 = (bf16[512,768]{1,0:T(8,128)(2,1)}, bf16[512,768]{1,0:T(8,128)(2,1)S(1)}, u32[]{:S(2)}, u32[]{:S(2)}) collective-permute-start(bf16[512,768]{1,0:T(8,128)(2,1)} %collective-permute-done.11), channel_id=1, source_target_pairs={{1,0},{2,3},{5,4},{6,7},{9,8},{10,11},{13,12},{14,15},{17,16},{18,... | collective-permute-start | bytes 2359304 | tf_op jit(solution)/shard_map/ppermute | solution.py:341
  66.3 48.8 %collective-permute-start.9 = (bf16[512,768]{1,0:T(8,128)(2,1)S(1)}, bf16[512,768]{1,0:T(8,128)(2,1)S(1)}, u32[]{:S(2)}, u32[]{:S(2)}) collective-permute-start(bf16[512,768]{1,0:T(8,128)(2,1)S(1)} %broadcast_select_fusion.2.far.refs_11_), channel_id=1, source_target_pairs={{0,16},{16,0},{1,17},{17,1},{2,18},{18,2},{3,19},{19,3},{4,20},{20... | collective-permute-start | bytes 2359304 | tf_op jit(solution)/shard_map/ppermute | solution.py:343
  82.7 51.5 %collective-permute-start.17 = (bf16[512,768]{1,0:T(8,128)(2,1)}, bf16[512,768]{1,0:T(8,128)(2,1)}, u32[]{:S(2)}, u32[]{:S(2)}) collective-permute-start(bf16[512,768]{1,0:T(8,128)(2,1)} %collective-permute-done.16), channel_id=1, source_target_pairs={{1,0},{2,3},{5,4},{6,7},{9,8},{10,11},{13,12},{14,15},{17,16},{18,... | collective-permute-start | bytes 2359304 | tf_op jit(solution)/shard_map/ppermute | solution.py:341
  86.1 44.6 %collective-permute-start.24 = (bf16[288,1024]{1,0:T(8,128)(2,1)}, bf16[288,1024]{1,0:T(8,128)(2,1)}, u32[]{:S(2)}, u32[]{:S(2)}) collective-permute-start(bf16[288,1024]{1,0:T(8,128)(2,1)} %get-tuple-element.30), channel_id=1, source_target_pairs={{0,2},{3,1},{4,6},{7,5},{8,10},{11,9},{12,14},{15,13},{16,18},{19,... | collective-permute-start | bytes 1769480 | tf_op jit(solution)/shard_map/ppermute | solution.py:348
  106.5 27.0 %collective-permute-start.22 = (bf16[288,1024]{1,0:T(8,128)(2,1)}, bf16[288,1024]{1,0:T(8,128)(2,1)}, u32[]{:S(2)}, u32[]{:S(2)}) collective-permute-start(bf16[288,1024]{1,0:T(8,128)(2,1)} %get-tuple-element.28), channel_id=1, source_target_pairs={{0,1},{3,2},{4,5},{7,6},{8,9},{11,10},{12,13},{15,14},{16,17},{19,... | collective-permute-start | bytes 1769480 | tf_op jit(solution)/shard_map/ppermute | solution.py:347
  113.9 26.1 %collective-permute-start.4 = (bf16[512,768]{1,0:T(8,128)(2,1)}, bf16[512,768]{1,0:T(8,128)(2,1)}, u32[]{:S(2)}, u32[]{:S(2)}) collective-permute-start(bf16[512,768]{1,0:T(8,128)(2,1)} %broadcast_select_fusion.3.far.refs_6_), channel_id=1, source_target_pairs={{0,16},{16,0},{1,17},{17,1},{2,18},{18,2},{3,19},{19,3},{4,20},{20... | collective-permute-start | bytes 2359304 | tf_op jit(solution)/shard_map/ppermute | solution.py:343
  116.1 30.8 %collective-permute-start.14 = (bf16[512,768]{1,0:T(8,128)(2,1)}, bf16[512,768]{1,0:T(8,128)(2,1)}, u32[]{:S(2)}, u32[]{:S(2)}) collective-permute-start(bf16[512,768]{1,0:T(8,128)(2,1)} %broadcast_select_fusion.1.far.refs_16_), channel_id=1, source_target_pairs={{0,16},{16,0},{1,17},{17,1},{2,18},{18,2},{3,19},{19,3},{4,20},{20... | collective-permute-start | bytes 2359304 | tf_op jit(solution)/shard_map/ppermute | solution.py:343
  134.3 34.4 %collective-permute-start.29 = (bf16[288,768]{1,0:T(8,128)(2,1)}, bf16[288,768]{1,0:T(8,128)(2,1)}, u32[]{:S(2)}, u32[]{:S(2)}) collective-permute-start(bf16[288,768]{1,0:T(8,128)(2,1)} %shard_map.129.refs_1_.d0), channel_id=1, source_target_pairs={{0,1},{3,2},{4,5},{7,6},{8,9},{11,10},{12,13},{15,14},{16,17},{19,... | collective-permute-start | bytes 1327112 | tf_op jit(solution)/shard_map/ppermute | solution.py:371
  140.0 60.5 %collective-permute-start.19 = (bf16[512,768]{1,0:T(8,128)(2,1)}, bf16[512,768]{1,0:T(8,128)(2,1)}, u32[]{:S(2)}, u32[]{:S(2)}) collective-permute-start(bf16[512,768]{1,0:T(8,128)(2,1)} %broadcast_select_fusion.far.refs_21_), channel_id=1, source_target_pairs={{0,16},{16,0},{1,17},{17,1},{2,18},{18,2},{3,19},{19,3},{4,20},{20... | collective-permute-start | bytes 2359304 | tf_op jit(solution)/shard_map/ppermute | solution.py:343
  146.8 37.5 %collective-permute-start.27 = (bf16[288,768]{1,0:T(8,128)(2,1)}, bf16[288,768]{1,0:T(8,128)(2,1)}, u32[]{:S(2)}, u32[]{:S(2)}) collective-permute-start(bf16[288,768]{1,0:T(8,128)(2,1)} %shard_map.128.refs_0_.d0), channel_id=1, source_target_pairs={{0,2},{3,1},{4,6},{7,5},{8,10},{11,9},{12,14},{15,13},{16,18},{19,... | collective-permute-start | bytes 1327112 | tf_op jit(solution)/shard_map/ppermute | solution.py:372
  149.7 36.7 %collective-permute-start.26 = (bf16[288,768]{1,0:T(8,128)(2,1)}, bf16[288,768]{1,0:T(8,128)(2,1)}, u32[]{:S(2)}, u32[]{:S(2)}) collective-permute-start(bf16[288,768]{1,0:T(8,128)(2,1)} %shard_map.128.refs_0_.d0), channel_id=1, source_target_pairs={{1,2},{2,1},{5,6},{6,5},{9,10},{10,9},{13,14},{14,13},{17,18},{18,... | collective-permute-start | bytes 1327112 | tf_op jit(solution)/shard_map/ppermute | solution.py:370
  151.9 36.0 %collective-permute-start.25 = (bf16[288,768]{1,0:T(8,128)(2,1)}, bf16[288,768]{1,0:T(8,128)(2,1)}, u32[]{:S(2)}, u32[]{:S(2)}) collective-permute-start(bf16[288,768]{1,0:T(8,128)(2,1)} %shard_map.128.refs_0_.d0), channel_id=1, source_target_pairs={{0,1},{3,2},{4,5},{7,6},{8,9},{11,10},{12,13},{15,14},{16,17},{19,... | collective-permute-start | bytes 1327112 | tf_op jit(solution)/shard_map/ppermute | solution.py:371
  168.7 26.2 %collective-permute-start.18 = (bf16[256,768]{1,0:T(8,128)(2,1)}, bf16[256,768]{1,0:T(8,128)(2,1)S(1)}, u32[]{:S(2)}, u32[]{:S(2)}) collective-permute-start(bf16[256,768]{1,0:T(8,128)(2,1)} %collective-permute-done.15.a.refs_20_), channel_id=1, source_target_pairs={{0,16},{16,0},{1,17},{17,1},{2,18},{18,2},{3,19},{19,3},{4,20},{20... | collective-permute-start | bytes 1179656 | tf_op jit(solution)/shard_map/ppermute | solution.py:339
  184.3 40.3 %collective-permute-start.35 = (bf16[288,768]{1,0:T(8,128)(2,1)}, bf16[288,768]{1,0:T(8,128)(2,1)}, u32[]{:S(2)}, u32[]{:S(2)}) collective-permute-start(bf16[288,768]{1,0:T(8,128)(2,1)} %shard_map.130.refs_2_.d0), channel_id=1, source_target_pairs={{0,2},{3,1},{4,6},{7,5},{8,10},{11,9},{12,14},{15,13},{16,18},{19,... | collective-permute-start | bytes 1327112 | tf_op jit(solution)/shard_map/ppermute | solution.py:372
  186.4 38.2 %collective-permute-start.34 = (bf16[288,768]{1,0:T(8,128)(2,1)}, bf16[288,768]{1,0:T(8,128)(2,1)}, u32[]{:S(2)}, u32[]{:S(2)}) collective-permute-start(bf16[288,768]{1,0:T(8,128)(2,1)} %shard_map.130.refs_2_.d0), channel_id=1, source_target_pairs={{1,2},{2,1},{5,6},{6,5},{9,10},{10,9},{13,14},{14,13},{17,18},{18,... | collective-permute-start | bytes 1327112 | tf_op jit(solution)/shard_map/ppermute | solution.py:370
  187.9 53.9 %collective-permute-start.32 = (bf16[512,768]{1,0:T(8,128)(2,1)}, bf16[512,768]{1,0:T(8,128)(2,1)}, u32[]{:S(2)}, u32[]{:S(2)}) collective-permute-start(bf16[512,768]{1,0:T(8,128)(2,1)} %get-tuple-element.34), channel_id=1, source_target_pairs={{1,0},{2,3},{5,4},{6,7},{9,8},{10,11},{13,12},{14,15},{17,16},{18,... | collective-permute-start | bytes 2359304 | tf_op jit(solution)/shard_map/ppermute | solution.py:386
  194.8 29.8 %collective-permute-start.33 = (bf16[288,768]{1,0:T(8,128)(2,1)}, bf16[288,768]{1,0:T(8,128)(2,1)}, u32[]{:S(2)}, u32[]{:S(2)}) collective-permute-start(bf16[288,768]{1,0:T(8,128)(2,1)} %shard_map.130.refs_2_.d0), channel_id=1, source_target_pairs={{0,1},{3,2},{4,5},{7,6},{8,9},{11,10},{12,13},{15,14},{16,17},{19,... | collective-permute-start | bytes 1327112 | tf_op jit(solution)/shard_map/ppermute | solution.py:371
  200.5 44.1 %collective-permute-start.28 = (bf16[512,768]{1,0:T(8,128)(2,1)}, bf16[512,768]{1,0:T(8,128)(2,1)}, u32[]{:S(2)}, u32[]{:S(2)}) collective-permute-start(bf16[512,768]{1,0:T(8,128)(2,1)} %get-tuple-element.32), channel_id=1, source_target_pairs={{1,0},{2,3},{5,4},{6,7},{9,8},{10,11},{13,12},{14,15},{17,16},{18,... | collective-permute-start | bytes 2359304 | tf_op jit(solution)/shard_map/ppermute | solution.py:386
  230.7 41.0 %collective-permute-start.36 = (bf16[512,768]{1,0:T(8,128)(2,1)}, bf16[512,768]{1,0:T(8,128)(2,1)}, u32[]{:S(2)}, u32[]{:S(2)}) collective-permute-start(bf16[512,768]{1,0:T(8,128)(2,1)} %get-tuple-element.36), channel_id=1, source_target_pairs={{1,0},{2,3},{5,4},{6,7},{9,8},{10,11},{13,12},{14,15},{17,16},{18,... | collective-permute-start | bytes 2359304 | tf_op jit(solution)/shard_map/ppermute | solution.py:386
  239.7 27.2 %collective-permute-start.38 = (bf16[288,768]{1,0:T(8,128)(2,1)}, bf16[288,768]{1,0:T(8,128)(2,1)}, u32[]{:S(2)}, u32[]{:S(2)}) collective-permute-start(bf16[288,768]{1,0:T(8,128)(2,1)} %shard_map.131.refs_3_.d0), channel_id=1, source_target_pairs={{1,2},{2,1},{5,6},{6,5},{9,10},{10,9},{13,14},{14,13},{17,18},{18,... | collective-permute-start | bytes 1327112 | tf_op jit(solution)/shard_map/ppermute | solution.py:370
  244.6 29.7 %collective-permute-start.21 = (bf16[32,2048]{1,0:T(8,128)(2,1)S(1)}, bf16[32,2048]{1,0:T(8,128)(2,1)S(1)}, u32[]{:S(2)}, u32[]{:S(2)}) collective-permute-start(bf16[32,2048]{1,0:T(8,128)(2,1)S(1)} %copy-done.40), channel_id=1, source_target_pairs={{1,0},{2,1},{3,2},{5,4},{6,5},{7,6},{9,8},{10,9},{11,10},{13,12},{... | collective-permute-start | bytes 393224 | tf_op jit(solution)/shard_map/ppermute | solution.py:19
  247.4 26.9 %collective-permute-start.20 = (bf16[256,2048]{1,0:T(8,128)(2,1)S(1)}, bf16[256,2048]{1,0:T(8,128)(2,1)S(1)}, u32[]{:S(2)}, u32[]{:S(2)}) collective-permute-start(bf16[256,2048]{1,0:T(8,128)(2,1)S(1)} %copy-done.49), channel_id=1, source_target_pairs={{4,0},{8,4},{12,8},{5,1},{9,5},{13,9},{6,2},{10,6},{14,10},{7,3},{... | collective-permute-start | bytes 3145736 | tf_op jit(solution)/shard_map/ppermute | solution.py:19
  (71 other events, 750.9 us)

commit v2 on v0

--- a/solution.py
+++ b/solution.py
@@ -1,11 +1,16 @@
+import functools
+
 import jax
 import jax.numpy as jnp
 from jax import lax
+from jax.experimental import pallas as pl
+from jax.experimental.pallas import tpu as pltpu
 from jax.sharding import PartitionSpec as P
 
 HEADS = 4
 GROUP = 4
 HD = 128
+MIB = 1024 * 1024
 
 
 def from_behind(block, axis, distance):
@@ -118,6 +123,485 @@
     return (below[None, None], before[None, None], grad_query, grad_key, grad_value, grad_gain)
 
 
+SWAP = [(0, 1), (1, 0), (2, 3), (3, 2)]
+ACROSS = [(1, 2), (2, 1)]
+OUTWARD = [(1, 0), (2, 3)]
+INWARD = [(0, 1), (3, 2)]
+FAR_INWARD = [(0, 2), (3, 1)]
+GRPS = [(0, 1), (1, 0)]
+
+
+def normalise_kernel(half, place_ref, tok_ref, mem_ref, gain_ref, n_ref, near_ref, far_ref):
+    seg_len = tok_ref.shape[0]
+    gain = gain_ref[...].astype(jnp.float32)
+
+    def piece(rows):
+        zf = rows.astype(jnp.float32)
+        inv = lax.rsqrt(jnp.mean(zf * zf, -1, keepdims=True) + 1e-05)
+        return (zf * inv * gain).astype(jnp.bfloat16)
+
+    step = 32
+
+    @pl.loop(0, seg_len // step)
+    def _(i):
+        at = pl.ds(pl.multiple_of(i * step, step), step)
+        n_ref[at, :] = piece(tok_ref[at, :])
+
+    n_ref[seg_len:, :] = piece(mem_ref[...])
+    near = pl.multiple_of(place_ref[0], 128)
+    far = pl.multiple_of(place_ref[1], 128)
+    near_ref[...] = n_ref[:, pl.ds(near, half)]
+    far_ref[...] = n_ref[:, pl.ds(far, half)]
+
+
+def halves_kernel(place_ref, wq, wk, wv, first, second, sems):
+    quarter = first.shape[0] // 2
+    qw = GROUP * HD
+    at = pl.ds(pl.multiple_of(place_ref[4] * quarter, quarter), quarter)
+    copies = []
+    for c in range(HEADS):
+        out = (first, second)[c // 2]
+        to = slice((c % 2) * quarter, (c % 2 + 1) * quarter)
+        for k, (w, start, wide) in enumerate(((wq, 0, qw), (wk, qw, HD), (wv, qw + HD, HD))):
+            copies.append(
+                pltpu.make_async_copy(
+                    w.at[at, c * wide : (c + 1) * wide],
+                    out.at[to, start : start + wide],
+                    sems.at[3 * c + k],
+                )
+            )
+    for copy in copies:
+        copy.start()
+    for copy in copies:
+        copy.wait()
+
+
+def fetch(copies):
+    copies = [pltpu.make_async_copy(*c) for c in copies]
+    for copy in copies:
+        copy.start()
+    return copies
+
+
+def weight_copies(refs, starts, c, w_ref, sems):
+    wq, wk, wv, a, far, ya, yfar = refs
+    block = wq.shape[0]
+    quarter = block // 2
+    qw = GROUP * HD
+    sources = [
+        (wq.at[:, c * qw : (c + 1) * qw], slice(0, block), slice(0, qw)),
+        (wk.at[:, c * HD : (c + 1) * HD], slice(0, block), slice(qw, qw + HD)),
+        (wv.at[:, c * HD : (c + 1) * HD], slice(0, block), slice(qw + HD, qw + 2 * HD)),
+    ]
+    at = block
+    for ref, start, rows in (
+        (a, starts[0], quarter),
+        (far, 0, 2 * quarter),
+        (ya, starts[1], quarter),
+        (yfar, 0, 2 * quarter),
+    ):
+        sources.append(
+            (ref.at[start : start + rows, :], slice(at, at + rows), slice(0, w_ref.shape[1]))
+        )
+        at += rows
+    return [(src, w_ref.at[r, k], sems.at[n]) for n, (src, r, k) in enumerate(sources)]
+
+
+def piece_rows(block):
+    quarter = block // 2
+    sizes = [block] + [quarter] * 6
+    waits = [(0, 1, 2), (3,), (4,), (), (5,), (6,), ()]
+    at = 0
+    for size, wait in zip(sizes, waits):
+        yield at, size, wait
+        at += size
+
+
+def head_kernel(c, starts, off_ref, n_hbm, wq, wk, wv, a, far, ya, yfar, hcot_hbm, *refs):
+    d_ref, dn_ref, w_ref, n_ref, h_ref, qkv_ref, sems = refs[-7:]
+    rows = n_ref.shape[0]
+    qw = GROUP * HD
+    first = fetch([(n_hbm, n_ref, sems.at[7])])[0]
+    copies = fetch(weight_copies((wq, wk, wv, a, far, ya, yfar), starts, c, w_ref, sems))
+    cots = fetch([(hcot_hbm.at[:, c * qw : (c + 1) * qw], h_ref, sems.at[8])])[0]
+    first.wait()
+    total = None
+    for i, (start, count, waits) in enumerate(piece_rows(wq.shape[0])):
+        for k in waits:
+            copies[k].wait()
+        at = pl.ds(pl.multiple_of(off_ref[i], 128), count)
+        part = jnp.dot(
+            n_ref[:, at], w_ref[start : start + count, :], preferred_element_type=jnp.float32
+        )
+        total = part if total is None else total + part
+    qkv_ref[...] = total.astype(jnp.bfloat16)
+    cots.wait()
+    mem = rows - (rows // 128) * 128
+    seg_len = rows - mem
+    keys = jnp.concatenate([qkv_ref[:, qw : qw + HD], qkv_ref[seg_len:, qw : qw + HD]], 0)
+    values = jnp.concatenate([qkv_ref[:, qw + HD :], qkv_ref[seg_len:, qw + HD :]], 0)
+    scale = HD ** (-0.5)
+    wide = rows + mem
+    row = lax.broadcasted_iota(jnp.int32, (rows, wide), 0)
+    col = lax.broadcasted_iota(jnp.int32, (rows, wide), 1)
+    need = jnp.where(col < seg_len, col, jnp.where(col < rows, 0, col - mem))
+    seen = row >= need
+    d_keys = None
+    d_values = None
+    for g in range(GROUP):
+        q = qkv_ref[:, g * HD : (g + 1) * HD]
+        da = h_ref[:, g * HD : (g + 1) * HD]
+        s = jnp.where(seen, times_t(q, keys) * scale, -1e30)
+        e = jnp.exp(s - jnp.max(s, -1, keepdims=True))
+        p = e / jnp.sum(e, -1, keepdims=True)
+        dp = times_t(da, values)
+        ds = (p * (dp - jnp.sum(p * dp, -1, keepdims=True)) * scale).astype(jnp.bfloat16)
+        d_ref[:, g * HD : (g + 1) * HD] = jnp.dot(
+            ds, keys, preferred_element_type=jnp.float32
+        ).astype(jnp.bfloat16)
+        dk = inner_rows(ds, q)
+        dv = inner_rows(p.astype(jnp.bfloat16), da)
+        d_keys = dk if d_keys is None else d_keys + dk
+        d_values = dv if d_values is None else d_values + dv
+    for at, both in ((qw, d_keys), (qw + HD, d_values)):
+        d_ref[:seg_len, at : at + HD] = both[:seg_len].astype(jnp.bfloat16)
+        d_ref[seg_len:, at : at + HD] = (both[seg_len:rows] + both[rows:]).astype(jnp.bfloat16)
+    for i, (start, count, _) in enumerate(piece_rows(wq.shape[0])):
+        at = pl.ds(pl.multiple_of(off_ref[i], 128), count)
+        part = times_t(d_ref[...], w_ref[start : start + count, :])
+        dn_ref[:, at] = refs[0][:, at] + part if len(refs) > 7 else part
+
+
+def rows_kernel(dn_ref, tok_ref, mem_ref, gain_ref, cot_ref, token_ref, memory_ref, gg_ref):
+    seg_len = tok_ref.shape[0]
+    gain = gain_ref[...].astype(jnp.float32)
+    step = mem_ref.shape[0]
+
+    def piece(rows, dn, cot):
+        zf = rows.astype(jnp.float32)
+        inv = lax.rsqrt(jnp.mean(zf * zf, -1, keepdims=True) + 1e-05)
+        unit = zf * inv
+        gg_ref[...] += jnp.sum(dn * unit, 0, keepdims=True)
+        du = dn * gain
+        out = cot.astype(jnp.float32) + inv * (
+            du - unit * jnp.mean(du * unit, -1, keepdims=True)
+        )
+        return out.astype(jnp.bfloat16)
+
+    gg_ref[...] = jnp.zeros_like(gg_ref)
+
+    @pl.loop(0, seg_len // step)
+    def _(i):
+        at = pl.ds(pl.multiple_of(i * step, step), step)
+        token_ref[at, :] = piece(tok_ref[at, :], dn_ref[at, :], cot_ref[at, :])
+
+    memory_ref[...] = piece(mem_ref[...], dn_ref[seg_len:, :], cot_ref[seg_len:, :])
+
+
+def turn_kernel(n0, n1, n2, n3, out_ref, cat_ref):
+    rows = n0.shape[0]
+    for i, ref in enumerate((n0, n1, n2, n3)):
+        cat_ref[i * rows : (i + 1) * rows, :] = ref[...]
+    for i in range(out_ref.shape[0] // 256):
+        at = slice(256 * i, 256 * (i + 1))
+        out_ref[at, :] = cat_ref[:, at].T
+
+
+def grads_kernel(place_ref, nt_ref, d0, d1, d2, d3, *refs):
+    other_ref, q_ref, k_ref, v_ref, dcat_ref = refs[-5:]
+
+    @pl.when(place_ref[5] == 1)
+    def _():
+        rows = d0.shape[0]
+        for i, ref in enumerate((d0, d1, d2, d3)):
+            dcat_ref[i * rows : (i + 1) * rows, :] = ref[...]
+        block = other_ref.shape[0]
+        qw = GROUP * HD
+        other = pl.ds(pl.multiple_of(place_ref[2], 128), block)
+        mine = pl.ds(pl.multiple_of(place_ref[3], 128), block)
+        other_ref[...] = jnp.dot(
+            nt_ref[other, :], dcat_ref[...], preferred_element_type=jnp.float32
+        ).astype(jnp.bfloat16)
+        total = jnp.dot(nt_ref[mine, :], dcat_ref[...], preferred_element_type=jnp.float32)
+        q_ref[...] = total[:, :qw]
+        k_ref[...] = total[:, qw : qw + HD]
+        v_ref[...] = total[:, qw + HD :]
+
+
+def place_kernel(heads, place_ref, *refs):
+    recvs = refs[: len(heads)]
+    q_ref, k_ref, v_ref, q_buf, k_buf, v_buf, sems = refs[-7:]
+    qw = GROUP * HD
+
+    @pl.when(place_ref[5] == 0)
+    def _():
+        for c, recv in zip(heads, recvs):
+            q_buf[...] = recv[:, :qw].astype(jnp.float32)
+            k_buf[...] = recv[:, qw : qw + HD].astype(jnp.float32)
+            v_buf[...] = recv[:, qw + HD :].astype(jnp.float32)
+            copies = [
+                pltpu.make_async_copy(buf, ref.at[:, c * wide : (c + 1) * wide], sems.at[k])
+                for k, (buf, ref, wide) in enumerate(
+                    ((q_buf, q_ref, qw), (k_buf, k_ref, HD), (v_buf, v_ref, HD))
+                )
+            ]
+            for copy in copies:
+                copy.start()
+            for copy in copies:
+                copy.wait()
+
+
+def copy_kernel(*refs):
+    count = len(refs) // 2
+    for src, dst in zip(refs[:count], refs[count:]):
+        dst[...] = src[...]
+
+
+class Order:
+    def __init__(self, mark):
+        self.mark = mark
+
+    def point(self, *values):
+        out = lax.optimization_barrier((self.mark,) + values)
+        self.mark = out[0]
+        return out[1] if len(values) == 1 else out[1:]
+
+
+def on_line(inputs, memory, out_cot, head_cot, w_query, w_key, w_value, gain):
+    tok = inputs[0, 0]
+    mem = memory[0, 0]
+    ocot = out_cot[0, 0]
+    hcot = head_cot[0, 0]
+    ws = (w_query[0], w_key[0], w_value[0])
+    width = tok.shape[1]
+    rows = tok.shape[0] + mem.shape[0]
+    block = w_query.shape[1]
+    quarter = block // 2
+    qw = GROUP * HD
+    cw = qw + 2 * HD
+    z = lax.axis_index("seg")
+    grp = lax.axis_index("grp")
+    pair = z // 2
+    inner = (z == 1) | (z == 2)
+    partner = z + 1 - 2 * (z % 2)
+    far_in = jnp.where(z < 2, 2, 1)
+    far_out = jnp.where(z < 2, 3, 0)
+    mine = grp * quarter
+    theirs = (1 - grp) * quarter
+    offsets = jnp.stack(
+        [z * block]
+        + [b * block + mine for b in (partner, far_out, far_in)]
+        + [b * block + theirs for b in (partner, far_out, far_in)]
+    ).astype(jnp.int32)
+    places = jnp.stack(
+        [
+            pair * 2 * block,
+            (1 - pair) * 2 * block,
+            pair * block,
+            (1 - pair) * block,
+            grp,
+            inner.astype(jnp.int32),
+        ]
+    ).astype(jnp.int32)
+
+    smem = pl.BlockSpec(memory_space=pltpu.SMEM)
+    vmem = pl.BlockSpec(memory_space=pltpu.VMEM)
+    bf16 = jnp.bfloat16
+    f32 = jnp.float32
+
+    def shape(r, c, dtype=bf16):
+        return jax.ShapeDtypeStruct((r, c), dtype)
+
+    free = pl.CostEstimate(flops=0, bytes_accessed=0, transcendentals=0)
+    anywhere = pl.BlockSpec(memory_space=pl.ANY)
+    hbm = pl.BlockSpec(memory_space=pltpu.HBM)
+
+    def part(r, c, at=0):
+        return pl.BlockSpec((r, c), lambda *_: (0, at), pipeline_mode=pl.Buffered(1))
+
+    def own_w(c):
+        return [part(block, qw, c), part(block, HD, c), part(block, HD, c)]
+
+    def call(kernel, outs, args, specs=None, mib=20, scratch=(), smems=1, aliases=None, out_specs=None):
+        specs = specs or {}
+        out_specs = out_specs or {}
+        args = tuple(
+            pltpu.with_memory_space_constraint(x, pltpu.HBM) if specs.get(k) is hbm else x
+            for k, x in enumerate(args)
+        )
+        many = isinstance(outs, tuple)
+        out_list = outs if many else (outs,)
+        ins = [smem] * smems + [specs.get(k) or part(*args[k].shape) for k in range(smems, len(args))]
+        ends = tuple(out_specs.get(k) or part(*o.shape) for k, o in enumerate(out_list))
+        return pl.pallas_call(
+            kernel,
+            grid=(1,),
+            out_shape=outs,
+            in_specs=ins,
+            out_specs=ends if many else ends[0],
+            scratch_shapes=scratch,
+            input_output_aliases=aliases or {},
+            compiler_params=pltpu.CompilerParams(vmem_limit_bytes=mib * MIB),
+            cost_estimate=free,
+        )(*args)
+
+    def permute(value, axis, route):
+        return lax.ppermute(value, axis, route)
+
+    def z_and(value):
+        return jnp.concatenate(value, 0)
+
+    order = Order(z.astype(jnp.int32))
+    h01, h23 = call(
+        halves_kernel,
+        (shape(block, cw), shape(block, cw)),
+        (places,) + ws,
+        specs={k: hbm for k in (1, 2, 3)},
+        scratch=[pltpu.SemaphoreType.DMA((12,))],
+    )
+
+    def head(i, pieces, starts, dn=()):
+        args = (offsets, normed) + ws + tuple(pieces) + (hcot,)
+        n = len(args)
+        return call(
+            functools.partial(head_kernel, i, starts),
+            (shape(rows, cw), shape(rows, width, f32)),
+            args + dn,
+            specs={k: hbm for k in range(1, n)} | {6: anywhere},
+            scratch=[
+                pltpu.VMEM((width, cw), bf16),
+                pltpu.VMEM((rows, width), bf16),
+                pltpu.VMEM((rows, qw), bf16),
+                pltpu.VMEM((rows, cw), bf16),
+                pltpu.SemaphoreType.DMA((9,)),
+            ],
+            aliases={n: 1} if dn else None,
+        )
+
+    whole_shapes = tuple(shape(block, n * HEADS, f32) for n in (qw, HD, HD))
+
+    def grads(i, n_t, ds, before):
+        args = (places, n_t) + tuple(ds) + tuple(before)
+        out = call(
+            grads_kernel,
+            (shape(block, cw),) + whole_shapes,
+            args,
+            specs={6 + k: anywhere for k in range(len(before))},
+            out_specs={1 + k: spec for k, spec in enumerate(own_w(i))},
+            scratch=[pltpu.VMEM((4 * rows, cw), bf16)],
+            aliases={6 + k: 1 + k for k in range(len(before))},
+        )
+        return out[0], out[1:]
+
+    def place(heads, recvs, before):
+        n = 1 + len(heads)
+        return call(
+            functools.partial(place_kernel, heads),
+            whole_shapes,
+            (places,) + tuple(recvs) + tuple(before),
+            specs={n + k: anywhere for k in range(3)},
+            out_specs={k: anywhere for k in range(3)},
+            scratch=[pltpu.VMEM((block, n), f32) for n in (qw, HD, HD)]
+            + [pltpu.SemaphoreType.DMA((3,))],
+            aliases={n + k: k for k in range(3)},
+        )
+
+    def pick(b, c):
+        return jnp.where(inner, b, c)
+
+    def send(d):
+        return [permute(d, "seg", r) for r in (FAR_INWARD, ACROSS, INWARD)]
+
+    a01 = permute(h01, "seg", SWAP)
+    normed, near, far = call(
+        functools.partial(normalise_kernel, 2 * block),
+        (shape(rows, width), shape(rows, 2 * block), shape(rows, 2 * block)),
+        (places, tok, mem, gain),
+    )
+    n_across = permute(far, "seg", ACROSS)
+    a01, n_across, h01, h23, normed, near, far = order.point(
+        a01, n_across, h01, h23, normed, near, far
+    )
+    a23 = permute(h23, "seg", SWAP)
+    b0 = permute(z_and([a01[:quarter], h01[:quarter]]), "seg", ACROSS)
+    ya01 = permute(a01, "grp", GRPS)
+    to1 = z_and([a01[quarter:], h01[quarter:]])
+    b0, ya01, a23, to1, h23, near, far = order.point(b0, ya01, a23, to1, h23, near, far)
+    ya23 = permute(a23, "grp", GRPS)
+    n_in = permute(near, "seg", INWARD)
+    b1 = permute(to1, "seg", ACROSS)
+    c0 = permute(b0, "seg", OUTWARD)
+    to2 = z_and([a23[:quarter], h23[:quarter]])
+    to3 = z_and([a23[quarter:], h23[quarter:]])
+    f0 = pick(b0, c0)
+    ya23, n_in, b1, f0, to2, to3, far = order.point(ya23, n_in, b1, f0, to2, to3, far)
+    yf0 = permute(f0, "grp", GRPS)
+    n_far = permute(far, "seg", FAR_INWARD)
+    b2 = permute(to2, "seg", ACROSS)
+    c1 = permute(b1, "seg", OUTWARD)
+    f1 = pick(b1, c1)
+    yf0, n_far, b2, f1, to3 = order.point(yf0, n_far, b2, f1, to3)
+    yf1 = permute(f1, "grp", GRPS)
+    b3 = permute(to3, "seg", ACROSS)
+    c2 = permute(b2, "seg", OUTWARD)
+    d0, dn = head(0, (a01, f0, ya01, yf0), (0, 0))
+    f2 = pick(b2, c2)
+    yf1, b3, f2, d0, dn = order.point(yf1, b3, f2, d0, dn)
+    yf2 = permute(f2, "grp", GRPS)
+    c3 = permute(b3, "seg", OUTWARD)
+    x0 = send(d0)
+    d1, dn = head(1, (a01, f1, ya01, yf1), (quarter, quarter), (dn,))
+    n_t = call(
+        turn_kernel,
+        shape(2 * block, 4 * rows),
+        (near, n_in, n_across, n_far),
+        scratch=[pltpu.VMEM((4 * rows, 2 * block), bf16)],
+        smems=0,
+    )
+    f3 = pick(b3, c3)
+    yf2, f3, x00, x01, x02, d1, dn, n_t = order.point(yf2, f3, *x0, d1, dn, n_t)
+    yf3 = permute(f3, "grp", GRPS)
+    x1 = send(d1)
+    o0, whole = grads(0, n_t, (d0, x02, x01, x00), ())
+    r0 = permute(o0, "seg", OUTWARD)
+    d2, dn = head(2, (a23, f2, ya23, yf2), (0, 0), (dn,))
+    yf3, x10, x11, x12, d2, dn, o0 = order.point(yf3, *x1, d2, dn, o0)
+    x2 = send(d2)
+    o1, whole = grads(1, n_t, (d1, x12, x11, x10), whole)
+    r1 = permute(o1, "seg", OUTWARD)
+    d3, dn = head(3, (a23, f3, ya23, yf3), (quarter, quarter), (dn,))
+    x20, x21, x22, d3, r0, dn, o1 = order.point(*x2, d3, r0, dn, o1)
+    x3 = send(d3)
+    o2, whole = grads(2, n_t, (d2, x22, x21, x20), whole)
+    r2 = permute(o2, "seg", OUTWARD)
+    token_part, memory_part, grad_g = call(
+        rows_kernel,
+        (shape(tok.shape[0], width), shape(mem.shape[0], width), shape(1, width, f32)),
+        (dn, tok, mem, gain, ocot),
+        smems=0,
+    )
+    x30, x31, x32, r1, r2, token_part, memory_part, grad_g = order.point(
+        *x3, r1, r2, token_part, memory_part, grad_g
+    )
+    o3, whole = grads(3, n_t, (d3, x32, x31, x30), whole)
+    r3 = permute(o3, "seg", OUTWARD)
+    below, before = deliver(token_part, memory_part)
+    gains = lax.all_to_all(grad_g.reshape(4, width // 4), "seg", 0, 0, tiled=True)
+    grad_gain = jnp.sum(gains, 0, keepdims=True)
+    whole = place((0, 1, 2), (r0, r1, r2), whole)
+    below = call(copy_kernel, shape(tok.shape[0], width), (below,), smems=0)
+    r3, below, q_, k_, v_ = order.point(r3, below, *whole)
+    grad_query, grad_key, grad_value = place((3,), (r3,), (q_, k_, v_))
+    return (
+        below[None, None],
+        before[None, None],
+        grad_query[None],
+        grad_key[None],
+        grad_value[None],
+        grad_gain,
+    )
+
+
 def solution(mesh):
     in_specs = (
         P("section", ("grp", "seg"), None, None),
@@ -137,6 +621,11 @@
         P(("grp", "section"), "seg", None),
         P(("grp", "section"), "seg"),
     )
+    line = mesh.shape["seg"] == 4 and mesh.shape["grp"] == 2
     return jax.shard_map(
-        on_device, mesh=mesh, in_specs=in_specs, out_specs=out_specs, check_vma=False
-    )
+        on_line if line else on_device,
+        mesh=mesh,
+        in_specs=in_specs,
+        out_specs=out_specs,
+        check_vma=False,
+    )

time: 597 us -> 245 us (0.41)
  waiting for transfers between devices: 469 us -> 90.5 us
  starting transfers between devices: 4.01 us -> 91.6 us
  matrix products: 77.9 us -> 0 us
  Pallas kernels: 0 us -> 53.8 us
  between operations: 14.4 us -> 1.33 us
  local copies, waits for them, and re-layouts: 16.3 us -> 3.65 us
  other arithmetic: 13.3 us -> 3.17 us
    reduce_scatter x3 -> x0, waiting for transfers between devices: 232 us -> none  [the longest x1 144 us: on_device(): lax.psum_scatter(grad_q[None].astype(jnp.bfloat16), 'seg', scatter_dimens...]
    all_gather x3 -> x0, waiting for transfers between devices: 230 us -> none  [the longest x1 143 us: on_device(): lax.all_gather(w_query, 'seg', axis=1, tiled=True)]
    ppermute x0 -> x35, waiting for transfers between devices: none -> 79.5 us  [permute(): return lax.ppermute(value, axis, route)]
    ppermute x0 -> x35, starting transfers between devices: none -> 72.8 us  [permute(): return lax.ppermute(value, axis, route)]
    dot_general x13 -> x0, matrix products: 70.3 us -> none  [the longest x1 13.8 us: on_device(): jnp.einsum('hgqk,khd->qhgd', d_scores, keys, preferred_element_type=jnp.f...]
    pallas_call x0 -> x15, Pallas kernels: none -> 53.8 us  [call(): pl.pallas_call(kernel, grid=(1,), out_shape=outs, in_specs=ins, out_specs...]
    all_to_all x0 -> x1, waiting for transfers between devices: none -> 10.9 us  [on_line(): lax.all_to_all(grad_g.reshape(4, width // 4), 'seg', 0, 0, tiled=True)]
    all_to_all x0 -> x1, starting transfers between devices: none -> 9.3 us  [on_line(): lax.all_to_all(grad_g.reshape(4, width // 4), 'seg', 0, 0, tiled=True)]
  transfers between devices with their start and end apart: 9 -> 38, of which waited for: 7 -> 10; matrix products, arithmetic and copies ran while one was open for 6% -> 1% of each run, Pallas kernels for 0% -> 20%
where the time goes in v2:
time: 245 us; the launch traced here: 244 us
  starting transfers between devices  91.6 us (37%)
  waiting for transfers between devices  90.5 us (37%)
  Pallas kernels  53.8 us (22%)
  local copies, waits for them, and re-layouts  3.65 us (1%)
  other arithmetic  3.17 us (1%)
    ppermute x35, waiting for transfers between devices, permute(): return lax.ppermute(value, axis, route)  79.5 us
    ppermute x35, starting transfers between devices, permute(): return lax.ppermute(value, axis, route)  72.8 us
    pallas_call x15, Pallas kernels, call(): pl.pallas_call(kernel, grid=(1,), out_shape=outs, in_specs=ins, out_specs...  53.8 us
    all_to_all x1, waiting for transfers between devices, on_line(): lax.all_to_all(grad_g.reshape(4, width // 4), 'seg', 0, 0, tiled=True)  10.9 us
    ppermute x2, starting transfers between devices, from_behind(): return lax.ppermute(block, axis, route)  9.44 us
    all_to_all x1, starting transfers between devices, on_line(): lax.all_to_all(grad_g.reshape(4, width // 4), 'seg', 0, 0, tiled=True)  9.3 us
  transfers between devices with their start and end apart: 38, of which 10 were waited for; matrix products, arithmetic and copies ran while one was open for 1% of the time, Pallas kernels for 20%

profile of v2, /device:TPU:7, one launch (start us, length us, event | category | flops | bytes accessed | tf_op | source)
XLA Modules:
  0.0 243.9 jit_solution(6408962447879704763)
XLA Ops:
  6.7 14.6 %collective-permute-done.a = bf16[512,768]{1,0:T(8,128)(2,1)S(1)} collective-permute-done((bf16[512,768]{1,0:T(8,128)(2,1)S(1)}, bf16[512,768]{1,0:T(8,128)(2,1)S(1)}, u32[]{:S(2)}, u32[]{:S(2)}) %collective-permute-start) | collective-permute-done | bytes 786464 | tf_op jit(solution)/shard_map/ppermute | solution.py:449
  22.1 5.0 %collective-permute-start.4 = (bf16[512,768]{1,0:T(8,128)(2,1)S(1)}, bf16[512,768]{1,0:T(8,128)(2,1)S(1)}, u32[]{:S(2)}, u32[]{:S(2)}) collective-permute-start(bf16[512,768]{1,0:T(8,128)(2,1)S(1)} %get-tuple-element.122), channel_id=1, source_target_pairs={{0,1},{1,0},{2,3},{3,2},{4,5},{5,4},{6,7},{7,6},{8,9},{9,8},{10,11... | collective-permute-start | bytes 2359304 | tf_op jit(solution)/shard_map/ppermute | solution.py:449
  27.5 15.4 %collective-permute-done.4.a = bf16[512,768]{1,0:T(8,128)(2,1)S(1)} collective-permute-done((bf16[512,768]{1,0:T(8,128)(2,1)S(1)}, bf16[512,768]{1,0:T(8,128)(2,1)S(1)}, u32[]{:S(2)}, u32[]{:S(2)}) %collective-permute-start.4) | collective-permute-done | bytes 786464 | tf_op jit(solution)/shard_map/ppermute | solution.py:449
  45.9 4.1 %collective-permute-start.6 = (bf16[288,1024]{1,0:T(8,128)(2,1)S(1)}, bf16[288,1024]{1,0:T(8,128)(2,1)S(1)}, u32[]{:S(2)}, u32[]{:S(2)}) collective-permute-start(bf16[288,1024]{1,0:T(8,128)(2,1)S(1)} %get-tuple-element.119.n0), channel_id=1, source_target_pairs={{0,1},{3,2},{4,5},{7,6},{8,9},{11,10},{12,13},{15,14},{16,17},{19,... | collective-permute-start | bytes 1769480 | tf_op jit(solution)/shard_map/ppermute | solution.py:449
  52.1 10.1 %collective-permute-done.8 = bf16[512,768]{1,0:T(8,128)(2,1)S(1)} collective-permute-done((bf16[512,768]{1,0:T(8,128)(2,1)S(1)}, bf16[512,768]{1,0:T(8,128)(2,1)S(1)}, u32[]{:S(2)}, u32[]{:S(2)}) %collective-permute-start.8) | collective-permute-done | bytes 786464 | tf_op jit(solution)/shard_map/ppermute | solution.py:449
  69.0 5.7 %collective-permute-start.10 = (bf16[288,1024]{1,0:T(8,128)(2,1)S(1)}, bf16[288,1024]{1,0:T(8,128)(2,1)S(1)}, u32[]{:S(2)}, u32[]{:S(2)}) collective-permute-start(bf16[288,1024]{1,0:T(8,128)(2,1)S(1)} %get-tuple-element.125), channel_id=1, source_target_pairs={{0,2},{3,1},{4,6},{7,5},{8,10},{11,9},{12,14},{15,13},{16,18},{19,... | collective-permute-start | bytes 1769480 | tf_op jit(solution)/shard_map/ppermute | solution.py:449
  74.7 7.3 %collective-permute-done.12 = bf16[512,768]{1,0:T(8,128)(2,1)S(1)} collective-permute-done((bf16[512,768]{1,0:T(8,128)(2,1)S(1)}, bf16[512,768]{1,0:T(8,128)(2,1)S(1)}, u32[]{:S(2)}, u32[]{:S(2)}) %collective-permute-start.12) | collective-permute-done | bytes 786464 | tf_op jit(solution)/shard_map/ppermute | solution.py:449
  86.6 7.7 %shard_map.129 = (bf16[288,768]{1,0:T(8,128)(2,1)S(1)}, f32[288,2048]{1,0:T(8,128)S(1)}) custom-call(s32[7]{0:T(128)S(1)} %stack.63.off_ref, bf16[288,2048]{1,0:T(8,128)(2,1)} %copy-done, bf16[512,2048]{1,0:T(8,128)(2,1)} %bitcast.35, bf16[512,512]{1,0:T(8,128)(2,1)} %bitcast.46, bf16[512,512]{1,0:T(8,128)(2,1)} %bitcast.51, bf16[512,768]{1,0:T(8,128)(2,1)} %copy-done.12, ...), custom_call_target="tpu_custom_call" | custom-call | tf_op jit(solution)/shard_map/pallas_call | solution.py:436
  94.3 19.8 %collective-permute-done.15 = bf16[512,768]{1,0:T(8,128)(2,1)} collective-permute-done((bf16[512,768]{1,0:T(8,128)(2,1)}, bf16[512,768]{1,0:T(8,128)(2,1)}, u32[]{:S(2)}, u32[]{:S(2)}) %collective-permute-start.15) | collective-permute-done | bytes 786464 | tf_op jit(solution)/shard_map/ppermute | solution.py:449
  116.8 6.3 %collective-permute-start.20 = (bf16[288,768]{1,0:T(8,128)(2,1)S(1)}, bf16[288,768]{1,0:T(8,128)(2,1)S(1)}, u32[]{:S(2)}, u32[]{:S(2)}) collective-permute-start(bf16[288,768]{1,0:T(8,128)(2,1)S(1)} %get-tuple-element.139.d0), channel_id=1, source_target_pairs={{0,1},{3,2},{4,5},{7,6},{8,9},{11,10},{12,13},{15,14},{16,17},{19,... | collective-permute-start | bytes 1327112 | tf_op jit(solution)/shard_map/ppermute | solution.py:449
  123.7 3.9 %collective-permute-start.18 = (bf16[288,768]{1,0:T(8,128)(2,1)S(1)}, bf16[288,768]{1,0:T(8,128)(2,1)S(1)}, u32[]{:S(2)}, u32[]{:S(2)}) collective-permute-start(bf16[288,768]{1,0:T(8,128)(2,1)S(1)} %get-tuple-element.139.d0), channel_id=1, source_target_pairs={{0,2},{3,1},{4,6},{7,5},{8,10},{11,9},{12,14},{15,13},{16,18},{19,... | collective-permute-start | bytes 1327112 | tf_op jit(solution)/shard_map/ppermute | solution.py:449
  128.3 7.9 %shard_map.130 = (bf16[288,768]{1,0:T(8,128)(2,1)S(1)}, f32[288,2048]{1,0:T(8,128)S(1)}) custom-call(s32[7]{0:T(128)S(1)} %stack.63.off_ref, bf16[288,2048]{1,0:T(8,128)(2,1)} %copy-done, bf16[512,2048]{1,0:T(8,128)(2,1)} %bitcast.36, bf16[512,512]{1,0:T(8,128)(2,1)} %bitcast.47, bf16[512,512]{1,0:T(8,128)(2,1)} %bitcast.52, ...), custom_call_target="tpu_custom_call", output_to_operand_aliasing={{1}: (10, {})} | custom-call | tf_op jit(solution)/shard_map/pallas_call | solution.py:436
  137.8 4.0 %collective-permute-start.24 = (bf16[288,768]{1,0:T(8,128)(2,1)S(1)}, bf16[288,768]{1,0:T(8,128)(2,1)S(1)}, u32[]{:S(2)}, u32[]{:S(2)}) collective-permute-start(bf16[288,768]{1,0:T(8,128)(2,1)S(1)} %get-tuple-element.149.d0), channel_id=1, source_target_pairs={{0,1},{3,2},{4,5},{7,6},{8,9},{11,10},{12,13},{15,14},{16,17},{19,... | collective-permute-start | bytes 1327112 | tf_op jit(solution)/shard_map/ppermute | solution.py:449
  142.5 3.7 %collective-permute-start.22 = (bf16[288,768]{1,0:T(8,128)(2,1)S(1)}, bf16[288,768]{1,0:T(8,128)(2,1)S(1)}, u32[]{:S(2)}, u32[]{:S(2)}) collective-permute-start(bf16[288,768]{1,0:T(8,128)(2,1)S(1)} %get-tuple-element.149.d0), channel_id=1, source_target_pairs={{0,2},{3,1},{4,6},{7,5},{8,10},{11,9},{12,14},{15,13},{16,18},{19,... | collective-permute-start | bytes 1327112 | tf_op jit(solution)/shard_map/ppermute | solution.py:449
  149.2 7.9 %shard_map.132 = (bf16[288,768]{1,0:T(8,128)(2,1)S(1)}, f32[288,2048]{1,0:T(8,128)S(1)}) custom-call(s32[7]{0:T(128)S(1)} %stack.63.off_ref, bf16[288,2048]{1,0:T(8,128)(2,1)} %copy-done, bf16[512,2048]{1,0:T(8,128)(2,1)} %bitcast.37, bf16[512,512]{1,0:T(8,128)(2,1)} %bitcast.48, bf16[512,512]{1,0:T(8,128)(2,1)} %bitcast.53, ...), custom_call_target="tpu_custom_call", output_to_operand_aliasing={{1}: (10, {})} | custom-call | tf_op jit(solution)/shard_map/pallas_call | solution.py:436
  157.1 4.0 %collective-permute-start.27 = (bf16[288,768]{1,0:T(8,128)(2,1)S(1)}, bf16[288,768]{1,0:T(8,128)(2,1)S(1)}, u32[]{:S(2)}, u32[]{:S(2)}) collective-permute-start(bf16[288,768]{1,0:T(8,128)(2,1)S(1)} %get-tuple-element.159.d0), channel_id=1, source_target_pairs={{0,1},{3,2},{4,5},{7,6},{8,9},{11,10},{12,13},{15,14},{16,17},{19,... | collective-permute-start | bytes 1327112 | tf_op jit(solution)/shard_map/ppermute | solution.py:449
  168.8 7.9 %shard_map.134 = (bf16[288,768]{1,0:T(8,128)(2,1)S(1)}, f32[288,2048]{1,0:T(8,128)S(1)}) custom-call(s32[7]{0:T(128)S(1)} %stack.63.off_ref, bf16[288,2048]{1,0:T(8,128)(2,1)} %copy-done, bf16[512,2048]{1,0:T(8,128)(2,1)} %bitcast.38, bf16[512,512]{1,0:T(8,128)(2,1)} %bitcast.49, bf16[512,512]{1,0:T(8,128)(2,1)} %bitcast.54, ...), custom_call_target="tpu_custom_call", output_to_operand_aliasing={{1}: (10, {})} | custom-call | tf_op jit(solution)/shard_map/pallas_call | solution.py:436
  179.7 6.3 %collective-permute-start.31 = (bf16[288,768]{1,0:T(8,128)(2,1)S(1)}, bf16[288,768]{1,0:T(8,128)(2,1)S(1)}, u32[]{:S(2)}, u32[]{:S(2)}) collective-permute-start(bf16[288,768]{1,0:T(8,128)(2,1)S(1)} %get-tuple-element.171.d0), channel_id=1, source_target_pairs={{0,1},{3,2},{4,5},{7,6},{8,9},{11,10},{12,13},{15,14},{16,17},{19,... | collective-permute-start | bytes 1327112 | tf_op jit(solution)/shard_map/ppermute | solution.py:449
  186.7 3.7 %collective-permute-start.29 = (bf16[288,768]{1,0:T(8,128)(2,1)S(1)}, bf16[288,768]{1,0:T(8,128)(2,1)S(1)}, u32[]{:S(2)}, u32[]{:S(2)}) collective-permute-start(bf16[288,768]{1,0:T(8,128)(2,1)S(1)} %get-tuple-element.171.d0), channel_id=1, source_target_pairs={{0,2},{3,1},{4,6},{7,5},{8,10},{11,9},{12,14},{15,13},{16,18},{19,... | collective-permute-start | bytes 1327112 | tf_op jit(solution)/shard_map/ppermute | solution.py:449
  196.0 6.2 %collective-permute-done.33.refs_2_ = bf16[512,768]{1,0:T(8,128)(2,1)S(1)} collective-permute-done((bf16[512,768]{1,0:T(8,128)(2,1)S(1)}, bf16[512,768]{1,0:T(8,128)(2,1)S(1)}, u32[]{:S(2)}, u32[]{:S(2)}) %collective-permute-start.33) | collective-permute-done | bytes 786464 | tf_op jit(solution)/shard_map/ppermute | solution.py:449
  202.1 8.1 %collective-permute-start.35 = (bf16[256,2048]{1,0:T(8,128)(2,1)}, bf16[256,2048]{1,0:T(8,128)(2,1)S(1)}, u32[]{:S(2)}, u32[]{:S(2)}) collective-permute-start(bf16[256,2048]{1,0:T(8,128)(2,1)} %get-tuple-element.190), channel_id=1, source_target_pairs={{4,0},{8,4},{12,8},{5,1},{9,5},{13,9},{6,2},{10,6},{14,10},{7,3},{... | collective-permute-start | bytes 3145736 | tf_op jit(solution)/shard_map/ppermute | solution.py:19
  214.8 9.3 %all-to-all-start = ((f32[4,1,512]{2,1,0:T(1,128)}), f32[4,1,512]{2,1,0:T(1,128)S(1)}, u32[]{:S(2)}, u32[]{:S(2)}) async-start(f32[4,1,512]{2,1,0:T(1,128)} %bitcast.32), calls=%async_computation | async-start | bytes 16384 | tf_op jit(solution)/shard_map/all_to_all | solution.py:589
  224.1 4.2 %shard_map.140 = (f32[512,2048]{1,0:T(8,128)}, f32[512,512]{1,0:T(8,128)}, f32[512,512]{1,0:T(8,128)}) custom-call(s32[6]{0:T(128)S(1)} %stack.55.place_ref, bf16[512,768]{1,0:T(8,128)(2,1)S(1)} %collective-permute-done.28.refs_0_, bf16[512,768]{1,0:T(8,128)(2,1)S(1)} %collective-permute-done.32.refs_1_, ...), custom_call_target="tpu_custom_call", output_to_operand_aliasing={{0}: (4, {}), {1}: (5, {}), {2}: (6, {})} | custom-call | tf_op jit(solution)/shard_map/pallas_call | solution.py:436
  228.3 10.9 %all-to-all-done = f32[4,1,512]{2,1,0:T(1,128)S(1)} async-done(((f32[4,1,512]{2,1,0:T(1,128)}), f32[4,1,512]{2,1,0:T(1,128)S(1)}, u32[]{:S(2)}, u32[]{:S(2)}) %all-to-all-start) | async-done | bytes 8224 | tf_op jit(solution)/shard_map/all_to_all | solution.py:589
  (120 shorter events, 58.8 us)
Async XLA Ops:
  2.8 18.5 %collective-permute-start = (bf16[512,768]{1,0:T(8,128)(2,1)S(1)}, bf16[512,768]{1,0:T(8,128)(2,1)S(1)}, u32[]{:S(2)}, u32[]{:S(2)}) collective-permute-start(bf16[512,768]{1,0:T(8,128)(2,1)S(1)} %get-tuple-element.114), channel_id=1, source_target_pairs={{0,1},{1,0},{2,3},{3,2},{4,5},{5,4},{6,7},{7,6},{8,9},{9,8},{10,11... | collective-permute-start | bytes 2359304 | tf_op jit(solution)/shard_map/ppermute | solution.py:449
  22.1 20.7 %collective-permute-start.4 = (bf16[512,768]{1,0:T(8,128)(2,1)S(1)}, bf16[512,768]{1,0:T(8,128)(2,1)S(1)}, u32[]{:S(2)}, u32[]{:S(2)}) collective-permute-start(bf16[512,768]{1,0:T(8,128)(2,1)S(1)} %get-tuple-element.122), channel_id=1, source_target_pairs={{0,1},{1,0},{2,3},{3,2},{4,5},{5,4},{6,7},{7,6},{8,9},{9,8},{10,11... | collective-permute-start | bytes 2359304 | tf_op jit(solution)/shard_map/ppermute | solution.py:449
  27.2 16.6 %collective-permute-start.3 = (bf16[512,768]{1,0:T(8,128)(2,1)S(1)}, bf16[512,768]{1,0:T(8,128)(2,1)S(1)}, u32[]{:S(2)}, u32[]{:S(2)}) collective-permute-start(bf16[512,768]{1,0:T(8,128)(2,1)S(1)} %collective-permute-done.a), channel_id=1, source_target_pairs={{0,16},{16,0},{1,17},{17,1},{2,18},{18,2},{3,19},{19,3},{4,20},{20... | collective-permute-start | bytes 2359304 | tf_op jit(solution)/shard_map/ppermute | solution.py:449
  44.7 17.6 %collective-permute-start.8 = (bf16[512,768]{1,0:T(8,128)(2,1)S(1)}, bf16[512,768]{1,0:T(8,128)(2,1)S(1)}, u32[]{:S(2)}, u32[]{:S(2)}) collective-permute-start(bf16[512,768]{1,0:T(8,128)(2,1)S(1)} %collective-permute-done.2), channel_id=1, source_target_pairs={{1,0},{2,3},{5,4},{6,7},{9,8},{10,11},{13,12},{14,15},{17,16},{18,... | collective-permute-start | bytes 2359304 | tf_op jit(solution)/shard_map/ppermute | solution.py:449
  45.9 16.4 %collective-permute-start.6 = (bf16[288,1024]{1,0:T(8,128)(2,1)S(1)}, bf16[288,1024]{1,0:T(8,128)(2,1)S(1)}, u32[]{:S(2)}, u32[]{:S(2)}) collective-permute-start(bf16[288,1024]{1,0:T(8,128)(2,1)S(1)} %get-tuple-element.119.n0), channel_id=1, source_target_pairs={{0,1},{3,2},{4,5},{7,6},{8,9},{11,10},{12,13},{15,14},{16,17},{19,... | collective-permute-start | bytes 1769480 | tf_op jit(solution)/shard_map/ppermute | solution.py:449
  65.9 16.1 %collective-permute-start.12 = (bf16[512,768]{1,0:T(8,128)(2,1)S(1)}, bf16[512,768]{1,0:T(8,128)(2,1)S(1)}, u32[]{:S(2)}, u32[]{:S(2)}) collective-permute-start(bf16[512,768]{1,0:T(8,128)(2,1)S(1)} %collective-permute-done.7), channel_id=1, source_target_pairs={{1,0},{2,3},{5,4},{6,7},{9,8},{10,11},{13,12},{14,15},{17,16},{18,... | collective-permute-start | bytes 2359304 | tf_op jit(solution)/shard_map/ppermute | solution.py:449
  67.2 15.8 %collective-permute-start.11 = (bf16[512,768]{1,0:T(8,128)(2,1)S(1)}, bf16[512,768]{1,0:T(8,128)(2,1)}, u32[]{:S(2)}, u32[]{:S(2)}) collective-permute-start(bf16[512,768]{1,0:T(8,128)(2,1)S(1)} %pad_maximum_fusion.2), channel_id=1, source_target_pairs={{1,2},{2,1},{5,6},{6,5},{9,10},{10,9},{13,14},{14,13},{17,18},{18,... | collective-permute-start | bytes 2359304 | tf_op jit(solution)/shard_map/ppermute | solution.py:449
  83.0 31.1 %collective-permute-start.15 = (bf16[512,768]{1,0:T(8,128)(2,1)}, bf16[512,768]{1,0:T(8,128)(2,1)}, u32[]{:S(2)}, u32[]{:S(2)}) collective-permute-start(bf16[512,768]{1,0:T(8,128)(2,1)} %collective-permute-done.11), channel_id=1, source_target_pairs={{1,0},{2,3},{5,4},{6,7},{9,8},{10,11},{13,12},{14,15},{17,16},{18,... | collective-permute-start | bytes 2359304 | tf_op jit(solution)/shard_map/ppermute | solution.py:449
  84.3 31.0 %collective-permute-start.14 = (bf16[512,768]{1,0:T(8,128)(2,1)}, bf16[512,768]{1,0:T(8,128)(2,1)}, u32[]{:S(2)}, u32[]{:S(2)}) collective-permute-start(bf16[512,768]{1,0:T(8,128)(2,1)} %pad_maximum_fusion.3), channel_id=1, source_target_pairs={{1,2},{2,1},{5,6},{6,5},{9,10},{10,9},{13,14},{14,13},{17,18},{18,... | collective-permute-start | bytes 2359304 | tf_op jit(solution)/shard_map/ppermute | solution.py:449
  85.9 29.5 %collective-permute-start.13 = (bf16[512,768]{1,0:T(8,128)(2,1)S(1)}, bf16[512,768]{1,0:T(8,128)(2,1)}, u32[]{:S(2)}, u32[]{:S(2)}) collective-permute-start(bf16[512,768]{1,0:T(8,128)(2,1)S(1)} %broadcast_select_fusion.2.far), channel_id=1, source_target_pairs={{0,16},{16,0},{1,17},{17,1},{2,18},{18,2},{3,19},{19,3},{4,20},{20... | collective-permute-start | bytes 2359304 | tf_op jit(solution)/shard_map/ppermute | solution.py:449
  115.4 20.8 %collective-permute-start.17 = (bf16[512,768]{1,0:T(8,128)(2,1)}, bf16[512,768]{1,0:T(8,128)(2,1)S(1)}, u32[]{:S(2)}, u32[]{:S(2)}) collective-permute-start(bf16[512,768]{1,0:T(8,128)(2,1)} %collective-permute-done.14), channel_id=1, source_target_pairs={{1,0},{2,3},{5,4},{6,7},{9,8},{10,11},{13,12},{14,15},{17,16},{18,... | collective-permute-start | bytes 2359304 | tf_op jit(solution)/shard_map/ppermute | solution.py:449
  116.7 19.6 %collective-permute-start.16 = (bf16[512,768]{1,0:T(8,128)(2,1)S(1)}, bf16[512,768]{1,0:T(8,128)(2,1)S(1)}, u32[]{:S(2)}, u32[]{:S(2)}) collective-permute-start(bf16[512,768]{1,0:T(8,128)(2,1)S(1)} %broadcast_select_fusion.1.far), channel_id=1, source_target_pairs={{0,16},{16,0},{1,17},{17,1},{2,18},{18,2},{3,19},{19,3},{4,20},{20... | collective-permute-start | bytes 2359304 | tf_op jit(solution)/shard_map/ppermute | solution.py:449
  116.8 19.5 %collective-permute-start.20 = (bf16[288,768]{1,0:T(8,128)(2,1)S(1)}, bf16[288,768]{1,0:T(8,128)(2,1)S(1)}, u32[]{:S(2)}, u32[]{:S(2)}) collective-permute-start(bf16[288,768]{1,0:T(8,128)(2,1)S(1)} %get-tuple-element.139.d0), channel_id=1, source_target_pairs={{0,1},{3,2},{4,5},{7,6},{8,9},{11,10},{12,13},{15,14},{16,17},{19,... | collective-permute-start | bytes 1327112 | tf_op jit(solution)/shard_map/ppermute | solution.py:449
  136.3 20.8 %collective-permute-start.21 = (bf16[512,768]{1,0:T(8,128)(2,1)S(1)}, bf16[512,768]{1,0:T(8,128)(2,1)S(1)}, u32[]{:S(2)}, u32[]{:S(2)}) collective-permute-start(bf16[512,768]{1,0:T(8,128)(2,1)S(1)} %broadcast_select_fusion.far), channel_id=1, source_target_pairs={{0,16},{16,0},{1,17},{17,1},{2,18},{18,2},{3,19},{19,3},{4,20},{20... | collective-permute-start | bytes 2359304 | tf_op jit(solution)/shard_map/ppermute | solution.py:449
  137.8 19.2 %collective-permute-start.24 = (bf16[288,768]{1,0:T(8,128)(2,1)S(1)}, bf16[288,768]{1,0:T(8,128)(2,1)S(1)}, u32[]{:S(2)}, u32[]{:S(2)}) collective-permute-start(bf16[288,768]{1,0:T(8,128)(2,1)S(1)} %get-tuple-element.149.d0), channel_id=1, source_target_pairs={{0,1},{3,2},{4,5},{7,6},{8,9},{11,10},{12,13},{15,14},{16,17},{19,... | collective-permute-start | bytes 1327112 | tf_op jit(solution)/shard_map/ppermute | solution.py:449
  147.9 28.8 %collective-permute-start.28 = (bf16[512,768]{1,0:T(8,128)(2,1)S(1)}, bf16[512,768]{1,0:T(8,128)(2,1)S(1)}, u32[]{:S(2)}, u32[]{:S(2)}) collective-permute-start(bf16[512,768]{1,0:T(8,128)(2,1)S(1)} %get-tuple-element.158), channel_id=1, source_target_pairs={{1,0},{2,3},{5,4},{6,7},{9,8},{10,11},{13,12},{14,15},{17,16},{18,... | collective-permute-start | bytes 2359304 | tf_op jit(solution)/shard_map/ppermute | solution.py:449
  157.1 19.6 %collective-permute-start.27 = (bf16[288,768]{1,0:T(8,128)(2,1)S(1)}, bf16[288,768]{1,0:T(8,128)(2,1)S(1)}, u32[]{:S(2)}, u32[]{:S(2)}) collective-permute-start(bf16[288,768]{1,0:T(8,128)(2,1)S(1)} %get-tuple-element.159.d0), channel_id=1, source_target_pairs={{0,1},{3,2},{4,5},{7,6},{8,9},{11,10},{12,13},{15,14},{16,17},{19,... | collective-permute-start | bytes 1327112 | tf_op jit(solution)/shard_map/ppermute | solution.py:449
  161.2 15.5 %collective-permute-start.26 = (bf16[288,768]{1,0:T(8,128)(2,1)S(1)}, bf16[288,768]{1,0:T(8,128)(2,1)S(1)}, u32[]{:S(2)}, u32[]{:S(2)}) collective-permute-start(bf16[288,768]{1,0:T(8,128)(2,1)S(1)} %get-tuple-element.159.d0), channel_id=1, source_target_pairs={{1,2},{2,1},{5,6},{6,5},{9,10},{10,9},{13,14},{14,13},{17,18},{18,... | collective-permute-start | bytes 1327112 | tf_op jit(solution)/shard_map/ppermute | solution.py:449
  167.5 26.1 %collective-permute-start.32 = (bf16[512,768]{1,0:T(8,128)(2,1)S(1)}, bf16[512,768]{1,0:T(8,128)(2,1)S(1)}, u32[]{:S(2)}, u32[]{:S(2)}) collective-permute-start(bf16[512,768]{1,0:T(8,128)(2,1)S(1)} %get-tuple-element.170), channel_id=1, source_target_pairs={{1,0},{2,3},{5,4},{6,7},{9,8},{10,11},{13,12},{14,15},{17,16},{18,... | collective-permute-start | bytes 2359304 | tf_op jit(solution)/shard_map/ppermute | solution.py:449
  178.4 23.8 %collective-permute-start.33 = (bf16[512,768]{1,0:T(8,128)(2,1)S(1)}, bf16[512,768]{1,0:T(8,128)(2,1)S(1)}, u32[]{:S(2)}, u32[]{:S(2)}) collective-permute-start(bf16[512,768]{1,0:T(8,128)(2,1)S(1)} %get-tuple-element.178), channel_id=1, source_target_pairs={{1,0},{2,3},{5,4},{6,7},{9,8},{10,11},{13,12},{14,15},{17,16},{18,... | collective-permute-start | bytes 2359304 | tf_op jit(solution)/shard_map/ppermute | solution.py:449
  202.1 37.7 %collective-permute-start.35 = (bf16[256,2048]{1,0:T(8,128)(2,1)}, bf16[256,2048]{1,0:T(8,128)(2,1)S(1)}, u32[]{:S(2)}, u32[]{:S(2)}) collective-permute-start(bf16[256,2048]{1,0:T(8,128)(2,1)} %get-tuple-element.190), channel_id=1, source_target_pairs={{4,0},{8,4},{12,8},{5,1},{9,5},{13,9},{6,2},{10,6},{14,10},{7,3},{... | collective-permute-start | bytes 3145736 | tf_op jit(solution)/shard_map/ppermute | solution.py:19
  212.3 28.6 %collective-permute-start.34 = (bf16[512,768]{1,0:T(8,128)(2,1)}, bf16[512,768]{1,0:T(8,128)(2,1)}, u32[]{:S(2)}, u32[]{:S(2)}) collective-permute-start(bf16[512,768]{1,0:T(8,128)(2,1)} %get-tuple-element.189), channel_id=1, source_target_pairs={{1,0},{2,3},{5,4},{6,7},{9,8},{10,11},{13,12},{14,15},{17,16},{18,... | collective-permute-start | bytes 2359304 | tf_op jit(solution)/shard_map/ppermute | solution.py:449
  213.5 26.3 %collective-permute-start.36 = (bf16[32,2048]{1,0:T(8,128)(2,1)}, bf16[32,2048]{1,0:T(8,128)(2,1)S(1)}, u32[]{:S(2)}, u32[]{:S(2)}) collective-permute-start(bf16[32,2048]{1,0:T(8,128)(2,1)} %get-tuple-element.201), channel_id=1, source_target_pairs={{1,0},{2,1},{3,2},{5,4},{6,5},{7,6},{9,8},{10,9},{11,10},{13,12},{... | collective-permute-start | bytes 393224 | tf_op jit(solution)/shard_map/ppermute | solution.py:19
  214.8 24.4 %all-to-all-start = ((f32[4,1,512]{2,1,0:T(1,128)}), f32[4,1,512]{2,1,0:T(1,128)S(1)}, u32[]{:S(2)}, u32[]{:S(2)}) async-start(f32[4,1,512]{2,1,0:T(1,128)} %bitcast.32), calls=%async_computation | async-start | bytes 16384 | tf_op jit(solution)/shard_map/all_to_all | solution.py:589
  (33 other events, 396.2 us)

commit v3 on v2

--- a/solution.py
+++ b/solution.py
@@ -272,7 +272,7 @@
         dn_ref[:, at] = refs[0][:, at] + part if len(refs) > 7 else part
 
 
-def rows_kernel(dn_ref, tok_ref, mem_ref, gain_ref, cot_ref, token_ref, memory_ref, gg_ref):
+def rows_kernel(dn_ref, tok_ref, mem_ref, gain_ref, cot_ref, token0, token1, memory_ref, gg_ref):
     seg_len = tok_ref.shape[0]
     gain = gain_ref[...].astype(jnp.float32)
     step = mem_ref.shape[0]
@@ -290,10 +290,13 @@
 
     gg_ref[...] = jnp.zeros_like(gg_ref)
 
-    @pl.loop(0, seg_len // step)
-    def _(i):
-        at = pl.ds(pl.multiple_of(i * step, step), step)
-        token_ref[at, :] = piece(tok_ref[at, :], dn_ref[at, :], cot_ref[at, :])
+    for k, token_ref in enumerate((token0, token1)):
+
+        @pl.loop(0, seg_len // 2 // step)
+        def _(i, token_ref=token_ref, k=k):
+            to = pl.ds(pl.multiple_of(i * step, step), step)
+            at = pl.ds(pl.multiple_of(k * seg_len // 2 + i * step, step), step)
+            token_ref[to, :] = piece(tok_ref[at, :], dn_ref[at, :], cot_ref[at, :])
 
     memory_ref[...] = piece(mem_ref[...], dn_ref[seg_len:, :], cot_ref[seg_len:, :])
 
@@ -307,54 +310,62 @@
         out_ref[at, :] = cat_ref[:, at].T
 
 
-def grads_kernel(place_ref, nt_ref, d0, d1, d2, d3, *refs):
-    other_ref, q_ref, k_ref, v_ref, dcat_ref = refs[-5:]
+def grads_kernel(first, count, own, place_ref, nt_ref, d0, d1, d2, d3, *refs):
+    dcat_ref = refs[-1]
+    outs = refs[-4 - (count > 0) : -1] if own else refs[-2:-1]
 
     @pl.when(place_ref[5] == 1)
     def _():
         rows = d0.shape[0]
         for i, ref in enumerate((d0, d1, d2, d3)):
             dcat_ref[i * rows : (i + 1) * rows, :] = ref[...]
-        block = other_ref.shape[0]
+        block = nt_ref.shape[0] // 2
         qw = GROUP * HD
-        other = pl.ds(pl.multiple_of(place_ref[2], 128), block)
-        mine = pl.ds(pl.multiple_of(place_ref[3], 128), block)
-        other_ref[...] = jnp.dot(
-            nt_ref[other, :], dcat_ref[...], preferred_element_type=jnp.float32
-        ).astype(jnp.bfloat16)
-        total = jnp.dot(nt_ref[mine, :], dcat_ref[...], preferred_element_type=jnp.float32)
-        q_ref[...] = total[:, :qw]
-        k_ref[...] = total[:, qw : qw + HD]
-        v_ref[...] = total[:, qw + HD :]
-
-
-def place_kernel(heads, place_ref, *refs):
-    recvs = refs[: len(heads)]
+        if count:
+            other = pl.ds(pl.multiple_of(place_ref[2] + first, 128), count)
+            outs[0][...] = jnp.dot(
+                nt_ref[other, :], dcat_ref[...], preferred_element_type=jnp.float32
+            ).astype(jnp.bfloat16)
+        if own:
+            mine = pl.ds(pl.multiple_of(place_ref[3], 128), block)
+            q_ref, k_ref, v_ref = outs[-3:]
+            total = jnp.dot(nt_ref[mine, :], dcat_ref[...], preferred_element_type=jnp.float32)
+            q_ref[...] = total[:, :qw]
+            k_ref[...] = total[:, qw : qw + HD]
+            v_ref[...] = total[:, qw + HD :]
+
+
+def place_kernel(spots, place_ref, *refs):
+    recvs = refs[: len(spots)]
     q_ref, k_ref, v_ref, q_buf, k_buf, v_buf, sems = refs[-7:]
     qw = GROUP * HD
 
     @pl.when(place_ref[5] == 0)
     def _():
-        for c, recv in zip(heads, recvs):
-            q_buf[...] = recv[:, :qw].astype(jnp.float32)
-            k_buf[...] = recv[:, qw : qw + HD].astype(jnp.float32)
-            v_buf[...] = recv[:, qw + HD :].astype(jnp.float32)
-            copies = [
-                pltpu.make_async_copy(buf, ref.at[:, c * wide : (c + 1) * wide], sems.at[k])
-                for k, (buf, ref, wide) in enumerate(
-                    ((q_buf, q_ref, qw), (k_buf, k_ref, HD), (v_buf, v_ref, HD))
+        waiting = []
+        for n, ((c, first), recv) in enumerate(zip(spots, recvs)):
+            count = recv.shape[0]
+            for k, (buf, ref, at, wide) in enumerate(
+                ((q_buf, q_ref, 0, qw), (k_buf, k_ref, qw, HD), (v_buf, v_ref, qw + HD, HD))
+            ):
+                buf[n, :count, :] = recv[:, at : at + wide].astype(jnp.float32)
+                copy = pltpu.make_async_copy(
+                    buf.at[n, :count, :],
+                    ref.at[first : first + count, c * wide : (c + 1) * wide],
+                    sems.at[n, k],
                 )
-            ]
-            for copy in copies:
                 copy.start()
-            for copy in copies:
-                copy.wait()
+                waiting.append(copy)
+        for copy in waiting:
+            copy.wait()
 
 
 def copy_kernel(*refs):
-    count = len(refs) // 2
-    for src, dst in zip(refs[:count], refs[count:]):
-        dst[...] = src[...]
+    out_ref = refs[-1]
+    at = 0
+    for ref in refs[:-1]:
+        out_ref[at : at + ref.shape[0], :] = ref[...]
+        at += ref.shape[0]
 
 
 class Order:
@@ -480,29 +491,33 @@
 
     whole_shapes = tuple(shape(block, n * HEADS, f32) for n in (qw, HD, HD))
 
-    def grads(i, n_t, ds, before):
-        args = (places, n_t) + tuple(ds) + tuple(before)
+    def grads(i, n_t, ds, before, first=0, count=block, own=True):
+        before = tuple(before) if own else ()
+        args = (places, n_t) + tuple(ds) + before
+        skip = 1 if count else 0
+        outs = ((shape(count, cw),) if count else ()) + (whole_shapes if own else ())
         out = call(
-            grads_kernel,
-            (shape(block, cw),) + whole_shapes,
+            functools.partial(grads_kernel, first, count, own),
+            outs,
             args,
             specs={6 + k: anywhere for k in range(len(before))},
-            out_specs={1 + k: spec for k, spec in enumerate(own_w(i))},
+            out_specs={skip + k: spec for k, spec in enumerate(own_w(i))} if own else None,
             scratch=[pltpu.VMEM((4 * rows, cw), bf16)],
-            aliases={6 + k: 1 + k for k in range(len(before))},
+            aliases={6 + k: skip + k for k in range(len(before))},
         )
-        return out[0], out[1:]
-
-    def place(heads, recvs, before):
-        n = 1 + len(heads)
+        return (out[0] if count else None), out[skip:]
+
+    def place(spots, recvs, before):
+        n = 1 + len(spots)
+        most = max(r.shape[0] for r in recvs)
         return call(
-            functools.partial(place_kernel, heads),
+            functools.partial(place_kernel, spots),
             whole_shapes,
             (places,) + tuple(recvs) + tuple(before),
             specs={n + k: anywhere for k in range(3)},
             out_specs={k: anywhere for k in range(3)},
-            scratch=[pltpu.VMEM((block, n), f32) for n in (qw, HD, HD)]
-            + [pltpu.SemaphoreType.DMA((3,))],
+            scratch=[pltpu.VMEM((len(spots), most, w), f32) for w in (qw, HD, HD)]
+            + [pltpu.SemaphoreType.DMA((len(spots), 3))],
             aliases={n + k: k for k in range(3)},
         )
 
@@ -510,7 +525,7 @@
         return jnp.where(inner, b, c)
 
     def send(d):
-        return [permute(d, "seg", r) for r in (FAR_INWARD, ACROSS, INWARD)]
+        return [permute(d, "seg", r) for r in (INWARD, FAR_INWARD, ACROSS)]
 
     a01 = permute(h01, "seg", SWAP)
     normed, near, far = call(
@@ -540,13 +555,13 @@
     b2 = permute(to2, "seg", ACROSS)
     c1 = permute(b1, "seg", OUTWARD)
     f1 = pick(b1, c1)
-    yf0, n_far, b2, f1, to3 = order.point(yf0, n_far, b2, f1, to3)
+    n_far, b2, f1, to3 = order.point(n_far, b2, f1, to3)
     yf1 = permute(f1, "grp", GRPS)
     b3 = permute(to3, "seg", ACROSS)
     c2 = permute(b2, "seg", OUTWARD)
     d0, dn = head(0, (a01, f0, ya01, yf0), (0, 0))
     f2 = pick(b2, c2)
-    yf1, b3, f2, d0, dn = order.point(yf1, b3, f2, d0, dn)
+    b3, f2, d0, dn = order.point(b3, f2, d0, dn)
     yf2 = permute(f2, "grp", GRPS)
     c3 = permute(b3, "seg", OUTWARD)
     x0 = send(d0)
@@ -554,44 +569,50 @@
     n_t = call(
         turn_kernel,
         shape(2 * block, 4 * rows),
-        (near, n_in, n_across, n_far),
+        (near, n_in, n_far, n_across),
         scratch=[pltpu.VMEM((4 * rows, 2 * block), bf16)],
         smems=0,
     )
     f3 = pick(b3, c3)
-    yf2, f3, x00, x01, x02, d1, dn, n_t = order.point(yf2, f3, *x0, d1, dn, n_t)
+    f3, x00, x01, x02, d1, dn, n_t = order.point(f3, *x0, d1, dn, n_t)
     yf3 = permute(f3, "grp", GRPS)
     x1 = send(d1)
-    o0, whole = grads(0, n_t, (d0, x02, x01, x00), ())
+    o0, whole = grads(0, n_t, (d0, x00, x01, x02), ())
     r0 = permute(o0, "seg", OUTWARD)
     d2, dn = head(2, (a23, f2, ya23, yf2), (0, 0), (dn,))
-    yf3, x10, x11, x12, d2, dn, o0 = order.point(yf3, *x1, d2, dn, o0)
+    x10, x11, x12, d2, dn, o0 = order.point(*x1, d2, dn, o0)
     x2 = send(d2)
-    o1, whole = grads(1, n_t, (d1, x12, x11, x10), whole)
+    o1, whole = grads(1, n_t, (d1, x10, x11, x12), whole)
     r1 = permute(o1, "seg", OUTWARD)
     d3, dn = head(3, (a23, f3, ya23, yf3), (quarter, quarter), (dn,))
     x20, x21, x22, d3, r0, dn, o1 = order.point(*x2, d3, r0, dn, o1)
     x3 = send(d3)
-    o2, whole = grads(2, n_t, (d2, x22, x21, x20), whole)
+    parts2 = (d2, x20, x21, x22)
+    o2, _ = grads(2, n_t, parts2, (), own=False)
     r2 = permute(o2, "seg", OUTWARD)
-    token_part, memory_part, grad_g = call(
+    half_rows = tok.shape[0] // 2
+    token0, token1, memory_part, grad_g = call(
         rows_kernel,
-        (shape(tok.shape[0], width), shape(mem.shape[0], width), shape(1, width, f32)),
+        (shape(half_rows, width), shape(half_rows, width), shape(mem.shape[0], width), shape(1, width, f32)),
         (dn, tok, mem, gain, ocot),
         smems=0,
     )
-    x30, x31, x32, r1, r2, token_part, memory_part, grad_g = order.point(
-        *x3, r1, r2, token_part, memory_part, grad_g
-    )
-    o3, whole = grads(3, n_t, (d3, x32, x31, x30), whole)
+    gains = lax.all_to_all(grad_g.reshape(4, width // 4), "seg", 0, 0, tiled=True)
+    x30, x31, x32, r1, r2, token0, token1, memory_part, gains = order.point(
+        *x3, r1, r2, token0, token1, memory_part, gains
+    )
+    parts3 = (d3, x30, x31, x32)
+    o3, _ = grads(3, n_t, parts3, (), own=False)
     r3 = permute(o3, "seg", OUTWARD)
-    below, before = deliver(token_part, memory_part)
-    gains = lax.all_to_all(grad_g.reshape(4, width // 4), "seg", 0, 0, tiled=True)
+    below0, before = deliver(token0, memory_part)
+    below1 = from_behind(token1, "section", -1)
+    _, whole = grads(2, n_t, parts2, whole, count=0)
+    _, whole = grads(3, n_t, parts3, whole, count=0)
     grad_gain = jnp.sum(gains, 0, keepdims=True)
-    whole = place((0, 1, 2), (r0, r1, r2), whole)
-    below = call(copy_kernel, shape(tok.shape[0], width), (below,), smems=0)
-    r3, below, q_, k_, v_ = order.point(r3, below, *whole)
-    grad_query, grad_key, grad_value = place((3,), (r3,), (q_, k_, v_))
+    whole = place(((0, 0), (1, 0), (2, 0)), (r0, r1, r2), whole)
+    below = call(copy_kernel, shape(tok.shape[0], width), (below0, below1), smems=0)
+    r3, before, below, grad_gain, q_, k_, v_ = order.point(r3, before, below, grad_gain, *whole)
+    grad_query, grad_key, grad_value = place(((3, 0),), (r3,), (q_, k_, v_))
     return (
         below[None, None],
         before[None, None],

time: 245 us -> 240 us (0.980)
  waiting for transfers between devices: 90.5 us -> 75.8 us
  blocking collectives: 0 us -> 8.75 us
  starting transfers between devices: 91.6 us -> 86.8 us
    all_to_all x1 -> x0, waiting for transfers between devices: 10.9 us -> none  [on_line(): lax.all_to_all(grad_g.reshape(4, width // 4), 'seg', 0, 0, tiled=True)]
    all_to_all x1 -> x0, starting transfers between devices: 9.3 us -> none  [on_line(): lax.all_to_all(grad_g.reshape(4, width // 4), 'seg', 0, 0, tiled=True)]
    all_to_all x0 -> x1, blocking collectives: none -> 8.75 us  [on_line(): lax.all_to_all(grad_g.reshape(4, width // 4), 'seg', 0, 0, tiled=True)]
    ppermute x2 -> x3, starting transfers between devices: 9.44 us -> 15.9 us  [from_behind(): return lax.ppermute(block, axis, route)]
    ppermute x35, waiting for transfers between devices: 79.5 us -> 75.8 us  [permute(): return lax.ppermute(value, axis, route)]
    unnamed x39 -> x74, local copies, waits for them, and re-layouts: 3.28 us -> 5.17 us
    pallas_call x15 -> x17, Pallas kernels: 53.8 us -> 55.3 us  [call(): pl.pallas_call(kernel, grid=(1,), out_shape=outs, in_specs=ins, out_specs...]
  transfers between devices with their start and end apart: 38 -> 38, of which waited for: 10 -> 9; matrix products, arithmetic and copies ran while one was open for 1% -> 1% of each run, Pallas kernels for 20% -> 21%
where the time goes in v3:
time: 240 us; the launch traced here: 237 us
  starting transfers between devices  86.8 us (36%)
  waiting for transfers between devices  75.8 us (32%)
  Pallas kernels  55.3 us (23%)
  blocking collectives  8.75 us (4%)
  local copies, waits for them, and re-layouts  5.54 us (2%)
  other arithmetic  3.25 us (1%)
    ppermute x35, waiting for transfers between devices, permute(): return lax.ppermute(value, axis, route)  75.8 us
    ppermute x35, starting transfers between devices, permute(): return lax.ppermute(value, axis, route)  71 us
    pallas_call x17, Pallas kernels, call(): pl.pallas_call(kernel, grid=(1,), out_shape=outs, in_specs=ins, out_specs...  55.3 us
    ppermute x3, starting transfers between devices, from_behind(): return lax.ppermute(block, axis, route)  15.9 us
    all_to_all x1, blocking collectives, on_line(): lax.all_to_all(grad_g.reshape(4, width // 4), 'seg', 0, 0, tiled=True)  8.75 us
    unnamed x74, local copies, waits for them, and re-layouts  5.17 us
  transfers between devices with their start and end apart: 38, of which 9 were waited for; matrix products, arithmetic and copies ran while one was open for 1% of the time, Pallas kernels for 21%

profile of v3, /device:TPU:7, one launch (start us, length us, event | category | flops | bytes accessed | tf_op | source)
XLA Modules:
  0.0 236.9 jit_solution(12636821214164150826)
XLA Ops:
  6.7 14.5 %collective-permute-done.a = bf16[512,768]{1,0:T(8,128)(2,1)S(1)} collective-permute-done((bf16[512,768]{1,0:T(8,128)(2,1)S(1)}, bf16[512,768]{1,0:T(8,128)(2,1)S(1)}, u32[]{:S(2)}, u32[]{:S(2)}) %collective-permute-start) | collective-permute-done | bytes 786464 | tf_op jit(solution)/shard_map/ppermute | solution.py:460
  22.1 5.1 %collective-permute-start.4 = (bf16[512,768]{1,0:T(8,128)(2,1)S(1)}, bf16[512,768]{1,0:T(8,128)(2,1)S(1)}, u32[]{:S(2)}, u32[]{:S(2)}) collective-permute-start(bf16[512,768]{1,0:T(8,128)(2,1)S(1)} %get-tuple-element.120), channel_id=1, source_target_pairs={{0,1},{1,0},{2,3},{3,2},{4,5},{5,4},{6,7},{7,6},{8,9},{9,8},{10,11... | collective-permute-start | bytes 2359304 | tf_op jit(solution)/shard_map/ppermute | solution.py:460
  27.5 15.4 %collective-permute-done.4.a = bf16[512,768]{1,0:T(8,128)(2,1)S(1)} collective-permute-done((bf16[512,768]{1,0:T(8,128)(2,1)S(1)}, bf16[512,768]{1,0:T(8,128)(2,1)S(1)}, u32[]{:S(2)}, u32[]{:S(2)}) %collective-permute-start.4) | collective-permute-done | bytes 786464 | tf_op jit(solution)/shard_map/ppermute | solution.py:460
  45.1 4.1 %collective-permute-start.6 = (bf16[288,1024]{1,0:T(8,128)(2,1)S(1)}, bf16[288,1024]{1,0:T(8,128)(2,1)S(1)}, u32[]{:S(2)}, u32[]{:S(2)}) collective-permute-start(bf16[288,1024]{1,0:T(8,128)(2,1)S(1)} %get-tuple-element.117.n0), channel_id=1, source_target_pairs={{0,1},{3,2},{4,5},{7,6},{8,9},{11,10},{12,13},{15,14},{16,17},{19,... | collective-permute-start | bytes 1769480 | tf_op jit(solution)/shard_map/ppermute | solution.py:460
  51.3 10.1 %collective-permute-done.8 = bf16[512,768]{1,0:T(8,128)(2,1)S(1)} collective-permute-done((bf16[512,768]{1,0:T(8,128)(2,1)S(1)}, bf16[512,768]{1,0:T(8,128)(2,1)S(1)}, u32[]{:S(2)}, u32[]{:S(2)}) %collective-permute-start.8) | collective-permute-done | bytes 786464 | tf_op jit(solution)/shard_map/ppermute | solution.py:460
  62.4 2.8 %collective-permute-done.5.ya = bf16[512,768]{1,0:T(8,128)(2,1)S(1)} collective-permute-done((bf16[512,768]{1,0:T(8,128)(2,1)S(1)}, bf16[512,768]{1,0:T(8,128)(2,1)S(1)}, u32[]{:S(2)}, u32[]{:S(2)}) %collective-permute-start.5) | collective-permute-done | bytes 786464 | tf_op jit(solution)/shard_map/ppermute | solution.py:460
  68.0 5.6 %collective-permute-start.9 = (bf16[288,1024]{1,0:T(8,128)(2,1)S(1)}, bf16[288,1024]{1,0:T(8,128)(2,1)S(1)}, u32[]{:S(2)}, u32[]{:S(2)}) collective-permute-start(bf16[288,1024]{1,0:T(8,128)(2,1)S(1)} %get-tuple-element.122), channel_id=1, source_target_pairs={{0,2},{3,1},{4,6},{7,5},{8,10},{11,9},{12,14},{15,13},{16,18},{19,... | collective-permute-start | bytes 1769480 | tf_op jit(solution)/shard_map/ppermute | solution.py:460
  73.9 7.3 %collective-permute-done.11 = bf16[512,768]{1,0:T(8,128)(2,1)S(1)} collective-permute-done((bf16[512,768]{1,0:T(8,128)(2,1)S(1)}, bf16[512,768]{1,0:T(8,128)(2,1)S(1)}, u32[]{:S(2)}, u32[]{:S(2)}) %collective-permute-start.11) | collective-permute-done | bytes 786464 | tf_op jit(solution)/shard_map/ppermute | solution.py:460
  84.5 2.6 %collective-permute-done.14.yfar = bf16[512,768]{1,0:T(8,128)(2,1)} collective-permute-done((bf16[512,768]{1,0:T(8,128)(2,1)S(1)}, bf16[512,768]{1,0:T(8,128)(2,1)}, u32[]{:S(2)}, u32[]{:S(2)}) %collective-permute-start.14) | collective-permute-done | bytes 786464 | tf_op jit(solution)/shard_map/ppermute | solution.py:460
  87.1 7.7 %shard_map.129 = (bf16[288,768]{1,0:T(8,128)(2,1)S(1)}, f32[288,2048]{1,0:T(8,128)S(1)}) custom-call(s32[7]{0:T(128)S(1)} %stack.63.off_ref, bf16[288,2048]{1,0:T(8,128)(2,1)} %copy-done, bf16[512,2048]{1,0:T(8,128)(2,1)} %bitcast.38, bf16[512,512]{1,0:T(8,128)(2,1)} %bitcast.49, bf16[512,512]{1,0:T(8,128)(2,1)} %bitcast.54, bf16[512,768]{1,0:T(8,128)(2,1)} %copy-done.29, ...), custom_call_target="tpu_custom_call" | custom-call | tf_op jit(solution)/shard_map/pallas_call | solution.py:447
  94.9 19.0 %collective-permute-done.13 = bf16[512,768]{1,0:T(8,128)(2,1)} collective-permute-done((bf16[512,768]{1,0:T(8,128)(2,1)}, bf16[512,768]{1,0:T(8,128)(2,1)}, u32[]{:S(2)}, u32[]{:S(2)}) %collective-permute-start.13) | collective-permute-done | bytes 786464 | tf_op jit(solution)/shard_map/ppermute | solution.py:460
  117.6 7.5 %collective-permute-start.17 = (bf16[288,768]{1,0:T(8,128)(2,1)S(1)}, bf16[288,768]{1,0:T(8,128)(2,1)S(1)}, u32[]{:S(2)}, u32[]{:S(2)}) collective-permute-start(bf16[288,768]{1,0:T(8,128)(2,1)S(1)} %get-tuple-element.134.d0), channel_id=1, source_target_pairs={{0,2},{3,1},{4,6},{7,5},{8,10},{11,9},{12,14},{15,13},{16,18},{19,... | collective-permute-start | bytes 1327112 | tf_op jit(solution)/shard_map/ppermute | solution.py:460
  127.6 7.9 %shard_map.130 = (bf16[288,768]{1,0:T(8,128)(2,1)S(1)}, f32[288,2048]{1,0:T(8,128)S(1)}) custom-call(s32[7]{0:T(128)S(1)} %stack.63.off_ref, bf16[288,2048]{1,0:T(8,128)(2,1)} %copy-done, bf16[512,2048]{1,0:T(8,128)(2,1)} %bitcast.39, bf16[512,512]{1,0:T(8,128)(2,1)} %bitcast.50, bf16[512,512]{1,0:T(8,128)(2,1)} %bitcast.55, ...), custom_call_target="tpu_custom_call", output_to_operand_aliasing={{1}: (10, {})} | custom-call | tf_op jit(solution)/shard_map/pallas_call | solution.py:447
  135.6 3.1 %collective-permute-done.16.d1 = bf16[288,768]{1,0:T(8,128)(2,1)S(1)} collective-permute-done((bf16[288,768]{1,0:T(8,128)(2,1)S(1)}, bf16[288,768]{1,0:T(8,128)(2,1)S(1)}, u32[]{:S(2)}, u32[]{:S(2)}) %collective-permute-start.16) | collective-permute-done | bytes 442400 | tf_op jit(solution)/shard_map/ppermute | solution.py:460
  139.4 6.6 %collective-permute-start.21 = (bf16[288,768]{1,0:T(8,128)(2,1)S(1)}, bf16[288,768]{1,0:T(8,128)(2,1)S(1)}, u32[]{:S(2)}, u32[]{:S(2)}) collective-permute-start(bf16[288,768]{1,0:T(8,128)(2,1)S(1)} %get-tuple-element.143.d0), channel_id=1, source_target_pairs={{0,2},{3,1},{4,6},{7,5},{8,10},{11,9},{12,14},{15,13},{16,18},{19,... | collective-permute-start | bytes 1327112 | tf_op jit(solution)/shard_map/ppermute | solution.py:460
  151.8 7.9 %shard_map.132 = (bf16[288,768]{1,0:T(8,128)(2,1)S(1)}, f32[288,2048]{1,0:T(8,128)S(1)}) custom-call(s32[7]{0:T(128)S(1)} %stack.63.off_ref, bf16[288,2048]{1,0:T(8,128)(2,1)} %copy-done, bf16[512,2048]{1,0:T(8,128)(2,1)} %bitcast.40, bf16[512,512]{1,0:T(8,128)(2,1)} %bitcast.51, bf16[512,512]{1,0:T(8,128)(2,1)} %bitcast.56, ...), custom_call_target="tpu_custom_call", output_to_operand_aliasing={{1}: (10, {})} | custom-call | tf_op jit(solution)/shard_map/pallas_call | solution.py:447
  160.4 6.5 %collective-permute-start.25 = (bf16[288,768]{1,0:T(8,128)(2,1)S(1)}, bf16[288,768]{1,0:T(8,128)(2,1)S(1)}, u32[]{:S(2)}, u32[]{:S(2)}) collective-permute-start(bf16[288,768]{1,0:T(8,128)(2,1)S(1)} %get-tuple-element.153.d0), channel_id=1, source_target_pairs={{0,2},{3,1},{4,6},{7,5},{8,10},{11,9},{12,14},{15,13},{16,18},{19,... | collective-permute-start | bytes 1327112 | tf_op jit(solution)/shard_map/ppermute | solution.py:460
  171.4 7.8 %shard_map.134 = (bf16[288,768]{1,0:T(8,128)(2,1)S(1)}, f32[288,2048]{1,0:T(8,128)S(1)}) custom-call(s32[7]{0:T(128)S(1)} %stack.63.off_ref, bf16[288,2048]{1,0:T(8,128)(2,1)} %copy-done, bf16[512,2048]{1,0:T(8,128)(2,1)} %bitcast.41, bf16[512,512]{1,0:T(8,128)(2,1)} %bitcast.52, bf16[512,512]{1,0:T(8,128)(2,1)} %bitcast.57, ...), custom_call_target="tpu_custom_call", output_to_operand_aliasing={{1}: (10, {})} | custom-call | tf_op jit(solution)/shard_map/pallas_call | solution.py:447
  182.2 7.4 %collective-permute-start.30 = (bf16[288,768]{1,0:T(8,128)(2,1)S(1)}, bf16[288,768]{1,0:T(8,128)(2,1)S(1)}, u32[]{:S(2)}, u32[]{:S(2)}) collective-permute-start(bf16[288,768]{1,0:T(8,128)(2,1)S(1)} %get-tuple-element.165.d0), channel_id=1, source_target_pairs={{0,2},{3,1},{4,6},{7,5},{8,10},{11,9},{12,14},{15,13},{16,18},{19,... | collective-permute-start | bytes 1327112 | tf_op jit(solution)/shard_map/ppermute | solution.py:460
  191.0 3.1 %shard_map.137 = (bf16[128,2048]{1,0:T(8,128)(2,1)}, bf16[128,2048]{1,0:T(8,128)(2,1)}, bf16[32,2048]{1,0:T(8,128)(2,1)}, f32[1,2048]{1,0:T(1,128)S(1)}) custom-call(f32[288,2048]{1,0:T(8,128)S(1)} %get-tuple-element.169.dn_ref, bf16[256,2048]{1,0:T(8,128)(2,1)S(1)} %bitcast.31, bf16[32,2048]{1,0:T(8,128)(2,1)S(1)} %bitcast.34, ...), custom_call_target="tpu_custom_call" | custom-call | tf_op jit(solution)/shard_map/pallas_call | solution.py:447
  194.1 8.7 %all_to_all.12 = f32[4,1,512]{2,1,0:T(1,128)S(1)} all-to-all(f32[4,1,512]{2,1,0:T(1,128)S(1)} %bitcast.35), channel_id=1, replica_groups=mesh['grp'=2,'section'=4,'seg'=4] {'seg'}, dimensions={0} | all-to-all | bytes 16384 | tf_op jit(solution)/shard_map/all_to_all | solution.py:600
  206.6 12.5 %collective-permute-start.36 = (bf16[128,2048]{1,0:T(8,128)(2,1)}, bf16[128,2048]{1,0:T(8,128)(2,1)}, u32[]{:S(2)}, u32[]{:S(2)}) collective-permute-start(bf16[128,2048]{1,0:T(8,128)(2,1)} %get-tuple-element.178), channel_id=1, source_target_pairs={{4,0},{8,4},{12,8},{5,1},{9,5},{13,9},{6,2},{10,6},{14,10},{7,3},{... | collective-permute-start | bytes 1572872 | tf_op jit(solution)/shard_map/ppermute | solution.py:19
  228.8 2.8 %shard_map.142 = (f32[512,2048]{1,0:T(8,128)}, f32[512,512]{1,0:T(8,128)}, f32[512,512]{1,0:T(8,128)}) custom-call(s32[6]{0:T(128)S(1)} %stack.55.place_ref, bf16[512,768]{1,0:T(8,128)(2,1)S(1)} %copy-done.14, bf16[512,768]{1,0:T(8,128)(2,1)S(1)} %copy-done.16, ...), custom_call_target="tpu_custom_call", output_to_operand_aliasing={{0}: (4, {}), {1}: (5, {}), {2}: (6, {})} | custom-call | tf_op jit(solution)/shard_map/pallas_call | solution.py:447
  233.9 2.4 %shard_map.143 = (f32[512,2048]{1,0:T(8,128)}, f32[512,512]{1,0:T(8,128)}, f32[512,512]{1,0:T(8,128)}) custom-call(s32[6]{0:T(128)S(1)} %stack.55.place_ref, bf16[512,768]{1,0:T(8,128)(2,1)} %collective-permute-done.34.refs_0_, f32[512,2048]{1,0:T(8,128)} %get-tuple-element.199.refs_1_, ...), custom_call_target="tpu_custom_call", output_to_operand_aliasing={{0}: (2, {}), {1}: (3, {}), {2}: (4, {})} | custom-call | tf_op jit(solution)/shard_map/pallas_call | solution.py:447
  (158 shorter events, 57.2 us)
Async XLA Ops:
  2.8 18.5 %collective-permute-start = (bf16[512,768]{1,0:T(8,128)(2,1)S(1)}, bf16[512,768]{1,0:T(8,128)(2,1)S(1)}, u32[]{:S(2)}, u32[]{:S(2)}) collective-permute-start(bf16[512,768]{1,0:T(8,128)(2,1)S(1)} %get-tuple-element.112), channel_id=1, source_target_pairs={{0,1},{1,0},{2,3},{3,2},{4,5},{5,4},{6,7},{7,6},{8,9},{9,8},{10,11... | collective-permute-start | bytes 2359304 | tf_op jit(solution)/shard_map/ppermute | solution.py:460
  22.1 20.8 %collective-permute-start.4 = (bf16[512,768]{1,0:T(8,128)(2,1)S(1)}, bf16[512,768]{1,0:T(8,128)(2,1)S(1)}, u32[]{:S(2)}, u32[]{:S(2)}) collective-permute-start(bf16[512,768]{1,0:T(8,128)(2,1)S(1)} %get-tuple-element.120), channel_id=1, source_target_pairs={{0,1},{1,0},{2,3},{3,2},{4,5},{5,4},{6,7},{7,6},{8,9},{9,8},{10,11... | collective-permute-start | bytes 2359304 | tf_op jit(solution)/shard_map/ppermute | solution.py:460
  27.2 16.6 %collective-permute-start.3 = (bf16[512,768]{1,0:T(8,128)(2,1)S(1)}, bf16[512,768]{1,0:T(8,128)(2,1)S(1)}, u32[]{:S(2)}, u32[]{:S(2)}) collective-permute-start(bf16[512,768]{1,0:T(8,128)(2,1)S(1)} %collective-permute-done.a), channel_id=1, source_target_pairs={{0,16},{16,0},{1,17},{17,1},{2,18},{18,2},{3,19},{19,3},{4,20},{20... | collective-permute-start | bytes 2359304 | tf_op jit(solution)/shard_map/ppermute | solution.py:460
  43.8 17.6 %collective-permute-start.8 = (bf16[512,768]{1,0:T(8,128)(2,1)S(1)}, bf16[512,768]{1,0:T(8,128)(2,1)S(1)}, u32[]{:S(2)}, u32[]{:S(2)}) collective-permute-start(bf16[512,768]{1,0:T(8,128)(2,1)S(1)} %collective-permute-done.2), channel_id=1, source_target_pairs={{1,0},{2,3},{5,4},{6,7},{9,8},{10,11},{13,12},{14,15},{17,16},{18,... | collective-permute-start | bytes 2359304 | tf_op jit(solution)/shard_map/ppermute | solution.py:460
  45.1 16.4 %collective-permute-start.6 = (bf16[288,1024]{1,0:T(8,128)(2,1)S(1)}, bf16[288,1024]{1,0:T(8,128)(2,1)S(1)}, u32[]{:S(2)}, u32[]{:S(2)}) collective-permute-start(bf16[288,1024]{1,0:T(8,128)(2,1)S(1)} %get-tuple-element.117.n0), channel_id=1, source_target_pairs={{0,1},{3,2},{4,5},{7,6},{8,9},{11,10},{12,13},{15,14},{16,17},{19,... | collective-permute-start | bytes 1769480 | tf_op jit(solution)/shard_map/ppermute | solution.py:460
  81.4 32.5 %collective-permute-start.13 = (bf16[512,768]{1,0:T(8,128)(2,1)}, bf16[512,768]{1,0:T(8,128)(2,1)}, u32[]{:S(2)}, u32[]{:S(2)}) collective-permute-start(bf16[512,768]{1,0:T(8,128)(2,1)} %collective-permute-done.10), channel_id=1, source_target_pairs={{1,0},{2,3},{5,4},{6,7},{9,8},{10,11},{13,12},{14,15},{17,16},{18,... | collective-permute-start | bytes 2359304 | tf_op jit(solution)/shard_map/ppermute | solution.py:460
  82.7 32.5 %collective-permute-start.12 = (bf16[512,768]{1,0:T(8,128)(2,1)}, bf16[512,768]{1,0:T(8,128)(2,1)}, u32[]{:S(2)}, u32[]{:S(2)}) collective-permute-start(bf16[512,768]{1,0:T(8,128)(2,1)} %pad_maximum_fusion.3), channel_id=1, source_target_pairs={{1,2},{2,1},{5,6},{6,5},{9,10},{10,9},{13,14},{14,13},{17,18},{18,... | collective-permute-start | bytes 2359304 | tf_op jit(solution)/shard_map/ppermute | solution.py:460
  84.3 40.8 %collective-permute-start.19 = (bf16[512,768]{1,0:T(8,128)(2,1)S(1)}, bf16[512,768]{1,0:T(8,128)(2,1)S(1)}, u32[]{:S(2)}, u32[]{:S(2)}) collective-permute-start(bf16[512,768]{1,0:T(8,128)(2,1)S(1)} %broadcast_select_fusion.2.far), channel_id=1, source_target_pairs={{0,16},{16,0},{1,17},{17,1},{2,18},{18,2},{3,19},{19,3},{4,20},{20... | collective-permute-start | bytes 2359304 | tf_op jit(solution)/shard_map/ppermute | solution.py:460
  115.2 20.3 %collective-permute-start.15 = (bf16[512,768]{1,0:T(8,128)(2,1)}, bf16[512,768]{1,0:T(8,128)(2,1)S(1)}, u32[]{:S(2)}, u32[]{:S(2)}) collective-permute-start(bf16[512,768]{1,0:T(8,128)(2,1)} %collective-permute-done.12), channel_id=1, source_target_pairs={{1,0},{2,3},{5,4},{6,7},{9,8},{10,11},{13,12},{14,15},{17,16},{18,... | collective-permute-start | bytes 2359304 | tf_op jit(solution)/shard_map/ppermute | solution.py:460
  116.6 33.9 %collective-permute-start.23 = (bf16[512,768]{1,0:T(8,128)(2,1)S(1)}, bf16[512,768]{1,0:T(8,128)(2,1)S(1)}, u32[]{:S(2)}, u32[]{:S(2)}) collective-permute-start(bf16[512,768]{1,0:T(8,128)(2,1)S(1)} %broadcast_select_fusion.1.far), channel_id=1, source_target_pairs={{0,16},{16,0},{1,17},{17,1},{2,18},{18,2},{3,19},{19,3},{4,20},{20... | collective-permute-start | bytes 2359304 | tf_op jit(solution)/shard_map/ppermute | solution.py:460
  116.9 18.7 %collective-permute-start.18 = (bf16[288,768]{1,0:T(8,128)(2,1)S(1)}, bf16[288,768]{1,0:T(8,128)(2,1)S(1)}, u32[]{:S(2)}, u32[]{:S(2)}) collective-permute-start(bf16[288,768]{1,0:T(8,128)(2,1)S(1)} %get-tuple-element.134.d0), channel_id=1, source_target_pairs={{1,2},{2,1},{5,6},{6,5},{9,10},{10,9},{13,14},{14,13},{17,18},{18,... | collective-permute-start | bytes 1327112 | tf_op jit(solution)/shard_map/ppermute | solution.py:460
  117.6 18.0 %collective-permute-start.17 = (bf16[288,768]{1,0:T(8,128)(2,1)S(1)}, bf16[288,768]{1,0:T(8,128)(2,1)S(1)}, u32[]{:S(2)}, u32[]{:S(2)}) collective-permute-start(bf16[288,768]{1,0:T(8,128)(2,1)S(1)} %get-tuple-element.134.d0), channel_id=1, source_target_pairs={{0,2},{3,1},{4,6},{7,5},{8,10},{11,9},{12,14},{15,13},{16,18},{19,... | collective-permute-start | bytes 1327112 | tf_op jit(solution)/shard_map/ppermute | solution.py:460
  138.7 21.0 %collective-permute-start.22 = (bf16[288,768]{1,0:T(8,128)(2,1)S(1)}, bf16[288,768]{1,0:T(8,128)(2,1)S(1)}, u32[]{:S(2)}, u32[]{:S(2)}) collective-permute-start(bf16[288,768]{1,0:T(8,128)(2,1)S(1)} %get-tuple-element.143.d0), channel_id=1, source_target_pairs={{1,2},{2,1},{5,6},{6,5},{9,10},{10,9},{13,14},{14,13},{17,18},{18,... | collective-permute-start | bytes 1327112 | tf_op jit(solution)/shard_map/ppermute | solution.py:460
  139.4 20.3 %collective-permute-start.21 = (bf16[288,768]{1,0:T(8,128)(2,1)S(1)}, bf16[288,768]{1,0:T(8,128)(2,1)S(1)}, u32[]{:S(2)}, u32[]{:S(2)}) collective-permute-start(bf16[288,768]{1,0:T(8,128)(2,1)S(1)} %get-tuple-element.143.d0), channel_id=1, source_target_pairs={{0,2},{3,1},{4,6},{7,5},{8,10},{11,9},{12,14},{15,13},{16,18},{19,... | collective-permute-start | bytes 1327112 | tf_op jit(solution)/shard_map/ppermute | solution.py:460
  147.5 22.6 %collective-permute-start.27 = (bf16[512,768]{1,0:T(8,128)(2,1)S(1)}, bf16[512,768]{1,0:T(8,128)(2,1)S(1)}, u32[]{:S(2)}, u32[]{:S(2)}) collective-permute-start(bf16[512,768]{1,0:T(8,128)(2,1)S(1)} %broadcast_select_fusion.far), channel_id=1, source_target_pairs={{0,16},{16,0},{1,17},{17,1},{2,18},{18,2},{3,19},{19,3},{4,20},{20... | collective-permute-start | bytes 2359304 | tf_op jit(solution)/shard_map/ppermute | solution.py:460
  150.5 28.8 %collective-permute-start.28 = (bf16[512,768]{1,0:T(8,128)(2,1)S(1)}, bf16[512,768]{1,0:T(8,128)(2,1)S(1)}, u32[]{:S(2)}, u32[]{:S(2)}) collective-permute-start(bf16[512,768]{1,0:T(8,128)(2,1)S(1)} %get-tuple-element.152), channel_id=1, source_target_pairs={{1,0},{2,3},{5,4},{6,7},{9,8},{10,11},{13,12},{14,15},{17,16},{18,... | collective-permute-start | bytes 2359304 | tf_op jit(solution)/shard_map/ppermute | solution.py:460
  159.7 19.6 %collective-permute-start.26 = (bf16[288,768]{1,0:T(8,128)(2,1)S(1)}, bf16[288,768]{1,0:T(8,128)(2,1)S(1)}, u32[]{:S(2)}, u32[]{:S(2)}) collective-permute-start(bf16[288,768]{1,0:T(8,128)(2,1)S(1)} %get-tuple-element.153.d0), channel_id=1, source_target_pairs={{1,2},{2,1},{5,6},{6,5},{9,10},{10,9},{13,14},{14,13},{17,18},{18,... | collective-permute-start | bytes 1327112 | tf_op jit(solution)/shard_map/ppermute | solution.py:460
  160.4 18.9 %collective-permute-start.25 = (bf16[288,768]{1,0:T(8,128)(2,1)S(1)}, bf16[288,768]{1,0:T(8,128)(2,1)S(1)}, u32[]{:S(2)}, u32[]{:S(2)}) collective-permute-start(bf16[288,768]{1,0:T(8,128)(2,1)S(1)} %get-tuple-element.153.d0), channel_id=1, source_target_pairs={{0,2},{3,1},{4,6},{7,5},{8,10},{11,9},{12,14},{15,13},{16,18},{19,... | collective-permute-start | bytes 1327112 | tf_op jit(solution)/shard_map/ppermute | solution.py:460
  170.1 32.7 %collective-permute-start.32 = (bf16[512,768]{1,0:T(8,128)(2,1)S(1)}, bf16[512,768]{1,0:T(8,128)(2,1)S(1)}, u32[]{:S(2)}, u32[]{:S(2)}) collective-permute-start(bf16[512,768]{1,0:T(8,128)(2,1)S(1)} %get-tuple-element.164), channel_id=1, source_target_pairs={{1,0},{2,3},{5,4},{6,7},{9,8},{10,11},{13,12},{14,15},{17,16},{18,... | collective-permute-start | bytes 2359304 | tf_op jit(solution)/shard_map/ppermute | solution.py:460
  180.2 22.6 %collective-permute-start.33 = (bf16[512,768]{1,0:T(8,128)(2,1)S(1)}, bf16[512,768]{1,0:T(8,128)(2,1)S(1)}, u32[]{:S(2)}, u32[]{:S(2)}) collective-permute-start(bf16[512,768]{1,0:T(8,128)(2,1)S(1)} %shard_map.136), channel_id=1, source_target_pairs={{1,0},{2,3},{5,4},{6,7},{9,8},{10,11},{13,12},{14,15},{17,16},{18,... | collective-permute-start | bytes 2359304 | tf_op jit(solution)/shard_map/ppermute | solution.py:460
  181.5 21.3 %collective-permute-start.31 = (bf16[288,768]{1,0:T(8,128)(2,1)S(1)}, bf16[288,768]{1,0:T(8,128)(2,1)S(1)}, u32[]{:S(2)}, u32[]{:S(2)}) collective-permute-start(bf16[288,768]{1,0:T(8,128)(2,1)S(1)} %get-tuple-element.165.d0), channel_id=1, source_target_pairs={{1,2},{2,1},{5,6},{6,5},{9,10},{10,9},{13,14},{14,13},{17,18},{18,... | collective-permute-start | bytes 1327112 | tf_op jit(solution)/shard_map/ppermute | solution.py:460
  182.2 20.6 %collective-permute-start.30 = (bf16[288,768]{1,0:T(8,128)(2,1)S(1)}, bf16[288,768]{1,0:T(8,128)(2,1)S(1)}, u32[]{:S(2)}, u32[]{:S(2)}) collective-permute-start(bf16[288,768]{1,0:T(8,128)(2,1)S(1)} %get-tuple-element.165.d0), channel_id=1, source_target_pairs={{0,2},{3,1},{4,6},{7,5},{8,10},{11,9},{12,14},{15,13},{16,18},{19,... | collective-permute-start | bytes 1327112 | tf_op jit(solution)/shard_map/ppermute | solution.py:460
  205.3 28.6 %collective-permute-start.34 = (bf16[512,768]{1,0:T(8,128)(2,1)}, bf16[512,768]{1,0:T(8,128)(2,1)}, u32[]{:S(2)}, u32[]{:S(2)}) collective-permute-start(bf16[512,768]{1,0:T(8,128)(2,1)} %shard_map.138), channel_id=1, source_target_pairs={{1,0},{2,3},{5,4},{6,7},{9,8},{10,11},{13,12},{14,15},{17,16},{18,... | collective-permute-start | bytes 2359304 | tf_op jit(solution)/shard_map/ppermute | solution.py:460
  206.6 25.0 %collective-permute-start.36 = (bf16[128,2048]{1,0:T(8,128)(2,1)}, bf16[128,2048]{1,0:T(8,128)(2,1)}, u32[]{:S(2)}, u32[]{:S(2)}) collective-permute-start(bf16[128,2048]{1,0:T(8,128)(2,1)} %get-tuple-element.178), channel_id=1, source_target_pairs={{4,0},{8,4},{12,8},{5,1},{9,5},{13,9},{6,2},{10,6},{14,10},{7,3},{... | collective-permute-start | bytes 1572872 | tf_op jit(solution)/shard_map/ppermute | solution.py:19
  (50 other events, 501.1 us)

commit v4 on v3

--- a/solution.py
+++ b/solution.py
@@ -301,10 +301,16 @@
     memory_ref[...] = piece(mem_ref[...], dn_ref[seg_len:, :], cot_ref[seg_len:, :])
 
 
-def turn_kernel(n0, n1, n2, n3, out_ref, cat_ref):
+def turn_kernel(n0, n1, n2, n3, out_ref, cat_ref, sems):
     rows = n0.shape[0]
-    for i, ref in enumerate((n0, n1, n2, n3)):
-        cat_ref[i * rows : (i + 1) * rows, :] = ref[...]
+    copies = fetch(
+        [
+            (ref, cat_ref.at[i * rows : (i + 1) * rows, :], sems.at[i])
+            for i, ref in enumerate((n0, n1, n2, n3))
+        ]
+    )
+    for copy in copies:
+        copy.wait()
     for i in range(out_ref.shape[0] // 256):
         at = slice(256 * i, 256 * (i + 1))
         out_ref[at, :] = cat_ref[:, at].T
@@ -337,14 +343,20 @@
 
 def place_kernel(spots, place_ref, *refs):
     recvs = refs[: len(spots)]
-    q_ref, k_ref, v_ref, q_buf, k_buf, v_buf, sems = refs[-7:]
+    q_ref, k_ref, v_ref, q_buf, k_buf, v_buf, sems = refs[len(spots) + 3 : len(spots) + 10]
+    held = refs[len(spots) + 10 :]
     qw = GROUP * HD
 
     @pl.when(place_ref[5] == 0)
     def _():
         waiting = []
+        if held:
+            coming = fetch([(recv, held[0].at[n], held[1].at[n]) for n, recv in enumerate(recvs)])
         for n, ((c, first), recv) in enumerate(zip(spots, recvs)):
             count = recv.shape[0]
+            if held:
+                coming[n].wait()
+                recv = held[0].at[n]
             for k, (buf, ref, at, wide) in enumerate(
                 ((q_buf, q_ref, 0, qw), (k_buf, k_ref, qw, HD), (v_buf, v_ref, qw + HD, HD))
             ):
@@ -507,17 +519,26 @@
         )
         return (out[0] if count else None), out[skip:]
 
-    def place(spots, recvs, before):
+    def place(spots, recvs, before, from_hbm=False):
         n = 1 + len(spots)
         most = max(r.shape[0] for r in recvs)
         return call(
             functools.partial(place_kernel, spots),
             whole_shapes,
             (places,) + tuple(recvs) + tuple(before),
-            specs={n + k: anywhere for k in range(3)},
+            specs={n + k: anywhere for k in range(3)}
+            | ({1 + k: hbm for k in range(len(spots))} if from_hbm else {}),
             out_specs={k: anywhere for k in range(3)},
             scratch=[pltpu.VMEM((len(spots), most, w), f32) for w in (qw, HD, HD)]
-            + [pltpu.SemaphoreType.DMA((len(spots), 3))],
+            + [pltpu.SemaphoreType.DMA((len(spots), 3))]
+            + (
+                [
+                    pltpu.VMEM((len(spots), most, cw), bf16),
+                    pltpu.SemaphoreType.DMA((len(spots),)),
+                ]
+                if from_hbm
+                else []
+            ),
             aliases={n + k: k for k in range(3)},
         )
 
@@ -542,26 +563,26 @@
     ya01 = permute(a01, "grp", GRPS)
     to1 = z_and([a01[quarter:], h01[quarter:]])
     b0, ya01, a23, to1, h23, near, far = order.point(b0, ya01, a23, to1, h23, near, far)
-    ya23 = permute(a23, "grp", GRPS)
-    n_in = permute(near, "seg", INWARD)
     b1 = permute(to1, "seg", ACROSS)
     c0 = permute(b0, "seg", OUTWARD)
     to2 = z_and([a23[:quarter], h23[:quarter]])
     to3 = z_and([a23[quarter:], h23[quarter:]])
     f0 = pick(b0, c0)
-    ya23, n_in, b1, f0, to2, to3, far = order.point(ya23, n_in, b1, f0, to2, to3, far)
+    b1, f0, to2, to3, a23, near, far = order.point(b1, f0, to2, to3, a23, near, far)
     yf0 = permute(f0, "grp", GRPS)
+    ya23 = permute(a23, "grp", GRPS)
     n_far = permute(far, "seg", FAR_INWARD)
     b2 = permute(to2, "seg", ACROSS)
     c1 = permute(b1, "seg", OUTWARD)
     f1 = pick(b1, c1)
-    n_far, b2, f1, to3 = order.point(n_far, b2, f1, to3)
+    n_far, b2, f1, to3, ya23, near = order.point(n_far, b2, f1, to3, ya23, near)
     yf1 = permute(f1, "grp", GRPS)
+    n_in = permute(near, "seg", INWARD)
     b3 = permute(to3, "seg", ACROSS)
     c2 = permute(b2, "seg", OUTWARD)
     d0, dn = head(0, (a01, f0, ya01, yf0), (0, 0))
     f2 = pick(b2, c2)
-    b3, f2, d0, dn = order.point(b3, f2, d0, dn)
+    b3, f2, d0, dn, n_in = order.point(b3, f2, d0, dn, n_in)
     yf2 = permute(f2, "grp", GRPS)
     c3 = permute(b3, "seg", OUTWARD)
     x0 = send(d0)
@@ -570,7 +591,8 @@
         turn_kernel,
         shape(2 * block, 4 * rows),
         (near, n_in, n_far, n_across),
-        scratch=[pltpu.VMEM((4 * rows, 2 * block), bf16)],
+        specs={k: hbm for k in range(4)},
+        scratch=[pltpu.VMEM((4 * rows, 2 * block), bf16), pltpu.SemaphoreType.DMA((4,))],
         smems=0,
     )
     f3 = pick(b3, c3)
@@ -609,7 +631,7 @@
     _, whole = grads(2, n_t, parts2, whole, count=0)
     _, whole = grads(3, n_t, parts3, whole, count=0)
     grad_gain = jnp.sum(gains, 0, keepdims=True)
-    whole = place(((0, 0), (1, 0), (2, 0)), (r0, r1, r2), whole)
+    whole = place(((0, 0), (1, 0), (2, 0)), (r0, r1, r2), whole, True)
     below = call(copy_kernel, shape(tok.shape[0], width), (below0, below1), smems=0)
     r3, before, below, grad_gain, q_, k_, v_ = order.point(r3, before, below, grad_gain, *whole)
     grad_query, grad_key, grad_value = place(((3, 0),), (r3,), (q_, k_, v_))

time: 240 us -> 239 us (level)
  waiting for transfers between devices: 75.8 us -> 53.2 us
  starting transfers between devices: 86.8 us -> 106 us
  Pallas kernels: 55.3 us -> 58.4 us
    ppermute x35, waiting for transfers between devices: 75.8 us -> 53.2 us  [permute(): return lax.ppermute(value, axis, route)]
    ppermute x35, starting transfers between devices: 71 us -> 89.6 us  [permute(): return lax.ppermute(value, axis, route)]
    pallas_call x17, Pallas kernels: 55.3 us -> 58.4 us  [call(): pl.pallas_call(kernel, grid=(1,), out_shape=outs, in_specs=ins, out_specs...]
    unnamed x74 -> x58, local copies, waits for them, and re-layouts: 5.17 us -> 3.68 us
  transfers between devices with their start and end apart: 38 -> 38, of which waited for: 9 -> 6; matrix products, arithmetic and copies ran while one was open for 1% -> 1% of each run, Pallas kernels for 21% -> 22%
where the time goes in v4:
time: 239 us; the launch traced here: 235 us
  starting transfers between devices  106 us (44%)
  Pallas kernels  58.4 us (24%)
  waiting for transfers between devices  53.2 us (22%)
  blocking collectives  8.72 us (4%)
  local copies, waits for them, and re-layouts  4.06 us (2%)
  other arithmetic  3.2 us (1%)
    ppermute x35, starting transfers between devices, permute(): return lax.ppermute(value, axis, route)  89.6 us
    pallas_call x17, Pallas kernels, call(): pl.pallas_call(kernel, grid=(1,), out_shape=outs, in_specs=ins, out_specs...  58.4 us
    ppermute x35, waiting for transfers between devices, permute(): return lax.ppermute(value, axis, route)  53.2 us
    ppermute x3, starting transfers between devices, from_behind(): return lax.ppermute(block, axis, route)  15.9 us
    all_to_all x1, blocking collectives, on_line(): lax.all_to_all(grad_g.reshape(4, width // 4), 'seg', 0, 0, tiled=True)  8.72 us
  transfers between devices with their start and end apart: 38, of which 6 were waited for; matrix products, arithmetic and copies ran while one was open for 1% of the time, Pallas kernels for 22%

profile of v4, /device:TPU:7, one launch (start us, length us, event | category | flops | bytes accessed | tf_op | source)
XLA Modules:
  0.0 234.7 jit_solution(13736197905057409452)
XLA Ops:
  0.7 2.0 shard_map.127
  6.7 14.5 %collective-permute-done.a = bf16[512,768]{1,0:T(8,128)(2,1)S(1)} collective-permute-done((bf16[512,768]{1,0:T(8,128)(2,1)S(1)}, bf16[512,768]{1,0:T(8,128)(2,1)S(1)}, u32[]{:S(2)}, u32[]{:S(2)}) %collective-permute-start) | collective-permute-done | bytes 786464 | tf_op jit(solution)/shard_map/ppermute | solution.py:472
  22.1 5.2 %collective-permute-start.4 = (bf16[512,768]{1,0:T(8,128)(2,1)S(1)}, bf16[512,768]{1,0:T(8,128)(2,1)S(1)}, u32[]{:S(2)}, u32[]{:S(2)}) collective-permute-start(bf16[512,768]{1,0:T(8,128)(2,1)S(1)} %get-tuple-element.122), channel_id=1, source_target_pairs={{0,1},{1,0},{2,3},{3,2},{4,5},{5,4},{6,7},{7,6},{8,9},{9,8},{10,11... | collective-permute-start | bytes 2359304 | tf_op jit(solution)/shard_map/ppermute | solution.py:472
  27.6 15.4 %collective-permute-done.4.a = bf16[512,768]{1,0:T(8,128)(2,1)S(1)} collective-permute-done((bf16[512,768]{1,0:T(8,128)(2,1)S(1)}, bf16[512,768]{1,0:T(8,128)(2,1)S(1)}, u32[]{:S(2)}, u32[]{:S(2)}) %collective-permute-start.4) | collective-permute-done | bytes 786464 | tf_op jit(solution)/shard_map/ppermute | solution.py:472
  47.1 14.4 %collective-permute-done.6 = bf16[512,768]{1,0:T(8,128)(2,1)S(1)} collective-permute-done((bf16[512,768]{1,0:T(8,128)(2,1)S(1)}, bf16[512,768]{1,0:T(8,128)(2,1)S(1)}, u32[]{:S(2)}, u32[]{:S(2)}) %collective-permute-start.6) | collective-permute-done | bytes 786464 | tf_op jit(solution)/shard_map/ppermute | solution.py:472
  64.7 6.6 %collective-permute-start.7 = (bf16[288,1024]{1,0:T(8,128)(2,1)S(1)}, bf16[288,1024]{1,0:T(8,128)(2,1)S(1)}, u32[]{:S(2)}, u32[]{:S(2)}) collective-permute-start(bf16[288,1024]{1,0:T(8,128)(2,1)S(1)} %get-tuple-element.125), channel_id=1, source_target_pairs={{0,2},{3,1},{4,6},{7,5},{8,10},{11,9},{12,14},{15,13},{16,18},{19,... | collective-permute-start | bytes 1769480 | tf_op jit(solution)/shard_map/ppermute | solution.py:472
  72.6 6.6 %collective-permute-done.9 = bf16[512,768]{1,0:T(8,128)(2,1)S(1)} collective-permute-done((bf16[512,768]{1,0:T(8,128)(2,1)S(1)}, bf16[512,768]{1,0:T(8,128)(2,1)S(1)}, u32[]{:S(2)}, u32[]{:S(2)}) %collective-permute-start.9) | collective-permute-done | bytes 786464 | tf_op jit(solution)/shard_map/ppermute | solution.py:472
  82.2 22.0 %collective-permute-start.14 = (bf16[288,1024]{1,0:T(8,128)(2,1)S(1)}, bf16[288,1024]{1,0:T(8,128)(2,1)}, u32[]{:S(2)}, u32[]{:S(2)}) collective-permute-start(bf16[288,1024]{1,0:T(8,128)(2,1)S(1)} %get-tuple-element.138.n0), channel_id=1, source_target_pairs={{0,1},{3,2},{4,5},{7,6},{8,9},{11,10},{12,13},{15,14},{16,17},{19,... | collective-permute-start | bytes 1769480 | tf_op jit(solution)/shard_map/ppermute | solution.py:472
  104.4 7.7 %shard_map.129 = (bf16[288,768]{1,0:T(8,128)(2,1)S(1)}, f32[288,2048]{1,0:T(8,128)S(1)}) custom-call(s32[7]{0:T(128)S(1)} %stack.63.off_ref, bf16[288,2048]{1,0:T(8,128)(2,1)} %copy-done, bf16[512,2048]{1,0:T(8,128)(2,1)} %bitcast.38, bf16[512,512]{1,0:T(8,128)(2,1)} %bitcast.49, bf16[512,512]{1,0:T(8,128)(2,1)} %bitcast.54, bf16[512,768]{1,0:T(8,128)(2,1)} %copy-done.16, ...), custom_call_target="tpu_custom_call" | custom-call | tf_op jit(solution)/shard_map/pallas_call | solution.py:459
  117.0 6.5 %collective-permute-start.17 = (bf16[288,768]{1,0:T(8,128)(2,1)S(1)}, bf16[288,768]{1,0:T(8,128)(2,1)S(1)}, u32[]{:S(2)}, u32[]{:S(2)}) collective-permute-start(bf16[288,768]{1,0:T(8,128)(2,1)S(1)} %get-tuple-element.140.d0), channel_id=1, source_target_pairs={{0,2},{3,1},{4,6},{7,5},{8,10},{11,9},{12,14},{15,13},{16,18},{19,... | collective-permute-start | bytes 1327112 | tf_op jit(solution)/shard_map/ppermute | solution.py:472
  125.0 2.3 shard_map.131.nt_ref
  127.4 7.9 %shard_map.130 = (bf16[288,768]{1,0:T(8,128)(2,1)S(1)}, f32[288,2048]{1,0:T(8,128)S(1)}) custom-call(s32[7]{0:T(128)S(1)} %stack.63.off_ref, bf16[288,2048]{1,0:T(8,128)(2,1)} %copy-done, bf16[512,2048]{1,0:T(8,128)(2,1)} %bitcast.39, bf16[512,512]{1,0:T(8,128)(2,1)} %bitcast.50, bf16[512,512]{1,0:T(8,128)(2,1)} %bitcast.55, ...), custom_call_target="tpu_custom_call", output_to_operand_aliasing={{1}: (10, {})} | custom-call | tf_op jit(solution)/shard_map/pallas_call | solution.py:459
  137.3 6.5 %collective-permute-start.21 = (bf16[288,768]{1,0:T(8,128)(2,1)S(1)}, bf16[288,768]{1,0:T(8,128)(2,1)S(1)}, u32[]{:S(2)}, u32[]{:S(2)}) collective-permute-start(bf16[288,768]{1,0:T(8,128)(2,1)S(1)} %get-tuple-element.149.d0), channel_id=1, source_target_pairs={{0,2},{3,1},{4,6},{7,5},{8,10},{11,9},{12,14},{15,13},{16,18},{19,... | collective-permute-start | bytes 1327112 | tf_op jit(solution)/shard_map/ppermute | solution.py:472
  148.4 7.9 %shard_map.132 = (bf16[288,768]{1,0:T(8,128)(2,1)S(1)}, f32[288,2048]{1,0:T(8,128)S(1)}) custom-call(s32[7]{0:T(128)S(1)} %stack.63.off_ref, bf16[288,2048]{1,0:T(8,128)(2,1)} %copy-done, bf16[512,2048]{1,0:T(8,128)(2,1)} %bitcast.40, bf16[512,512]{1,0:T(8,128)(2,1)} %bitcast.51, bf16[512,512]{1,0:T(8,128)(2,1)} %bitcast.56, ...), custom_call_target="tpu_custom_call", output_to_operand_aliasing={{1}: (10, {})} | custom-call | tf_op jit(solution)/shard_map/pallas_call | solution.py:459
  157.0 6.5 %collective-permute-start.25 = (bf16[288,768]{1,0:T(8,128)(2,1)S(1)}, bf16[288,768]{1,0:T(8,128)(2,1)S(1)}, u32[]{:S(2)}, u32[]{:S(2)}) collective-permute-start(bf16[288,768]{1,0:T(8,128)(2,1)S(1)} %get-tuple-element.159.d0), channel_id=1, source_target_pairs={{0,2},{3,1},{4,6},{7,5},{8,10},{11,9},{12,14},{15,13},{16,18},{19,... | collective-permute-start | bytes 1327112 | tf_op jit(solution)/shard_map/ppermute | solution.py:472
  168.0 7.8 %shard_map.134 = (bf16[288,768]{1,0:T(8,128)(2,1)S(1)}, f32[288,2048]{1,0:T(8,128)S(1)}) custom-call(s32[7]{0:T(128)S(1)} %stack.63.off_ref, bf16[288,2048]{1,0:T(8,128)(2,1)} %copy-done, bf16[512,2048]{1,0:T(8,128)(2,1)} %bitcast.41, bf16[512,512]{1,0:T(8,128)(2,1)} %bitcast.52, bf16[512,512]{1,0:T(8,128)(2,1)} %bitcast.57, ...), custom_call_target="tpu_custom_call", output_to_operand_aliasing={{1}: (10, {})} | custom-call | tf_op jit(solution)/shard_map/pallas_call | solution.py:459
  179.4 7.7 %collective-permute-start.30 = (bf16[288,768]{1,0:T(8,128)(2,1)S(1)}, bf16[288,768]{1,0:T(8,128)(2,1)S(1)}, u32[]{:S(2)}, u32[]{:S(2)}) collective-permute-start(bf16[288,768]{1,0:T(8,128)(2,1)S(1)} %get-tuple-element.171.d0), channel_id=1, source_target_pairs={{0,2},{3,1},{4,6},{7,5},{8,10},{11,9},{12,14},{15,13},{16,18},{19,... | collective-permute-start | bytes 1327112 | tf_op jit(solution)/shard_map/ppermute | solution.py:472
  188.4 3.1 %shard_map.137 = (bf16[128,2048]{1,0:T(8,128)(2,1)}, bf16[128,2048]{1,0:T(8,128)(2,1)}, bf16[32,2048]{1,0:T(8,128)(2,1)}, f32[1,2048]{1,0:T(1,128)S(1)}) custom-call(f32[288,2048]{1,0:T(8,128)S(1)} %get-tuple-element.175.dn_ref, bf16[256,2048]{1,0:T(8,128)(2,1)S(1)} %bitcast.31, bf16[32,2048]{1,0:T(8,128)(2,1)S(1)} %bitcast.34, ...), custom_call_target="tpu_custom_call" | custom-call | tf_op jit(solution)/shard_map/pallas_call | solution.py:459
  191.5 8.7 %all_to_all.12 = f32[4,1,512]{2,1,0:T(1,128)S(1)} all-to-all(f32[4,1,512]{2,1,0:T(1,128)S(1)} %bitcast.35), channel_id=1, replica_groups=mesh['grp'=2,'section'=4,'seg'=4] {'seg'}, dimensions={0} | all-to-all | bytes 16384 | tf_op jit(solution)/shard_map/all_to_all | solution.py:622
  203.4 12.5 %collective-permute-start.36 = (bf16[128,2048]{1,0:T(8,128)(2,1)}, bf16[128,2048]{1,0:T(8,128)(2,1)}, u32[]{:S(2)}, u32[]{:S(2)}) collective-permute-start(bf16[128,2048]{1,0:T(8,128)(2,1)} %get-tuple-element.184), channel_id=1, source_target_pairs={{4,0},{8,4},{12,8},{5,1},{9,5},{13,9},{6,2},{10,6},{14,10},{7,3},{... | collective-permute-start | bytes 1572872 | tf_op jit(solution)/shard_map/ppermute | solution.py:19
  215.9 2.1 collective-permute-start.37
  225.3 4.0 %shard_map.142 = (f32[512,2048]{1,0:T(8,128)}, f32[512,512]{1,0:T(8,128)}, f32[512,512]{1,0:T(8,128)}) custom-call(s32[6]{0:T(128)S(1)} %stack.55.place_ref, bf16[512,768]{1,0:T(8,128)(2,1)} %copy-done.20, bf16[512,768]{1,0:T(8,128)(2,1)} %copy-done.21, bf16[512,768]{1,0:T(8,128)(2,1)} %copy-done.22, ...), custom_call_target="tpu_custom_call", output_to_operand_aliasing={{0}: (4, {}), {1}: (5, {}), {2}: (6, {})} | custom-call | tf_op jit(solution)/shard_map/pallas_call | solution.py:459
  229.4 2.2 shard_map.139
  231.6 2.4 %shard_map.143 = (f32[512,2048]{1,0:T(8,128)}, f32[512,512]{1,0:T(8,128)}, f32[512,512]{1,0:T(8,128)}) custom-call(s32[6]{0:T(128)S(1)} %stack.55.place_ref, bf16[512,768]{1,0:T(8,128)(2,1)} %collective-permute-done.34.refs_0_, f32[512,2048]{1,0:T(8,128)} %get-tuple-element.205.refs_1_, ...), custom_call_target="tpu_custom_call", output_to_operand_aliasing={{0}: (2, {}), {1}: (3, {}), {2}: (4, {})} | custom-call | tf_op jit(solution)/shard_map/pallas_call | solution.py:459
  (142 shorter events, 50.6 us)
Async XLA Ops:
  2.8 18.5 %collective-permute-start = (bf16[512,768]{1,0:T(8,128)(2,1)S(1)}, bf16[512,768]{1,0:T(8,128)(2,1)S(1)}, u32[]{:S(2)}, u32[]{:S(2)}) collective-permute-start(bf16[512,768]{1,0:T(8,128)(2,1)S(1)} %get-tuple-element.115), channel_id=1, source_target_pairs={{0,1},{1,0},{2,3},{3,2},{4,5},{5,4},{6,7},{7,6},{8,9},{9,8},{10,11... | collective-permute-start | bytes 2359304 | tf_op jit(solution)/shard_map/ppermute | solution.py:472
  22.1 20.9 %collective-permute-start.4 = (bf16[512,768]{1,0:T(8,128)(2,1)S(1)}, bf16[512,768]{1,0:T(8,128)(2,1)S(1)}, u32[]{:S(2)}, u32[]{:S(2)}) collective-permute-start(bf16[512,768]{1,0:T(8,128)(2,1)S(1)} %get-tuple-element.122), channel_id=1, source_target_pairs={{0,1},{1,0},{2,3},{3,2},{4,5},{5,4},{6,7},{7,6},{8,9},{9,8},{10,11... | collective-permute-start | bytes 2359304 | tf_op jit(solution)/shard_map/ppermute | solution.py:472
  61.6 17.6 %collective-permute-start.9 = (bf16[512,768]{1,0:T(8,128)(2,1)S(1)}, bf16[512,768]{1,0:T(8,128)(2,1)S(1)}, u32[]{:S(2)}, u32[]{:S(2)}) collective-permute-start(bf16[512,768]{1,0:T(8,128)(2,1)S(1)} %collective-permute-done.5), channel_id=1, source_target_pairs={{1,0},{2,3},{5,4},{6,7},{9,8},{10,11},{13,12},{14,15},{17,16},{18,... | collective-permute-start | bytes 2359304 | tf_op jit(solution)/shard_map/ppermute | solution.py:472
  71.3 33.0 %collective-permute-start.13 = (bf16[512,768]{1,0:T(8,128)(2,1)S(1)}, bf16[512,768]{1,0:T(8,128)(2,1)}, u32[]{:S(2)}, u32[]{:S(2)}) collective-permute-start(bf16[512,768]{1,0:T(8,128)(2,1)S(1)} %broadcast_select_fusion.3.far), channel_id=1, source_target_pairs={{0,16},{16,0},{1,17},{17,1},{2,18},{18,2},{3,19},{19,3},{4,20},{20... | collective-permute-start | bytes 2359304 | tf_op jit(solution)/shard_map/ppermute | solution.py:472
  79.4 32.8 %collective-permute-start.12 = (bf16[512,768]{1,0:T(8,128)(2,1)}, bf16[512,768]{1,0:T(8,128)(2,1)}, u32[]{:S(2)}, u32[]{:S(2)}) collective-permute-start(bf16[512,768]{1,0:T(8,128)(2,1)} %collective-permute-done.8), channel_id=1, source_target_pairs={{1,0},{2,3},{5,4},{6,7},{9,8},{10,11},{13,12},{14,15},{17,16},{18,... | collective-permute-start | bytes 2359304 | tf_op jit(solution)/shard_map/ppermute | solution.py:472
  80.7 32.7 %collective-permute-start.11 = (bf16[512,768]{1,0:T(8,128)(2,1)}, bf16[512,768]{1,0:T(8,128)(2,1)}, u32[]{:S(2)}, u32[]{:S(2)}) collective-permute-start(bf16[512,768]{1,0:T(8,128)(2,1)} %pad_maximum_fusion.3), channel_id=1, source_target_pairs={{1,2},{2,1},{5,6},{6,5},{9,10},{10,9},{13,14},{14,13},{17,18},{18,... | collective-permute-start | bytes 2359304 | tf_op jit(solution)/shard_map/ppermute | solution.py:472
  82.2 31.1 %collective-permute-start.14 = (bf16[288,1024]{1,0:T(8,128)(2,1)S(1)}, bf16[288,1024]{1,0:T(8,128)(2,1)}, u32[]{:S(2)}, u32[]{:S(2)}) collective-permute-start(bf16[288,1024]{1,0:T(8,128)(2,1)S(1)} %get-tuple-element.138.n0), channel_id=1, source_target_pairs={{0,1},{3,2},{4,5},{7,6},{8,9},{11,10},{12,13},{15,14},{16,17},{19,... | collective-permute-start | bytes 1769480 | tf_op jit(solution)/shard_map/ppermute | solution.py:472
  104.3 19.2 %collective-permute-start.19 = (bf16[512,768]{1,0:T(8,128)(2,1)S(1)}, bf16[512,768]{1,0:T(8,128)(2,1)S(1)}, u32[]{:S(2)}, u32[]{:S(2)}) collective-permute-start(bf16[512,768]{1,0:T(8,128)(2,1)S(1)} %broadcast_select_fusion.2.far), channel_id=1, source_target_pairs={{0,16},{16,0},{1,17},{17,1},{2,18},{18,2},{3,19},{19,3},{4,20},{20... | collective-permute-start | bytes 2359304 | tf_op jit(solution)/shard_map/ppermute | solution.py:472
  113.4 21.8 %collective-permute-start.15 = (bf16[512,768]{1,0:T(8,128)(2,1)}, bf16[512,768]{1,0:T(8,128)(2,1)S(1)}, u32[]{:S(2)}, u32[]{:S(2)}) collective-permute-start(bf16[512,768]{1,0:T(8,128)(2,1)} %collective-permute-done.11), channel_id=1, source_target_pairs={{1,0},{2,3},{5,4},{6,7},{9,8},{10,11},{13,12},{14,15},{17,16},{18,... | collective-permute-start | bytes 2359304 | tf_op jit(solution)/shard_map/ppermute | solution.py:472
  114.9 32.2 %collective-permute-start.23 = (bf16[512,768]{1,0:T(8,128)(2,1)S(1)}, bf16[512,768]{1,0:T(8,128)(2,1)S(1)}, u32[]{:S(2)}, u32[]{:S(2)}) collective-permute-start(bf16[512,768]{1,0:T(8,128)(2,1)S(1)} %broadcast_select_fusion.1.far), channel_id=1, source_target_pairs={{0,16},{16,0},{1,17},{17,1},{2,18},{18,2},{3,19},{19,3},{4,20},{20... | collective-permute-start | bytes 2359304 | tf_op jit(solution)/shard_map/ppermute | solution.py:472
  116.4 19.0 %collective-permute-start.18 = (bf16[288,768]{1,0:T(8,128)(2,1)S(1)}, bf16[288,768]{1,0:T(8,128)(2,1)S(1)}, u32[]{:S(2)}, u32[]{:S(2)}) collective-permute-start(bf16[288,768]{1,0:T(8,128)(2,1)S(1)} %get-tuple-element.140.d0), channel_id=1, source_target_pairs={{1,2},{2,1},{5,6},{6,5},{9,10},{10,9},{13,14},{14,13},{17,18},{18,... | collective-permute-start | bytes 1327112 | tf_op jit(solution)/shard_map/ppermute | solution.py:472
  117.0 18.3 %collective-permute-start.17 = (bf16[288,768]{1,0:T(8,128)(2,1)S(1)}, bf16[288,768]{1,0:T(8,128)(2,1)S(1)}, u32[]{:S(2)}, u32[]{:S(2)}) collective-permute-start(bf16[288,768]{1,0:T(8,128)(2,1)S(1)} %get-tuple-element.140.d0), channel_id=1, source_target_pairs={{0,2},{3,1},{4,6},{7,5},{8,10},{11,9},{12,14},{15,13},{16,18},{19,... | collective-permute-start | bytes 1327112 | tf_op jit(solution)/shard_map/ppermute | solution.py:472
  136.7 19.6 %collective-permute-start.22 = (bf16[288,768]{1,0:T(8,128)(2,1)S(1)}, bf16[288,768]{1,0:T(8,128)(2,1)S(1)}, u32[]{:S(2)}, u32[]{:S(2)}) collective-permute-start(bf16[288,768]{1,0:T(8,128)(2,1)S(1)} %get-tuple-element.149.d0), channel_id=1, source_target_pairs={{1,2},{2,1},{5,6},{6,5},{9,10},{10,9},{13,14},{14,13},{17,18},{18,... | collective-permute-start | bytes 1327112 | tf_op jit(solution)/shard_map/ppermute | solution.py:472
  137.3 19.0 %collective-permute-start.21 = (bf16[288,768]{1,0:T(8,128)(2,1)S(1)}, bf16[288,768]{1,0:T(8,128)(2,1)S(1)}, u32[]{:S(2)}, u32[]{:S(2)}) collective-permute-start(bf16[288,768]{1,0:T(8,128)(2,1)S(1)} %get-tuple-element.149.d0), channel_id=1, source_target_pairs={{0,2},{3,1},{4,6},{7,5},{8,10},{11,9},{12,14},{15,13},{16,18},{19,... | collective-permute-start | bytes 1327112 | tf_op jit(solution)/shard_map/ppermute | solution.py:472
  145.2 21.5 %collective-permute-start.27 = (bf16[512,768]{1,0:T(8,128)(2,1)S(1)}, bf16[512,768]{1,0:T(8,128)(2,1)S(1)}, u32[]{:S(2)}, u32[]{:S(2)}) collective-permute-start(bf16[512,768]{1,0:T(8,128)(2,1)S(1)} %broadcast_select_fusion.far), channel_id=1, source_target_pairs={{0,16},{16,0},{1,17},{17,1},{2,18},{18,2},{3,19},{19,3},{4,20},{20... | collective-permute-start | bytes 2359304 | tf_op jit(solution)/shard_map/ppermute | solution.py:472
  147.1 28.8 %collective-permute-start.28 = (bf16[512,768]{1,0:T(8,128)(2,1)S(1)}, bf16[512,768]{1,0:T(8,128)(2,1)S(1)}, u32[]{:S(2)}, u32[]{:S(2)}) collective-permute-start(bf16[512,768]{1,0:T(8,128)(2,1)S(1)} %get-tuple-element.158), channel_id=1, source_target_pairs={{1,0},{2,3},{5,4},{6,7},{9,8},{10,11},{13,12},{14,15},{17,16},{18,... | collective-permute-start | bytes 2359304 | tf_op jit(solution)/shard_map/ppermute | solution.py:472
  156.3 19.6 %collective-permute-start.26 = (bf16[288,768]{1,0:T(8,128)(2,1)S(1)}, bf16[288,768]{1,0:T(8,128)(2,1)S(1)}, u32[]{:S(2)}, u32[]{:S(2)}) collective-permute-start(bf16[288,768]{1,0:T(8,128)(2,1)S(1)} %get-tuple-element.159.d0), channel_id=1, source_target_pairs={{1,2},{2,1},{5,6},{6,5},{9,10},{10,9},{13,14},{14,13},{17,18},{18,... | collective-permute-start | bytes 1327112 | tf_op jit(solution)/shard_map/ppermute | solution.py:472
  157.0 18.9 %collective-permute-start.25 = (bf16[288,768]{1,0:T(8,128)(2,1)S(1)}, bf16[288,768]{1,0:T(8,128)(2,1)S(1)}, u32[]{:S(2)}, u32[]{:S(2)}) collective-permute-start(bf16[288,768]{1,0:T(8,128)(2,1)S(1)} %get-tuple-element.159.d0), channel_id=1, source_target_pairs={{0,2},{3,1},{4,6},{7,5},{8,10},{11,9},{12,14},{15,13},{16,18},{19,... | collective-permute-start | bytes 1327112 | tf_op jit(solution)/shard_map/ppermute | solution.py:472
  166.7 33.5 %collective-permute-start.32 = (bf16[512,768]{1,0:T(8,128)(2,1)S(1)}, bf16[512,768]{1,0:T(8,128)(2,1)S(1)}, u32[]{:S(2)}, u32[]{:S(2)}) collective-permute-start(bf16[512,768]{1,0:T(8,128)(2,1)S(1)} %get-tuple-element.170), channel_id=1, source_target_pairs={{1,0},{2,3},{5,4},{6,7},{9,8},{10,11},{13,12},{14,15},{17,16},{18,... | collective-permute-start | bytes 2359304 | tf_op jit(solution)/shard_map/ppermute | solution.py:472
  177.4 22.9 %collective-permute-start.33 = (bf16[512,768]{1,0:T(8,128)(2,1)S(1)}, bf16[512,768]{1,0:T(8,128)(2,1)S(1)}, u32[]{:S(2)}, u32[]{:S(2)}) collective-permute-start(bf16[512,768]{1,0:T(8,128)(2,1)S(1)} %shard_map.136), channel_id=1, source_target_pairs={{1,0},{2,3},{5,4},{6,7},{9,8},{10,11},{13,12},{14,15},{17,16},{18,... | collective-permute-start | bytes 2359304 | tf_op jit(solution)/shard_map/ppermute | solution.py:472
  178.7 21.5 %collective-permute-start.31 = (bf16[288,768]{1,0:T(8,128)(2,1)S(1)}, bf16[288,768]{1,0:T(8,128)(2,1)S(1)}, u32[]{:S(2)}, u32[]{:S(2)}) collective-permute-start(bf16[288,768]{1,0:T(8,128)(2,1)S(1)} %get-tuple-element.171.d0), channel_id=1, source_target_pairs={{1,2},{2,1},{5,6},{6,5},{9,10},{10,9},{13,14},{14,13},{17,18},{18,... | collective-permute-start | bytes 1327112 | tf_op jit(solution)/shard_map/ppermute | solution.py:472
  179.4 20.9 %collective-permute-start.30 = (bf16[288,768]{1,0:T(8,128)(2,1)S(1)}, bf16[288,768]{1,0:T(8,128)(2,1)S(1)}, u32[]{:S(2)}, u32[]{:S(2)}) collective-permute-start(bf16[288,768]{1,0:T(8,128)(2,1)S(1)} %get-tuple-element.171.d0), channel_id=1, source_target_pairs={{0,2},{3,1},{4,6},{7,5},{8,10},{11,9},{12,14},{15,13},{16,18},{19,... | collective-permute-start | bytes 1327112 | tf_op jit(solution)/shard_map/ppermute | solution.py:472
  202.1 29.5 %collective-permute-start.34 = (bf16[512,768]{1,0:T(8,128)(2,1)}, bf16[512,768]{1,0:T(8,128)(2,1)}, u32[]{:S(2)}, u32[]{:S(2)}) collective-permute-start(bf16[512,768]{1,0:T(8,128)(2,1)} %shard_map.138), channel_id=1, source_target_pairs={{1,0},{2,3},{5,4},{6,7},{9,8},{10,11},{13,12},{14,15},{17,16},{18,... | collective-permute-start | bytes 2359304 | tf_op jit(solution)/shard_map/ppermute | solution.py:472
  203.4 26.0 %collective-permute-start.36 = (bf16[128,2048]{1,0:T(8,128)(2,1)}, bf16[128,2048]{1,0:T(8,128)(2,1)}, u32[]{:S(2)}, u32[]{:S(2)}) collective-permute-start(bf16[128,2048]{1,0:T(8,128)(2,1)} %get-tuple-element.184), channel_id=1, source_target_pairs={{4,0},{8,4},{12,8},{5,1},{9,5},{13,9},{6,2},{10,6},{14,10},{7,3},{... | collective-permute-start | bytes 1572872 | tf_op jit(solution)/shard_map/ppermute | solution.py:19
  (42 other events, 437.9 us)

commit v5 on v4

--- a/solution.py
+++ b/solution.py
@@ -562,27 +562,27 @@
     b0 = permute(z_and([a01[:quarter], h01[:quarter]]), "seg", ACROSS)
     ya01 = permute(a01, "grp", GRPS)
     to1 = z_and([a01[quarter:], h01[quarter:]])
-    b0, ya01, a23, to1, h23, near, far = order.point(b0, ya01, a23, to1, h23, near, far)
+    n_far = permute(far, "seg", FAR_INWARD)
+    b0, ya01, a23, to1, h23, near, n_far = order.point(b0, ya01, a23, to1, h23, near, n_far)
+    ya23 = permute(a23, "grp", GRPS)
     b1 = permute(to1, "seg", ACROSS)
     c0 = permute(b0, "seg", OUTWARD)
     to2 = z_and([a23[:quarter], h23[:quarter]])
     to3 = z_and([a23[quarter:], h23[quarter:]])
     f0 = pick(b0, c0)
-    b1, f0, to2, to3, a23, near, far = order.point(b1, f0, to2, to3, a23, near, far)
+    ya23, b1, f0, to2, to3, near = order.point(ya23, b1, f0, to2, to3, near)
     yf0 = permute(f0, "grp", GRPS)
-    ya23 = permute(a23, "grp", GRPS)
-    n_far = permute(far, "seg", FAR_INWARD)
+    n_in = permute(near, "seg", INWARD)
     b2 = permute(to2, "seg", ACROSS)
     c1 = permute(b1, "seg", OUTWARD)
     f1 = pick(b1, c1)
-    n_far, b2, f1, to3, ya23, near = order.point(n_far, b2, f1, to3, ya23, near)
+    n_in, b2, f1, to3 = order.point(n_in, b2, f1, to3)
     yf1 = permute(f1, "grp", GRPS)
-    n_in = permute(near, "seg", INWARD)
     b3 = permute(to3, "seg", ACROSS)
     c2 = permute(b2, "seg", OUTWARD)
     d0, dn = head(0, (a01, f0, ya01, yf0), (0, 0))
     f2 = pick(b2, c2)
-    b3, f2, d0, dn, n_in = order.point(b3, f2, d0, dn, n_in)
+    b3, f2, d0, dn = order.point(b3, f2, d0, dn)
     yf2 = permute(f2, "grp", GRPS)
     c3 = permute(b3, "seg", OUTWARD)
     x0 = send(d0)

time: 239 us -> 236 us (0.987)
  starting transfers between devices: 106 us -> 86.3 us
  waiting for transfers between devices: 53.2 us -> 69.4 us
    ppermute x35, starting transfers between devices: 89.6 us -> 69.9 us  [permute(): return lax.ppermute(value, axis, route)]
    ppermute x35, waiting for transfers between devices: 53.2 us -> 69.4 us  [permute(): return lax.ppermute(value, axis, route)]
    unnamed x58 -> x60, local copies, waits for them, and re-layouts: 3.68 us -> 5.4 us
  transfers between devices with their start and end apart: 38 -> 38, of which waited for: 6 -> 7; matrix products, arithmetic and copies ran while one was open for 1% -> 1% of each run, Pallas kernels for 22% -> 22%
where the time goes in v5:
time: 236 us; the launch traced here: 233 us
  starting transfers between devices  86.3 us (37%)
  waiting for transfers between devices  69.4 us (29%)
  Pallas kernels  58.4 us (25%)
  blocking collectives  8.73 us (4%)
  local copies, waits for them, and re-layouts  5.77 us (2%)
  other arithmetic  3.19 us (1%)
    ppermute x35, starting transfers between devices, permute(): return lax.ppermute(value, axis, route)  69.9 us
    ppermute x35, waiting for transfers between devices, permute(): return lax.ppermute(value, axis, route)  69.4 us
    pallas_call x17, Pallas kernels, call(): pl.pallas_call(kernel, grid=(1,), out_shape=outs, in_specs=ins, out_specs...  58.4 us
    ppermute x3, starting transfers between devices, from_behind(): return lax.ppermute(block, axis, route)  16.5 us
    all_to_all x1, blocking collectives, on_line(): lax.all_to_all(grad_g.reshape(4, width // 4), 'seg', 0, 0, tiled=True)  8.73 us
    unnamed x60, local copies, waits for them, and re-layouts  5.4 us
  transfers between devices with their start and end apart: 38, of which 7 were waited for; matrix products, arithmetic and copies ran while one was open for 1% of the time, Pallas kernels for 22%

profile of v5, /device:TPU:7, one launch (start us, length us, event | category | flops | bytes accessed | tf_op | source)
XLA Modules:
  0.0 233.3 jit_solution(1848751993861575625)
XLA Ops:
  6.7 14.5 %collective-permute-done.a = bf16[512,768]{1,0:T(8,128)(2,1)S(1)} collective-permute-done((bf16[512,768]{1,0:T(8,128)(2,1)S(1)}, bf16[512,768]{1,0:T(8,128)(2,1)S(1)}, u32[]{:S(2)}, u32[]{:S(2)}) %collective-permute-start) | collective-permute-done | bytes 786464 | tf_op jit(solution)/shard_map/ppermute | solution.py:472
  22.1 5.2 %collective-permute-start.4 = (bf16[512,768]{1,0:T(8,128)(2,1)S(1)}, bf16[512,768]{1,0:T(8,128)(2,1)S(1)}, u32[]{:S(2)}, u32[]{:S(2)}) collective-permute-start(bf16[512,768]{1,0:T(8,128)(2,1)S(1)} %get-tuple-element.118), channel_id=1, source_target_pairs={{0,1},{1,0},{2,3},{3,2},{4,5},{5,4},{6,7},{7,6},{8,9},{9,8},{10,11... | collective-permute-start | bytes 2359304 | tf_op jit(solution)/shard_map/ppermute | solution.py:472
  27.6 2.1 collective-permute-start.5
  29.7 25.0 %collective-permute-done.5.n2 = bf16[288,1024]{1,0:T(8,128)(2,1)S(1)} collective-permute-done((bf16[288,1024]{1,0:T(8,128)(2,1)S(1)}, bf16[288,1024]{1,0:T(8,128)(2,1)S(1)}, u32[]{:S(2)}, u32[]{:S(2)}) %collective-permute-start.5) | collective-permute-done | bytes 589856 | tf_op jit(solution)/shard_map/ppermute | solution.py:472
  59.0 15.4 %collective-permute-done.8 = bf16[512,768]{1,0:T(8,128)(2,1)S(1)} collective-permute-done((bf16[512,768]{1,0:T(8,128)(2,1)S(1)}, bf16[512,768]{1,0:T(8,128)(2,1)S(1)}, u32[]{:S(2)}, u32[]{:S(2)}) %collective-permute-start.8) | collective-permute-done | bytes 786464 | tf_op jit(solution)/shard_map/ppermute | solution.py:472
  77.4 6.6 %collective-permute-start.9 = (bf16[288,1024]{1,0:T(8,128)(2,1)S(1)}, bf16[288,1024]{1,0:T(8,128)(2,1)S(1)}, u32[]{:S(2)}, u32[]{:S(2)}) collective-permute-start(bf16[288,1024]{1,0:T(8,128)(2,1)S(1)} %get-tuple-element.120.n0), channel_id=1, source_target_pairs={{0,1},{3,2},{4,5},{7,6},{8,9},{11,10},{12,13},{15,14},{16,17},{19,... | collective-permute-start | bytes 1769480 | tf_op jit(solution)/shard_map/ppermute | solution.py:472
  84.3 8.6 %collective-permute-done.11 = bf16[512,768]{1,0:T(8,128)(2,1)S(1)} collective-permute-done((bf16[512,768]{1,0:T(8,128)(2,1)S(1)}, bf16[512,768]{1,0:T(8,128)(2,1)S(1)}, u32[]{:S(2)}, u32[]{:S(2)}) %collective-permute-start.11) | collective-permute-done | bytes 786464 | tf_op jit(solution)/shard_map/ppermute | solution.py:472
  98.6 7.7 %shard_map.129 = (bf16[288,768]{1,0:T(8,128)(2,1)S(1)}, f32[288,2048]{1,0:T(8,128)S(1)}) custom-call(s32[7]{0:T(128)S(1)} %stack.63.off_ref, bf16[288,2048]{1,0:T(8,128)(2,1)} %copy-done, bf16[512,2048]{1,0:T(8,128)(2,1)} %bitcast.38, bf16[512,512]{1,0:T(8,128)(2,1)} %bitcast.49, bf16[512,512]{1,0:T(8,128)(2,1)} %bitcast.54, bf16[512,768]{1,0:T(8,128)(2,1)} %copy-done.16, ...), custom_call_target="tpu_custom_call" | custom-call | tf_op jit(solution)/shard_map/pallas_call | solution.py:459
  106.3 3.9 %collective-permute-done.13 = bf16[512,768]{1,0:T(8,128)(2,1)} collective-permute-done((bf16[512,768]{1,0:T(8,128)(2,1)}, bf16[512,768]{1,0:T(8,128)(2,1)}, u32[]{:S(2)}, u32[]{:S(2)}) %collective-permute-start.13) | collective-permute-done | bytes 786464 | tf_op jit(solution)/shard_map/ppermute | solution.py:472
  113.9 7.1 %collective-permute-start.17 = (bf16[288,768]{1,0:T(8,128)(2,1)S(1)}, bf16[288,768]{1,0:T(8,128)(2,1)S(1)}, u32[]{:S(2)}, u32[]{:S(2)}) collective-permute-start(bf16[288,768]{1,0:T(8,128)(2,1)S(1)} %get-tuple-element.132.d0), channel_id=1, source_target_pairs={{0,2},{3,1},{4,6},{7,5},{8,10},{11,9},{12,14},{15,13},{16,18},{19,... | collective-permute-start | bytes 1327112 | tf_op jit(solution)/shard_map/ppermute | solution.py:472
  122.6 2.3 shard_map.131.nt_ref
  125.0 7.8 %shard_map.130 = (bf16[288,768]{1,0:T(8,128)(2,1)S(1)}, f32[288,2048]{1,0:T(8,128)S(1)}) custom-call(s32[7]{0:T(128)S(1)} %stack.63.off_ref, bf16[288,2048]{1,0:T(8,128)(2,1)} %copy-done, bf16[512,2048]{1,0:T(8,128)(2,1)} %bitcast.39, bf16[512,512]{1,0:T(8,128)(2,1)} %bitcast.50, bf16[512,512]{1,0:T(8,128)(2,1)} %bitcast.55, ...), custom_call_target="tpu_custom_call", output_to_operand_aliasing={{1}: (10, {})} | custom-call | tf_op jit(solution)/shard_map/pallas_call | solution.py:459
  134.1 6.5 %collective-permute-start.21 = (bf16[288,768]{1,0:T(8,128)(2,1)S(1)}, bf16[288,768]{1,0:T(8,128)(2,1)S(1)}, u32[]{:S(2)}, u32[]{:S(2)}) collective-permute-start(bf16[288,768]{1,0:T(8,128)(2,1)S(1)} %get-tuple-element.141.d0), channel_id=1, source_target_pairs={{0,2},{3,1},{4,6},{7,5},{8,10},{11,9},{12,14},{15,13},{16,18},{19,... | collective-permute-start | bytes 1327112 | tf_op jit(solution)/shard_map/ppermute | solution.py:472
  146.5 7.9 %shard_map.132 = (bf16[288,768]{1,0:T(8,128)(2,1)S(1)}, f32[288,2048]{1,0:T(8,128)S(1)}) custom-call(s32[7]{0:T(128)S(1)} %stack.63.off_ref, bf16[288,2048]{1,0:T(8,128)(2,1)} %copy-done, bf16[512,2048]{1,0:T(8,128)(2,1)} %bitcast.40, bf16[512,512]{1,0:T(8,128)(2,1)} %bitcast.51, bf16[512,512]{1,0:T(8,128)(2,1)} %bitcast.56, ...), custom_call_target="tpu_custom_call", output_to_operand_aliasing={{1}: (10, {})} | custom-call | tf_op jit(solution)/shard_map/pallas_call | solution.py:459
  155.1 6.5 %collective-permute-start.25 = (bf16[288,768]{1,0:T(8,128)(2,1)S(1)}, bf16[288,768]{1,0:T(8,128)(2,1)S(1)}, u32[]{:S(2)}, u32[]{:S(2)}) collective-permute-start(bf16[288,768]{1,0:T(8,128)(2,1)S(1)} %get-tuple-element.151.d0), channel_id=1, source_target_pairs={{0,2},{3,1},{4,6},{7,5},{8,10},{11,9},{12,14},{15,13},{16,18},{19,... | collective-permute-start | bytes 1327112 | tf_op jit(solution)/shard_map/ppermute | solution.py:472
  166.1 7.9 %shard_map.134 = (bf16[288,768]{1,0:T(8,128)(2,1)S(1)}, f32[288,2048]{1,0:T(8,128)S(1)}) custom-call(s32[7]{0:T(128)S(1)} %stack.63.off_ref, bf16[288,2048]{1,0:T(8,128)(2,1)} %copy-done, bf16[512,2048]{1,0:T(8,128)(2,1)} %bitcast.41, bf16[512,512]{1,0:T(8,128)(2,1)} %bitcast.52, bf16[512,512]{1,0:T(8,128)(2,1)} %bitcast.57, ...), custom_call_target="tpu_custom_call", output_to_operand_aliasing={{1}: (10, {})} | custom-call | tf_op jit(solution)/shard_map/pallas_call | solution.py:459
  177.4 7.7 %collective-permute-start.30 = (bf16[288,768]{1,0:T(8,128)(2,1)S(1)}, bf16[288,768]{1,0:T(8,128)(2,1)S(1)}, u32[]{:S(2)}, u32[]{:S(2)}) collective-permute-start(bf16[288,768]{1,0:T(8,128)(2,1)S(1)} %get-tuple-element.163.d0), channel_id=1, source_target_pairs={{0,2},{3,1},{4,6},{7,5},{8,10},{11,9},{12,14},{15,13},{16,18},{19,... | collective-permute-start | bytes 1327112 | tf_op jit(solution)/shard_map/ppermute | solution.py:472
  186.5 3.1 %shard_map.137 = (bf16[128,2048]{1,0:T(8,128)(2,1)}, bf16[128,2048]{1,0:T(8,128)(2,1)}, bf16[32,2048]{1,0:T(8,128)(2,1)}, f32[1,2048]{1,0:T(1,128)S(1)}) custom-call(f32[288,2048]{1,0:T(8,128)S(1)} %get-tuple-element.167.dn_ref, bf16[256,2048]{1,0:T(8,128)(2,1)S(1)} %bitcast.31, bf16[32,2048]{1,0:T(8,128)(2,1)S(1)} %bitcast.34, ...), custom_call_target="tpu_custom_call" | custom-call | tf_op jit(solution)/shard_map/pallas_call | solution.py:459
  189.5 8.7 %all_to_all.12 = f32[4,1,512]{2,1,0:T(1,128)S(1)} all-to-all(f32[4,1,512]{2,1,0:T(1,128)S(1)} %bitcast.35), channel_id=1, replica_groups=mesh['grp'=2,'section'=4,'seg'=4] {'seg'}, dimensions={0} | all-to-all | bytes 16384 | tf_op jit(solution)/shard_map/all_to_all | solution.py:622
  201.5 13.1 %collective-permute-start.36 = (bf16[128,2048]{1,0:T(8,128)(2,1)}, bf16[128,2048]{1,0:T(8,128)(2,1)}, u32[]{:S(2)}, u32[]{:S(2)}) collective-permute-start(bf16[128,2048]{1,0:T(8,128)(2,1)} %get-tuple-element.176), channel_id=1, source_target_pairs={{4,0},{8,4},{12,8},{5,1},{9,5},{13,9},{6,2},{10,6},{14,10},{7,3},{... | collective-permute-start | bytes 1572872 | tf_op jit(solution)/shard_map/ppermute | solution.py:19
  214.5 2.1 collective-permute-start.37
  224.0 4.0 %shard_map.142 = (f32[512,2048]{1,0:T(8,128)}, f32[512,512]{1,0:T(8,128)}, f32[512,512]{1,0:T(8,128)}) custom-call(s32[6]{0:T(128)S(1)} %stack.55.place_ref, bf16[512,768]{1,0:T(8,128)(2,1)} %copy-done.20, bf16[512,768]{1,0:T(8,128)(2,1)} %copy-done.21, bf16[512,768]{1,0:T(8,128)(2,1)} %copy-done.22, ...), custom_call_target="tpu_custom_call", output_to_operand_aliasing={{0}: (4, {}), {1}: (5, {}), {2}: (6, {})} | custom-call | tf_op jit(solution)/shard_map/pallas_call | solution.py:459
  228.0 2.2 shard_map.139
  230.2 2.4 %shard_map.143 = (f32[512,2048]{1,0:T(8,128)}, f32[512,512]{1,0:T(8,128)}, f32[512,512]{1,0:T(8,128)}) custom-call(s32[6]{0:T(128)S(1)} %stack.55.place_ref, bf16[512,768]{1,0:T(8,128)(2,1)} %collective-permute-done.34.refs_0_, f32[512,2048]{1,0:T(8,128)} %get-tuple-element.197.refs_1_, ...), custom_call_target="tpu_custom_call", output_to_operand_aliasing={{0}: (2, {}), {1}: (3, {}), {2}: (4, {})} | custom-call | tf_op jit(solution)/shard_map/pallas_call | solution.py:459
  (144 shorter events, 53.5 us)
Async XLA Ops:
  2.8 18.5 %collective-permute-start = (bf16[512,768]{1,0:T(8,128)(2,1)S(1)}, bf16[512,768]{1,0:T(8,128)(2,1)S(1)}, u32[]{:S(2)}, u32[]{:S(2)}) collective-permute-start(bf16[512,768]{1,0:T(8,128)(2,1)S(1)} %get-tuple-element.111), channel_id=1, source_target_pairs={{0,1},{1,0},{2,3},{3,2},{4,5},{5,4},{6,7},{7,6},{8,9},{9,8},{10,11... | collective-permute-start | bytes 2359304 | tf_op jit(solution)/shard_map/ppermute | solution.py:472
  21.4 33.3 %collective-permute-start.2 = (bf16[512,768]{1,0:T(8,128)(2,1)S(1)}, bf16[512,768]{1,0:T(8,128)(2,1)S(1)}, u32[]{:S(2)}, u32[]{:S(2)}) collective-permute-start(bf16[512,768]{1,0:T(8,128)(2,1)S(1)} %pad_maximum_fusion), channel_id=1, source_target_pairs={{1,2},{2,1},{5,6},{6,5},{9,10},{10,9},{13,14},{14,13},{17,18},{18,... | collective-permute-start | bytes 2359304 | tf_op jit(solution)/shard_map/ppermute | solution.py:472
  22.1 32.6 %collective-permute-start.4 = (bf16[512,768]{1,0:T(8,128)(2,1)S(1)}, bf16[512,768]{1,0:T(8,128)(2,1)S(1)}, u32[]{:S(2)}, u32[]{:S(2)}) collective-permute-start(bf16[512,768]{1,0:T(8,128)(2,1)S(1)} %get-tuple-element.118), channel_id=1, source_target_pairs={{0,1},{1,0},{2,3},{3,2},{4,5},{5,4},{6,7},{7,6},{8,9},{9,8},{10,11... | collective-permute-start | bytes 2359304 | tf_op jit(solution)/shard_map/ppermute | solution.py:472
  27.4 27.3 %collective-permute-start.3 = (bf16[512,768]{1,0:T(8,128)(2,1)S(1)}, bf16[512,768]{1,0:T(8,128)(2,1)S(1)}, u32[]{:S(2)}, u32[]{:S(2)}) collective-permute-start(bf16[512,768]{1,0:T(8,128)(2,1)S(1)} %collective-permute-done.a), channel_id=1, source_target_pairs={{0,16},{16,0},{1,17},{17,1},{2,18},{18,2},{3,19},{19,3},{4,20},{20... | collective-permute-start | bytes 2359304 | tf_op jit(solution)/shard_map/ppermute | solution.py:472
  27.6 27.1 %collective-permute-start.5 = (bf16[288,1024]{1,0:T(8,128)(2,1)S(1)}, bf16[288,1024]{1,0:T(8,128)(2,1)S(1)}, u32[]{:S(2)}, u32[]{:S(2)}) collective-permute-start(bf16[288,1024]{1,0:T(8,128)(2,1)S(1)} %get-tuple-element.114), channel_id=1, source_target_pairs={{0,2},{3,1},{4,6},{7,5},{8,10},{11,9},{12,14},{15,13},{16,18},{19,... | collective-permute-start | bytes 1769480 | tf_op jit(solution)/shard_map/ppermute | solution.py:472
  55.5 18.8 %collective-permute-start.8 = (bf16[512,768]{1,0:T(8,128)(2,1)S(1)}, bf16[512,768]{1,0:T(8,128)(2,1)S(1)}, u32[]{:S(2)}, u32[]{:S(2)}) collective-permute-start(bf16[512,768]{1,0:T(8,128)(2,1)S(1)} %collective-permute-done.2), channel_id=1, source_target_pairs={{1,0},{2,3},{5,4},{6,7},{9,8},{10,11},{13,12},{14,15},{17,16},{18,... | collective-permute-start | bytes 2359304 | tf_op jit(solution)/shard_map/ppermute | solution.py:472
  74.5 18.4 %collective-permute-start.11 = (bf16[512,768]{1,0:T(8,128)(2,1)S(1)}, bf16[512,768]{1,0:T(8,128)(2,1)S(1)}, u32[]{:S(2)}, u32[]{:S(2)}) collective-permute-start(bf16[512,768]{1,0:T(8,128)(2,1)S(1)} %collective-permute-done.7), channel_id=1, source_target_pairs={{1,0},{2,3},{5,4},{6,7},{9,8},{10,11},{13,12},{14,15},{17,16},{18,... | collective-permute-start | bytes 2359304 | tf_op jit(solution)/shard_map/ppermute | solution.py:472
  96.9 24.2 %collective-permute-start.19 = (bf16[512,768]{1,0:T(8,128)(2,1)S(1)}, bf16[512,768]{1,0:T(8,128)(2,1)S(1)}, u32[]{:S(2)}, u32[]{:S(2)}) collective-permute-start(bf16[512,768]{1,0:T(8,128)(2,1)S(1)} %broadcast_select_fusion.2.far), channel_id=1, source_target_pairs={{0,16},{16,0},{1,17},{17,1},{2,18},{18,2},{3,19},{19,3},{4,20},{20... | collective-permute-start | bytes 2359304 | tf_op jit(solution)/shard_map/ppermute | solution.py:472
  111.5 21.3 %collective-permute-start.15 = (bf16[512,768]{1,0:T(8,128)(2,1)}, bf16[512,768]{1,0:T(8,128)(2,1)S(1)}, u32[]{:S(2)}, u32[]{:S(2)}) collective-permute-start(bf16[512,768]{1,0:T(8,128)(2,1)} %collective-permute-done.12), channel_id=1, source_target_pairs={{1,0},{2,3},{5,4},{6,7},{9,8},{10,11},{13,12},{14,15},{17,16},{18,... | collective-permute-start | bytes 2359304 | tf_op jit(solution)/shard_map/ppermute | solution.py:472
  113.0 32.2 %collective-permute-start.23 = (bf16[512,768]{1,0:T(8,128)(2,1)S(1)}, bf16[512,768]{1,0:T(8,128)(2,1)S(1)}, u32[]{:S(2)}, u32[]{:S(2)}) collective-permute-start(bf16[512,768]{1,0:T(8,128)(2,1)S(1)} %broadcast_select_fusion.1.far), channel_id=1, source_target_pairs={{0,16},{16,0},{1,17},{17,1},{2,18},{18,2},{3,19},{19,3},{4,20},{20... | collective-permute-start | bytes 2359304 | tf_op jit(solution)/shard_map/ppermute | solution.py:472
  113.2 19.7 %collective-permute-start.18 = (bf16[288,768]{1,0:T(8,128)(2,1)S(1)}, bf16[288,768]{1,0:T(8,128)(2,1)S(1)}, u32[]{:S(2)}, u32[]{:S(2)}) collective-permute-start(bf16[288,768]{1,0:T(8,128)(2,1)S(1)} %get-tuple-element.132.d0), channel_id=1, source_target_pairs={{1,2},{2,1},{5,6},{6,5},{9,10},{10,9},{13,14},{14,13},{17,18},{18,... | collective-permute-start | bytes 1327112 | tf_op jit(solution)/shard_map/ppermute | solution.py:472
  113.9 19.0 %collective-permute-start.17 = (bf16[288,768]{1,0:T(8,128)(2,1)S(1)}, bf16[288,768]{1,0:T(8,128)(2,1)S(1)}, u32[]{:S(2)}, u32[]{:S(2)}) collective-permute-start(bf16[288,768]{1,0:T(8,128)(2,1)S(1)} %get-tuple-element.132.d0), channel_id=1, source_target_pairs={{0,2},{3,1},{4,6},{7,5},{8,10},{11,9},{12,14},{15,13},{16,18},{19,... | collective-permute-start | bytes 1327112 | tf_op jit(solution)/shard_map/ppermute | solution.py:472
  133.4 21.0 %collective-permute-start.22 = (bf16[288,768]{1,0:T(8,128)(2,1)S(1)}, bf16[288,768]{1,0:T(8,128)(2,1)S(1)}, u32[]{:S(2)}, u32[]{:S(2)}) collective-permute-start(bf16[288,768]{1,0:T(8,128)(2,1)S(1)} %get-tuple-element.141.d0), channel_id=1, source_target_pairs={{1,2},{2,1},{5,6},{6,5},{9,10},{10,9},{13,14},{14,13},{17,18},{18,... | collective-permute-start | bytes 1327112 | tf_op jit(solution)/shard_map/ppermute | solution.py:472
  134.1 20.3 %collective-permute-start.21 = (bf16[288,768]{1,0:T(8,128)(2,1)S(1)}, bf16[288,768]{1,0:T(8,128)(2,1)S(1)}, u32[]{:S(2)}, u32[]{:S(2)}) collective-permute-start(bf16[288,768]{1,0:T(8,128)(2,1)S(1)} %get-tuple-element.141.d0), channel_id=1, source_target_pairs={{0,2},{3,1},{4,6},{7,5},{8,10},{11,9},{12,14},{15,13},{16,18},{19,... | collective-permute-start | bytes 1327112 | tf_op jit(solution)/shard_map/ppermute | solution.py:472
  142.2 22.6 %collective-permute-start.27 = (bf16[512,768]{1,0:T(8,128)(2,1)S(1)}, bf16[512,768]{1,0:T(8,128)(2,1)S(1)}, u32[]{:S(2)}, u32[]{:S(2)}) collective-permute-start(bf16[512,768]{1,0:T(8,128)(2,1)S(1)} %broadcast_select_fusion.far), channel_id=1, source_target_pairs={{0,16},{16,0},{1,17},{17,1},{2,18},{18,2},{3,19},{19,3},{4,20},{20... | collective-permute-start | bytes 2359304 | tf_op jit(solution)/shard_map/ppermute | solution.py:472
  145.2 28.8 %collective-permute-start.28 = (bf16[512,768]{1,0:T(8,128)(2,1)S(1)}, bf16[512,768]{1,0:T(8,128)(2,1)S(1)}, u32[]{:S(2)}, u32[]{:S(2)}) collective-permute-start(bf16[512,768]{1,0:T(8,128)(2,1)S(1)} %get-tuple-element.150), channel_id=1, source_target_pairs={{1,0},{2,3},{5,4},{6,7},{9,8},{10,11},{13,12},{14,15},{17,16},{18,... | collective-permute-start | bytes 2359304 | tf_op jit(solution)/shard_map/ppermute | solution.py:472
  154.4 19.6 %collective-permute-start.26 = (bf16[288,768]{1,0:T(8,128)(2,1)S(1)}, bf16[288,768]{1,0:T(8,128)(2,1)S(1)}, u32[]{:S(2)}, u32[]{:S(2)}) collective-permute-start(bf16[288,768]{1,0:T(8,128)(2,1)S(1)} %get-tuple-element.151.d0), channel_id=1, source_target_pairs={{1,2},{2,1},{5,6},{6,5},{9,10},{10,9},{13,14},{14,13},{17,18},{18,... | collective-permute-start | bytes 1327112 | tf_op jit(solution)/shard_map/ppermute | solution.py:472
  155.1 18.9 %collective-permute-start.25 = (bf16[288,768]{1,0:T(8,128)(2,1)S(1)}, bf16[288,768]{1,0:T(8,128)(2,1)S(1)}, u32[]{:S(2)}, u32[]{:S(2)}) collective-permute-start(bf16[288,768]{1,0:T(8,128)(2,1)S(1)} %get-tuple-element.151.d0), channel_id=1, source_target_pairs={{0,2},{3,1},{4,6},{7,5},{8,10},{11,9},{12,14},{15,13},{16,18},{19,... | collective-permute-start | bytes 1327112 | tf_op jit(solution)/shard_map/ppermute | solution.py:472
  164.8 33.5 %collective-permute-start.32 = (bf16[512,768]{1,0:T(8,128)(2,1)S(1)}, bf16[512,768]{1,0:T(8,128)(2,1)S(1)}, u32[]{:S(2)}, u32[]{:S(2)}) collective-permute-start(bf16[512,768]{1,0:T(8,128)(2,1)S(1)} %get-tuple-element.162), channel_id=1, source_target_pairs={{1,0},{2,3},{5,4},{6,7},{9,8},{10,11},{13,12},{14,15},{17,16},{18,... | collective-permute-start | bytes 2359304 | tf_op jit(solution)/shard_map/ppermute | solution.py:472
  175.5 22.9 %collective-permute-start.33 = (bf16[512,768]{1,0:T(8,128)(2,1)S(1)}, bf16[512,768]{1,0:T(8,128)(2,1)S(1)}, u32[]{:S(2)}, u32[]{:S(2)}) collective-permute-start(bf16[512,768]{1,0:T(8,128)(2,1)S(1)} %shard_map.136), channel_id=1, source_target_pairs={{1,0},{2,3},{5,4},{6,7},{9,8},{10,11},{13,12},{14,15},{17,16},{18,... | collective-permute-start | bytes 2359304 | tf_op jit(solution)/shard_map/ppermute | solution.py:472
  176.8 21.5 %collective-permute-start.31 = (bf16[288,768]{1,0:T(8,128)(2,1)S(1)}, bf16[288,768]{1,0:T(8,128)(2,1)S(1)}, u32[]{:S(2)}, u32[]{:S(2)}) collective-permute-start(bf16[288,768]{1,0:T(8,128)(2,1)S(1)} %get-tuple-element.163.d0), channel_id=1, source_target_pairs={{1,2},{2,1},{5,6},{6,5},{9,10},{10,9},{13,14},{14,13},{17,18},{18,... | collective-permute-start | bytes 1327112 | tf_op jit(solution)/shard_map/ppermute | solution.py:472
  177.4 20.9 %collective-permute-start.30 = (bf16[288,768]{1,0:T(8,128)(2,1)S(1)}, bf16[288,768]{1,0:T(8,128)(2,1)S(1)}, u32[]{:S(2)}, u32[]{:S(2)}) collective-permute-start(bf16[288,768]{1,0:T(8,128)(2,1)S(1)} %get-tuple-element.163.d0), channel_id=1, source_target_pairs={{0,2},{3,1},{4,6},{7,5},{8,10},{11,9},{12,14},{15,13},{16,18},{19,... | collective-permute-start | bytes 1327112 | tf_op jit(solution)/shard_map/ppermute | solution.py:472
  200.2 30.1 %collective-permute-start.34 = (bf16[512,768]{1,0:T(8,128)(2,1)}, bf16[512,768]{1,0:T(8,128)(2,1)}, u32[]{:S(2)}, u32[]{:S(2)}) collective-permute-start(bf16[512,768]{1,0:T(8,128)(2,1)} %shard_map.138), channel_id=1, source_target_pairs={{1,0},{2,3},{5,4},{6,7},{9,8},{10,11},{13,12},{14,15},{17,16},{18,... | collective-permute-start | bytes 2359304 | tf_op jit(solution)/shard_map/ppermute | solution.py:472
  201.5 26.5 %collective-permute-start.36 = (bf16[128,2048]{1,0:T(8,128)(2,1)}, bf16[128,2048]{1,0:T(8,128)(2,1)}, u32[]{:S(2)}, u32[]{:S(2)}) collective-permute-start(bf16[128,2048]{1,0:T(8,128)(2,1)} %get-tuple-element.176), channel_id=1, source_target_pairs={{4,0},{8,4},{12,8},{5,1},{9,5},{13,9},{6,2},{10,6},{14,10},{7,3},{... | collective-permute-start | bytes 1572872 | tf_op jit(solution)/shard_map/ppermute | solution.py:19
  (43 other events, 437.0 us)
